TPU v7x, 32 devices: a whole 2x2x4 slice. The times are simulated.
32 devices in a mesh: freq: 4 (over x, core), frame: 8 (over z, y).
Axes of the slice: x: 2, y: 2, z: 4, core: 2. Of those that a mesh axis runs over, the one named last changes fastest.
Arguments:
- spectra: bfloat16 [2, 24, 1024, 2048], P(None, None, 'freq', 'frame'), may hold values from -6 to 6
- norm_gain: float32 [1024], replicated, may hold values from 0.25 to 1.75
- w_in: bfloat16 [1024, 1024], replicated, may hold values from -0.1875 to 0.1875
- b_in: float32 [1024], replicated, may hold values from -3 to 3
- w_mid: bfloat16 [1024, 1024], replicated, may hold values from -0.1875 to 0.1875
- b_mid: float32 [1024], replicated, may hold values from -3 to 3
- w_out: bfloat16 [1024, 1024], replicated, may hold values from -0.1875 to 0.1875
- b_out: float32 [1024], replicated, may hold values from -3 to 3
Outputs:
- demixed: float32 [2, 24, 1024, 2048], P(None, None, 'freq', 'frame')
- variances: bfloat16 [24, 1024, 2048], P(None, 'freq', 'frame')
All inputs are finite; a program needn't handle non-finite values.
Results may differ from a plain program's by a relative error of at most 0.0032.
Values may be sent and summed in bfloat16 or wider, within the bound.
No kernel may reach another device: no remote copies, remote signals or barrier semaphores. Data moves between devices by JAX's collectives and lax.ppermute only.
A program may use at most 128 MiB of HBM per device.

v0:
```python
import jax
import jax.numpy as jnp
from jax import lax
from jax.sharding import PartitionSpec as P

epsilon = 1e-05
power_floor = 0.001
variance_floor = 0.25


def coefficients(numer_real, numer_imag, denom, source, count):
    is_self = (jnp.arange(count, dtype=jnp.int32) == source)[:, None]
    coef_real = jnp.where(is_self, 1.0 - lax.rsqrt(denom), numer_real / denom)
    coef_imag = jnp.where(is_self, 0.0, numer_imag / denom)
    return (coef_real, coef_imag)


def on_device(spectra, norm_gain, w_in, b_in, w_mid, b_mid, w_out, b_out):
    real_part = spectra[0].astype(jnp.float32)
    imag_part = spectra[1].astype(jnp.float32)
    count = spectra.shape[1]
    frames = spectra.shape[3] * lax.axis_size("frame")
    logpower = jnp.log(real_part * real_part + imag_part * imag_part + power_floor).astype(
        jnp.bfloat16
    )
    values = lax.all_to_all(logpower, "freq", split_axis=2, concat_axis=1, tiled=True).astype(
        jnp.float32
    )
    average = jnp.mean(values, axis=1, keepdims=True)
    centred = values - average
    spread = jnp.mean(centred * centred, axis=1, keepdims=True)
    normed = (centred * lax.rsqrt(spread + epsilon) * norm_gain[None, :, None]).astype(jnp.bfloat16)
    hidden_one = jax.nn.silu(
        jnp.einsum("nft,fh->nth", normed, w_in, preferred_element_type=jnp.float32) + b_in
    ).astype(jnp.bfloat16)
    hidden_two = jax.nn.silu(
        jnp.einsum("nth,hg->ntg", hidden_one, w_mid, preferred_element_type=jnp.float32) + b_mid
    ).astype(jnp.bfloat16)
    output_pre = (
        jnp.einsum("nth,hf->nft", hidden_two, w_out, preferred_element_type=jnp.float32)
        + b_out[None, :, None]
    )
    frame_variances = (jax.nn.softplus(output_pre) + variance_floor).astype(jnp.bfloat16)
    variances = lax.all_to_all(frame_variances, "freq", split_axis=1, concat_axis=2, tiled=True)
    weight = 1.0 / variances.astype(jnp.float32)

    def sweep(source, carry):
        demix_real, demix_imag = carry
        pick_real = lax.dynamic_index_in_dim(demix_real, source, 0, keepdims=False)
        pick_imag = lax.dynamic_index_in_dim(demix_imag, source, 0, keepdims=False)
        numer_real = jnp.sum(weight * (demix_real * pick_real + demix_imag * pick_imag), axis=2)
        numer_imag = jnp.sum(weight * (demix_imag * pick_real - demix_real * pick_imag), axis=2)
        denom = jnp.sum(weight * (pick_real * pick_real + pick_imag * pick_imag), axis=2)
        numer_real, numer_imag, denom = lax.psum((numer_real, numer_imag, denom), "frame")
        coef_real, coef_imag = coefficients(
            numer_real / frames, numer_imag / frames, denom / frames, source, count
        )
        coef_real = coef_real[:, :, None]
        coef_imag = coef_imag[:, :, None]
        new_real = demix_real - (coef_real * pick_real - coef_imag * pick_imag)
        new_imag = demix_imag - (coef_real * pick_imag + coef_imag * pick_real)
        return (new_real, new_imag)

    demix_real, demix_imag = lax.fori_loop(0, count, sweep, (real_part, imag_part))
    return (jnp.stack([demix_real, demix_imag]), variances)


def solution(mesh):
    in_specs = (P(None, None, "freq", "frame"), P(), P(), P(), P(), P(), P(), P())
    out_specs = (P(None, None, "freq", "frame"), P(None, "freq", "frame"))
    return jax.shard_map(
        on_device, mesh=mesh, in_specs=in_specs, out_specs=out_specs, check_vma=False
    )
```

profile of v0, /device:TPU:0, one launch (start us, length us, event | category | flops | bytes accessed | tf_op | source)
XLA Modules:
  0.0 2395.0 jit_solution(12013755768932757171)
XLA Ops:
  28.0 40.9 %all_to_all.27 = bf16[24,256,256]{1,0,2:T(8,128)(2,1)S(1)} all-to-all(bf16[24,256,256]{1,0,2:T(8,128)(2,1)S(1)} %log_convert_fusion), channel_id=1, replica_groups=mesh['freq'=4,'frame'=8] {'freq'}, dimensions={2} | all-to-all | bytes 6291456 | tf_op jit(solution)/shard_map/all_to_all | solution.py:26
  75.2 11.2 fusion.14
  86.5 11.8 fusion.5
  142.2 13.3 all-to-all-done.1
  190.3 2187.0 %while.15 = (s32[]{:T(128)}, f32[24,256,256]{2,1,0:T(8,128)}, f32[24,256,256]{2,1,0:T(8,128)}, f32[24,256,256]{2,1,0:T(8,128)}, s32[]{:T(128)}) while((s32[]{:T(128)}, f32[24,256,256]{2,1,0:T(8,128)}, f32[24,256,256]{2,1,0:T(8,128)}, f32[24,256,256]{2,1,0:T(8,128)}, s32[]{:T(128)}) %tuple.56), condition=%wide.region_9.10_spmd, body=%wide.region_2.9_spmd.sunk | while | flops 31703064 | bytes 47349924 | solution.py:64
  191.4 8.7 multiply_reduce_fusion.4
  200.1 69.9 %all-reduce.5.cloned.1.call-done = (f32[24,256]{1,0:T(8,128)}, f32[24,256]{1,0:T(8,128)}, f32[24,256]{1,0:T(8,128)}) async-done(((f32[24,256]{1,0:T(8,128)}, f32[24,256]{1,0:T(8,128)}, f32[24,256]{1,0:T(8,128)}), (f32[24,256]{1,0:T(8,128)}, f32[24,256]{1,0:T(8,128)}, f32[24,256]{1,0:T(8,128)})) %all-reduce.5.cloned.1.call-update) | async-done | bytes 73744 | tf_op jit(solution)/shard_map/while/body/eval_jaxpr/psum | solution.py:54
  270.9 10.9 add_subtract_fusion.2
  282.8 8.7 multiply_reduce_fusion.4
  291.6 69.6 %all-reduce.5.cloned.1.call-done = (f32[24,256]{1,0:T(8,128)}, f32[24,256]{1,0:T(8,128)}, f32[24,256]{1,0:T(8,128)}) async-done(((f32[24,256]{1,0:T(8,128)}, f32[24,256]{1,0:T(8,128)}, f32[24,256]{1,0:T(8,128)}), (f32[24,256]{1,0:T(8,128)}, f32[24,256]{1,0:T(8,128)}, f32[24,256]{1,0:T(8,128)})) %all-reduce.5.cloned.1.call-update) | async-done | bytes 73744 | tf_op jit(solution)/shard_map/while/body/eval_jaxpr/psum | solution.py:54
  362.0 10.9 add_subtract_fusion.2
  373.9 8.7 multiply_reduce_fusion.4
  382.7 69.6 %all-reduce.5.cloned.1.call-done = (f32[24,256]{1,0:T(8,128)}, f32[24,256]{1,0:T(8,128)}, f32[24,256]{1,0:T(8,128)}) async-done(((f32[24,256]{1,0:T(8,128)}, f32[24,256]{1,0:T(8,128)}, f32[24,256]{1,0:T(8,128)}), (f32[24,256]{1,0:T(8,128)}, f32[24,256]{1,0:T(8,128)}, f32[24,256]{1,0:T(8,128)})) %all-reduce.5.cloned.1.call-update) | async-done | bytes 73744 | tf_op jit(solution)/shard_map/while/body/eval_jaxpr/psum | solution.py:54
  453.1 10.9 add_subtract_fusion.2
  465.0 8.7 multiply_reduce_fusion.4
  473.8 69.6 %all-reduce.5.cloned.1.call-done = (f32[24,256]{1,0:T(8,128)}, f32[24,256]{1,0:T(8,128)}, f32[24,256]{1,0:T(8,128)}) async-done(((f32[24,256]{1,0:T(8,128)}, f32[24,256]{1,0:T(8,128)}, f32[24,256]{1,0:T(8,128)}), (f32[24,256]{1,0:T(8,128)}, f32[24,256]{1,0:T(8,128)}, f32[24,256]{1,0:T(8,128)})) %all-reduce.5.cloned.1.call-update) | async-done | bytes 73744 | tf_op jit(solution)/shard_map/while/body/eval_jaxpr/psum | solution.py:54
  544.2 10.9 add_subtract_fusion.2
  556.1 8.7 multiply_reduce_fusion.4
  564.9 69.6 %all-reduce.5.cloned.1.call-done = (f32[24,256]{1,0:T(8,128)}, f32[24,256]{1,0:T(8,128)}, f32[24,256]{1,0:T(8,128)}) async-done(((f32[24,256]{1,0:T(8,128)}, f32[24,256]{1,0:T(8,128)}, f32[24,256]{1,0:T(8,128)}), (f32[24,256]{1,0:T(8,128)}, f32[24,256]{1,0:T(8,128)}, f32[24,256]{1,0:T(8,128)})) %all-reduce.5.cloned.1.call-update) | async-done | bytes 73744 | tf_op jit(solution)/shard_map/while/body/eval_jaxpr/psum | solution.py:54
  635.3 10.9 add_subtract_fusion.2
  656.0 69.6 %all-reduce.5.cloned.1.call-done = (f32[24,256]{1,0:T(8,128)}, f32[24,256]{1,0:T(8,128)}, f32[24,256]{1,0:T(8,128)}) async-done(((f32[24,256]{1,0:T(8,128)}, f32[24,256]{1,0:T(8,128)}, f32[24,256]{1,0:T(8,128)}), (f32[24,256]{1,0:T(8,128)}, f32[24,256]{1,0:T(8,128)}, f32[24,256]{1,0:T(8,128)})) %all-reduce.5.cloned.1.call-update) | async-done | bytes 73744 | tf_op jit(solution)/shard_map/while/body/eval_jaxpr/psum | solution.py:54
  726.4 10.9 add_subtract_fusion.2
  747.1 69.6 %all-reduce.5.cloned.1.call-done = (f32[24,256]{1,0:T(8,128)}, f32[24,256]{1,0:T(8,128)}, f32[24,256]{1,0:T(8,128)}) async-done(((f32[24,256]{1,0:T(8,128)}, f32[24,256]{1,0:T(8,128)}, f32[24,256]{1,0:T(8,128)}), (f32[24,256]{1,0:T(8,128)}, f32[24,256]{1,0:T(8,128)}, f32[24,256]{1,0:T(8,128)})) %all-reduce.5.cloned.1.call-update) | async-done | bytes 73744 | tf_op jit(solution)/shard_map/while/body/eval_jaxpr/psum | solution.py:54
  817.5 10.9 add_subtract_fusion.2
  838.2 69.6 %all-reduce.5.cloned.1.call-done = (f32[24,256]{1,0:T(8,128)}, f32[24,256]{1,0:T(8,128)}, f32[24,256]{1,0:T(8,128)}) async-done(((f32[24,256]{1,0:T(8,128)}, f32[24,256]{1,0:T(8,128)}, f32[24,256]{1,0:T(8,128)}), (f32[24,256]{1,0:T(8,128)}, f32[24,256]{1,0:T(8,128)}, f32[24,256]{1,0:T(8,128)})) %all-reduce.5.cloned.1.call-update) | async-done | bytes 73744 | tf_op jit(solution)/shard_map/while/body/eval_jaxpr/psum | solution.py:54
  908.6 10.9 add_subtract_fusion.2
  929.3 69.6 %all-reduce.5.cloned.1.call-done = (f32[24,256]{1,0:T(8,128)}, f32[24,256]{1,0:T(8,128)}, f32[24,256]{1,0:T(8,128)}) async-done(((f32[24,256]{1,0:T(8,128)}, f32[24,256]{1,0:T(8,128)}, f32[24,256]{1,0:T(8,128)}), (f32[24,256]{1,0:T(8,128)}, f32[24,256]{1,0:T(8,128)}, f32[24,256]{1,0:T(8,128)})) %all-reduce.5.cloned.1.call-update) | async-done | bytes 73744 | tf_op jit(solution)/shard_map/while/body/eval_jaxpr/psum | solution.py:54
  999.7 10.9 add_subtract_fusion.2
  1020.4 69.6 %all-reduce.5.cloned.1.call-done = (f32[24,256]{1,0:T(8,128)}, f32[24,256]{1,0:T(8,128)}, f32[24,256]{1,0:T(8,128)}) async-done(((f32[24,256]{1,0:T(8,128)}, f32[24,256]{1,0:T(8,128)}, f32[24,256]{1,0:T(8,128)}), (f32[24,256]{1,0:T(8,128)}, f32[24,256]{1,0:T(8,128)}, f32[24,256]{1,0:T(8,128)})) %all-reduce.5.cloned.1.call-update) | async-done | bytes 73744 | tf_op jit(solution)/shard_map/while/body/eval_jaxpr/psum | solution.py:54
  1090.8 10.9 add_subtract_fusion.2
  1111.5 69.6 %all-reduce.5.cloned.1.call-done = (f32[24,256]{1,0:T(8,128)}, f32[24,256]{1,0:T(8,128)}, f32[24,256]{1,0:T(8,128)}) async-done(((f32[24,256]{1,0:T(8,128)}, f32[24,256]{1,0:T(8,128)}, f32[24,256]{1,0:T(8,128)}), (f32[24,256]{1,0:T(8,128)}, f32[24,256]{1,0:T(8,128)}, f32[24,256]{1,0:T(8,128)})) %all-reduce.5.cloned.1.call-update) | async-done | bytes 73744 | tf_op jit(solution)/shard_map/while/body/eval_jaxpr/psum | solution.py:54
  1182.0 10.9 add_subtract_fusion.2
  1202.7 69.6 %all-reduce.5.cloned.1.call-done = (f32[24,256]{1,0:T(8,128)}, f32[24,256]{1,0:T(8,128)}, f32[24,256]{1,0:T(8,128)}) async-done(((f32[24,256]{1,0:T(8,128)}, f32[24,256]{1,0:T(8,128)}, f32[24,256]{1,0:T(8,128)}), (f32[24,256]{1,0:T(8,128)}, f32[24,256]{1,0:T(8,128)}, f32[24,256]{1,0:T(8,128)})) %all-reduce.5.cloned.1.call-update) | async-done | bytes 73744 | tf_op jit(solution)/shard_map/while/body/eval_jaxpr/psum | solution.py:54
  1273.1 10.9 add_subtract_fusion.2
  1293.8 69.6 %all-reduce.5.cloned.1.call-done = (f32[24,256]{1,0:T(8,128)}, f32[24,256]{1,0:T(8,128)}, f32[24,256]{1,0:T(8,128)}) async-done(((f32[24,256]{1,0:T(8,128)}, f32[24,256]{1,0:T(8,128)}, f32[24,256]{1,0:T(8,128)}), (f32[24,256]{1,0:T(8,128)}, f32[24,256]{1,0:T(8,128)}, f32[24,256]{1,0:T(8,128)})) %all-reduce.5.cloned.1.call-update) | async-done | bytes 73744 | tf_op jit(solution)/shard_map/while/body/eval_jaxpr/psum | solution.py:54
  1364.2 10.9 add_subtract_fusion.2
  1384.9 69.6 %all-reduce.5.cloned.1.call-done = (f32[24,256]{1,0:T(8,128)}, f32[24,256]{1,0:T(8,128)}, f32[24,256]{1,0:T(8,128)}) async-done(((f32[24,256]{1,0:T(8,128)}, f32[24,256]{1,0:T(8,128)}, f32[24,256]{1,0:T(8,128)}), (f32[24,256]{1,0:T(8,128)}, f32[24,256]{1,0:T(8,128)}, f32[24,256]{1,0:T(8,128)})) %all-reduce.5.cloned.1.call-update) | async-done | bytes 73744 | tf_op jit(solution)/shard_map/while/body/eval_jaxpr/psum | solution.py:54
  1455.3 10.9 add_subtract_fusion.2
  1467.2 8.7 multiply_reduce_fusion.4
  1476.0 69.6 %all-reduce.5.cloned.1.call-done = (f32[24,256]{1,0:T(8,128)}, f32[24,256]{1,0:T(8,128)}, f32[24,256]{1,0:T(8,128)}) async-done(((f32[24,256]{1,0:T(8,128)}, f32[24,256]{1,0:T(8,128)}, f32[24,256]{1,0:T(8,128)}), (f32[24,256]{1,0:T(8,128)}, f32[24,256]{1,0:T(8,128)}, f32[24,256]{1,0:T(8,128)})) %all-reduce.5.cloned.1.call-update) | async-done | bytes 73744 | tf_op jit(solution)/shard_map/while/body/eval_jaxpr/psum | solution.py:54
  1546.4 10.9 add_subtract_fusion.2
  1558.3 8.7 multiply_reduce_fusion.4
  1567.1 69.6 %all-reduce.5.cloned.1.call-done = (f32[24,256]{1,0:T(8,128)}, f32[24,256]{1,0:T(8,128)}, f32[24,256]{1,0:T(8,128)}) async-done(((f32[24,256]{1,0:T(8,128)}, f32[24,256]{1,0:T(8,128)}, f32[24,256]{1,0:T(8,128)}), (f32[24,256]{1,0:T(8,128)}, f32[24,256]{1,0:T(8,128)}, f32[24,256]{1,0:T(8,128)})) %all-reduce.5.cloned.1.call-update) | async-done | bytes 73744 | tf_op jit(solution)/shard_map/while/body/eval_jaxpr/psum | solution.py:54
  1637.5 10.9 add_subtract_fusion.2
  1649.4 8.7 multiply_reduce_fusion.4
  1658.2 69.6 %all-reduce.5.cloned.1.call-done = (f32[24,256]{1,0:T(8,128)}, f32[24,256]{1,0:T(8,128)}, f32[24,256]{1,0:T(8,128)}) async-done(((f32[24,256]{1,0:T(8,128)}, f32[24,256]{1,0:T(8,128)}, f32[24,256]{1,0:T(8,128)}), (f32[24,256]{1,0:T(8,128)}, f32[24,256]{1,0:T(8,128)}, f32[24,256]{1,0:T(8,128)})) %all-reduce.5.cloned.1.call-update) | async-done | bytes 73744 | tf_op jit(solution)/shard_map/while/body/eval_jaxpr/psum | solution.py:54
  1728.6 10.9 add_subtract_fusion.2
  1740.6 8.7 multiply_reduce_fusion.4
  1749.3 69.6 %all-reduce.5.cloned.1.call-done = (f32[24,256]{1,0:T(8,128)}, f32[24,256]{1,0:T(8,128)}, f32[24,256]{1,0:T(8,128)}) async-done(((f32[24,256]{1,0:T(8,128)}, f32[24,256]{1,0:T(8,128)}, f32[24,256]{1,0:T(8,128)}), (f32[24,256]{1,0:T(8,128)}, f32[24,256]{1,0:T(8,128)}, f32[24,256]{1,0:T(8,128)})) %all-reduce.5.cloned.1.call-update) | async-done | bytes 73744 | tf_op jit(solution)/shard_map/while/body/eval_jaxpr/psum | solution.py:54
  1819.7 10.9 add_subtract_fusion.2
  1831.7 8.7 multiply_reduce_fusion.4
  1840.4 69.6 %all-reduce.5.cloned.1.call-done = (f32[24,256]{1,0:T(8,128)}, f32[24,256]{1,0:T(8,128)}, f32[24,256]{1,0:T(8,128)}) async-done(((f32[24,256]{1,0:T(8,128)}, f32[24,256]{1,0:T(8,128)}, f32[24,256]{1,0:T(8,128)}), (f32[24,256]{1,0:T(8,128)}, f32[24,256]{1,0:T(8,128)}, f32[24,256]{1,0:T(8,128)})) %all-reduce.5.cloned.1.call-update) | async-done | bytes 73744 | tf_op jit(solution)/shard_map/while/body/eval_jaxpr/psum | solution.py:54
  1910.8 10.9 add_subtract_fusion.2
  1931.5 69.6 %all-reduce.5.cloned.1.call-done = (f32[24,256]{1,0:T(8,128)}, f32[24,256]{1,0:T(8,128)}, f32[24,256]{1,0:T(8,128)}) async-done(((f32[24,256]{1,0:T(8,128)}, f32[24,256]{1,0:T(8,128)}, f32[24,256]{1,0:T(8,128)}), (f32[24,256]{1,0:T(8,128)}, f32[24,256]{1,0:T(8,128)}, f32[24,256]{1,0:T(8,128)})) %all-reduce.5.cloned.1.call-update) | async-done | bytes 73744 | tf_op jit(solution)/shard_map/while/body/eval_jaxpr/psum | solution.py:54
  2001.9 10.9 add_subtract_fusion.2
  2022.6 69.6 %all-reduce.5.cloned.1.call-done = (f32[24,256]{1,0:T(8,128)}, f32[24,256]{1,0:T(8,128)}, f32[24,256]{1,0:T(8,128)}) async-done(((f32[24,256]{1,0:T(8,128)}, f32[24,256]{1,0:T(8,128)}, f32[24,256]{1,0:T(8,128)}), (f32[24,256]{1,0:T(8,128)}, f32[24,256]{1,0:T(8,128)}, f32[24,256]{1,0:T(8,128)})) %all-reduce.5.cloned.1.call-update) | async-done | bytes 73744 | tf_op jit(solution)/shard_map/while/body/eval_jaxpr/psum | solution.py:54
  2093.0 10.9 add_subtract_fusion.2
  2113.7 69.6 %all-reduce.5.cloned.1.call-done = (f32[24,256]{1,0:T(8,128)}, f32[24,256]{1,0:T(8,128)}, f32[24,256]{1,0:T(8,128)}) async-done(((f32[24,256]{1,0:T(8,128)}, f32[24,256]{1,0:T(8,128)}, f32[24,256]{1,0:T(8,128)}), (f32[24,256]{1,0:T(8,128)}, f32[24,256]{1,0:T(8,128)}, f32[24,256]{1,0:T(8,128)})) %all-reduce.5.cloned.1.call-update) | async-done | bytes 73744 | tf_op jit(solution)/shard_map/while/body/eval_jaxpr/psum | solution.py:54
  2184.1 10.9 add_subtract_fusion.2
  2204.8 69.6 %all-reduce.5.cloned.1.call-done = (f32[24,256]{1,0:T(8,128)}, f32[24,256]{1,0:T(8,128)}, f32[24,256]{1,0:T(8,128)}) async-done(((f32[24,256]{1,0:T(8,128)}, f32[24,256]{1,0:T(8,128)}, f32[24,256]{1,0:T(8,128)}), (f32[24,256]{1,0:T(8,128)}, f32[24,256]{1,0:T(8,128)}, f32[24,256]{1,0:T(8,128)})) %all-reduce.5.cloned.1.call-update) | async-done | bytes 73744 | tf_op jit(solution)/shard_map/while/body/eval_jaxpr/psum | solution.py:54
  2275.3 10.9 add_subtract_fusion.2
  2296.0 69.6 %all-reduce.5.cloned.1.call-done = (f32[24,256]{1,0:T(8,128)}, f32[24,256]{1,0:T(8,128)}, f32[24,256]{1,0:T(8,128)}) async-done(((f32[24,256]{1,0:T(8,128)}, f32[24,256]{1,0:T(8,128)}, f32[24,256]{1,0:T(8,128)}), (f32[24,256]{1,0:T(8,128)}, f32[24,256]{1,0:T(8,128)}, f32[24,256]{1,0:T(8,128)})) %all-reduce.5.cloned.1.call-update) | async-done | bytes 73744 | tf_op jit(solution)/shard_map/while/body/eval_jaxpr/psum | solution.py:54
  2366.4 10.9 add_subtract_fusion.2
  2377.2 10.9 pad_maximum_fusion
  (171 shorter events, 274.5 us)
Async XLA Ops:
  7.2 68.0 %copy-start = (bf16[1024,1024]{1,0:T(8,128)(2,1)S(1)}, bf16[1024,1024]{1,0:T(8,128)(2,1)}, u32[]{:S(2)}) copy-start(bf16[1024,1024]{1,0:T(8,128)(2,1)} %param.14) | copy-start | bytes 6291460
  71.5 3.7 copy-start.3
  71.5 3.7 copy-start.4
  75.2 11.3 copy-start.5
  75.2 11.3 copy-start.6
  113.9 41.7 %all-to-all-start.1 = ((bf16[4,2,196608]{2,1,0:T(2,128)(2,1)}), bf16[4,2,196608]{2,1,0:T(2,128)(2,1)}, u32[]{:S(2)}, u32[]{:S(2)}) async-start(bf16[4,2,196608]{2,1,0:T(2,128)(2,1)} %reshape.44), calls=%async_computation.1 | async-start | bytes 6291456 | tf_op jit(solution)/shard_map/all_to_all | solution.py:44
  173.7 1.7 copy-start.2
  190.3 79.8 %all-reduce.5.cloned.1.call-start = ((), (), s32[]{:S(2)}) async-start(), calls=%async_computation.2 | async-start | bytes 147456 | tf_op jit(solution)/shard_map/while/body/eval_jaxpr/psum | solution.py:54
  281.7 79.4 %all-reduce.5.cloned.1.call-start = ((), (), s32[]{:S(2)}) async-start(), calls=%async_computation.2 | async-start | bytes 147456 | tf_op jit(solution)/shard_map/while/body/eval_jaxpr/psum | solution.py:54
  372.8 79.4 %all-reduce.5.cloned.1.call-start = ((), (), s32[]{:S(2)}) async-start(), calls=%async_computation.2 | async-start | bytes 147456 | tf_op jit(solution)/shard_map/while/body/eval_jaxpr/psum | solution.py:54
  463.9 79.4 %all-reduce.5.cloned.1.call-start = ((), (), s32[]{:S(2)}) async-start(), calls=%async_computation.2 | async-start | bytes 147456 | tf_op jit(solution)/shard_map/while/body/eval_jaxpr/psum | solution.py:54
  555.0 79.4 %all-reduce.5.cloned.1.call-start = ((), (), s32[]{:S(2)}) async-start(), calls=%async_computation.2 | async-start | bytes 147456 | tf_op jit(solution)/shard_map/while/body/eval_jaxpr/psum | solution.py:54
  646.2 79.4 %all-reduce.5.cloned.1.call-start = ((), (), s32[]{:S(2)}) async-start(), calls=%async_computation.2 | async-start | bytes 147456 | tf_op jit(solution)/shard_map/while/body/eval_jaxpr/psum | solution.py:54
  737.3 79.4 %all-reduce.5.cloned.1.call-start = ((), (), s32[]{:S(2)}) async-start(), calls=%async_computation.2 | async-start | bytes 147456 | tf_op jit(solution)/shard_map/while/body/eval_jaxpr/psum | solution.py:54
  828.4 79.4 %all-reduce.5.cloned.1.call-start = ((), (), s32[]{:S(2)}) async-start(), calls=%async_computation.2 | async-start | bytes 147456 | tf_op jit(solution)/shard_map/while/body/eval_jaxpr/psum | solution.py:54
  919.5 79.4 %all-reduce.5.cloned.1.call-start = ((), (), s32[]{:S(2)}) async-start(), calls=%async_computation.2 | async-start | bytes 147456 | tf_op jit(solution)/shard_map/while/body/eval_jaxpr/psum | solution.py:54
  1010.6 79.4 %all-reduce.5.cloned.1.call-start = ((), (), s32[]{:S(2)}) async-start(), calls=%async_computation.2 | async-start | bytes 147456 | tf_op jit(solution)/shard_map/while/body/eval_jaxpr/psum | solution.py:54
  1101.7 79.4 %all-reduce.5.cloned.1.call-start = ((), (), s32[]{:S(2)}) async-start(), calls=%async_computation.2 | async-start | bytes 147456 | tf_op jit(solution)/shard_map/while/body/eval_jaxpr/psum | solution.py:54
  1192.8 79.4 %all-reduce.5.cloned.1.call-start = ((), (), s32[]{:S(2)}) async-start(), calls=%async_computation.2 | async-start | bytes 147456 | tf_op jit(solution)/shard_map/while/body/eval_jaxpr/psum | solution.py:54
  1283.9 79.4 %all-reduce.5.cloned.1.call-start = ((), (), s32[]{:S(2)}) async-start(), calls=%async_computation.2 | async-start | bytes 147456 | tf_op jit(solution)/shard_map/while/body/eval_jaxpr/psum | solution.py:54
  1375.0 79.4 %all-reduce.5.cloned.1.call-start = ((), (), s32[]{:S(2)}) async-start(), calls=%async_computation.2 | async-start | bytes 147456 | tf_op jit(solution)/shard_map/while/body/eval_jaxpr/psum | solution.py:54
  1466.1 79.4 %all-reduce.5.cloned.1.call-start = ((), (), s32[]{:S(2)}) async-start(), calls=%async_computation.2 | async-start | bytes 147456 | tf_op jit(solution)/shard_map/while/body/eval_jaxpr/psum | solution.py:54
  1557.2 79.4 %all-reduce.5.cloned.1.call-start = ((), (), s32[]{:S(2)}) async-start(), calls=%async_computation.2 | async-start | bytes 147456 | tf_op jit(solution)/shard_map/while/body/eval_jaxpr/psum | solution.py:54
  1648.3 79.4 %all-reduce.5.cloned.1.call-start = ((), (), s32[]{:S(2)}) async-start(), calls=%async_computation.2 | async-start | bytes 147456 | tf_op jit(solution)/shard_map/while/body/eval_jaxpr/psum | solution.py:54
  1739.5 79.4 %all-reduce.5.cloned.1.call-start = ((), (), s32[]{:S(2)}) async-start(), calls=%async_computation.2 | async-start | bytes 147456 | tf_op jit(solution)/shard_map/while/body/eval_jaxpr/psum | solution.py:54
  1830.6 79.4 %all-reduce.5.cloned.1.call-start = ((), (), s32[]{:S(2)}) async-start(), calls=%async_computation.2 | async-start | bytes 147456 | tf_op jit(solution)/shard_map/while/body/eval_jaxpr/psum | solution.py:54
  1921.7 79.4 %all-reduce.5.cloned.1.call-start = ((), (), s32[]{:S(2)}) async-start(), calls=%async_computation.2 | async-start | bytes 147456 | tf_op jit(solution)/shard_map/while/body/eval_jaxpr/psum | solution.py:54
  2012.8 79.4 %all-reduce.5.cloned.1.call-start = ((), (), s32[]{:S(2)}) async-start(), calls=%async_computation.2 | async-start | bytes 147456 | tf_op jit(solution)/shard_map/while/body/eval_jaxpr/psum | solution.py:54
  2103.9 79.4 %all-reduce.5.cloned.1.call-start = ((), (), s32[]{:S(2)}) async-start(), calls=%async_computation.2 | async-start | bytes 147456 | tf_op jit(solution)/shard_map/while/body/eval_jaxpr/psum | solution.py:54
  2195.0 79.4 %all-reduce.5.cloned.1.call-start = ((), (), s32[]{:S(2)}) async-start(), calls=%async_computation.2 | async-start | bytes 147456 | tf_op jit(solution)/shard_map/while/body/eval_jaxpr/psum | solution.py:54
  2286.1 79.4 %all-reduce.5.cloned.1.call-start = ((), (), s32[]{:S(2)}) async-start(), calls=%async_computation.2 | async-start | bytes 147456 | tf_op jit(solution)/shard_map/while/body/eval_jaxpr/psum | solution.py:54
  2377.2 10.9 copy-start.1
Sparse Core Ops, SparseCore 0:
  200.2 69.7 all-reduce.4
  291.7 69.4 all-reduce.4
  382.8 69.4 all-reduce.4
  473.9 69.4 all-reduce.4
  565.0 69.4 all-reduce.4
  656.1 69.4 all-reduce.4
  747.2 69.4 all-reduce.4
  838.3 69.4 all-reduce.4
  929.4 69.4 all-reduce.4
  1020.5 69.4 all-reduce.4
  1111.7 69.4 all-reduce.4
  1202.8 69.4 all-reduce.4
  1293.9 69.4 all-reduce.4
  1385.0 69.4 all-reduce.4
  1476.1 69.4 all-reduce.4
  1567.2 69.4 all-reduce.4
  1658.3 69.4 all-reduce.4
  1749.4 69.4 all-reduce.4
  1840.5 69.4 all-reduce.4
  1931.6 69.4 all-reduce.4
  2022.7 69.4 all-reduce.4
  2113.8 69.4 all-reduce.4
  2205.0 69.4 all-reduce.4
  2296.1 69.4 all-reduce.4
where the time goes:
time: 2400 us
  waiting for transfers between devices  1680 us (70%)
  other arithmetic  548 us (23%)
  local copies, waits for them, and re-layouts  79.7 us (3%)
  blocking collectives  40.9 us (2%)
    psum x24, waiting for transfers between devices, sweep(): lax.psum((numer_real, numer_imag, denom), 'frame')  1670 us
    sub x24, other arithmetic, sweep(): new_imag = demix_imag - (coef_real * pick_imag + coef_imag * pick_real)  260 us
    reduce_sum x24, other arithmetic, sweep(): jnp.sum(weight * (demix_real * pick_real + demix_imag * pick_imag), axis=2)  209 us
  transfers between devices with their start and end apart: 25, of which 25 were waited for; matrix products, arithmetic and copies ran while one was open for 1% of the time, Pallas kernels for 0%

commit v1 on v0

v1 whole, which is shorter than its diff:
```python
import functools

import jax
import jax.numpy as jnp
from jax import lax
from jax.experimental import pallas as pl
from jax.experimental.pallas import tpu as pltpu
from jax.sharding import PartitionSpec as P

epsilon = 1e-05
power_floor = 0.001
variance_floor = 0.25
GROUP = 8
LANES = 128
BF16 = jnp.bfloat16
F32 = jnp.float32
SMEM = pltpu.SMEM
VMEM = pltpu.VMEM


def options(mib=48):
    return pltpu.CompilerParams(vmem_limit_bytes=mib * 1024 * 1024)


def cost(flops, moved, transcendentals=0):
    return pl.CostEstimate(
        flops=int(flops), bytes_accessed=int(moved), transcendentals=int(transcendentals)
    )


def exchange(value, axis, mask):
    size = lax.axis_size(axis)
    return lax.ppermute(value, axis, [(i, i ^ mask) for i in range(size)])


def prepare_kernel(place, x_ref, *refs, owners, each, chunks, count):
    powers, l_ref, rows = refs[:-2], refs[-2], refs[-1]
    mine = place[0]
    bins, frames = x_ref.shape[2], x_ref.shape[3]
    for c in range(chunks):
        for m in range(owners):
            for i in range(each):
                source = c * GROUP + (mine ^ m) * each + i
                re = x_ref[0, source].astype(F32)
                im = x_ref[1, source].astype(F32)
                powers[c * owners + m][i] = jnp.log(re * re + im * im + power_floor).astype(BF16)
    wide = frames // LANES
    for i in range(wide):
        block = x_ref[:, :, :, i * LANES : (i + 1) * LANES].astype(F32)
        rows[i] = block.reshape(2 * count * bins, LANES)

    def one(f, carry):
        both = jnp.concatenate(
            [rows[i, pl.ds(f, 2 * count, stride=bins), :] for i in range(wide)], axis=1
        )
        re, im = both[:count], both[count:]
        upper = jnp.concatenate([re, im], axis=1)
        lower = jnp.concatenate([im, -re], axis=1)
        l_ref[f] = jnp.concatenate([upper, lower], axis=0).astype(BF16)
        return carry

    lax.fori_loop(0, bins, one, 0)


def prepare(spectra, place, owners, each, chunks):
    _, count, bins, frames = spectra.shape
    step = 16
    power = jax.ShapeDtypeStruct((each, bins, frames), BF16)
    shapes = [power] * (chunks * owners)
    shapes.append(jax.ShapeDtypeStruct((bins, 2 * count, 2 * frames), BF16))
    specs = [pl.BlockSpec((each, step, frames), lambda b: (0, b, 0))] * (chunks * owners)
    specs.append(pl.BlockSpec((step, 2 * count, 2 * frames), lambda b: (b, 0, 0)))
    return pl.pallas_call(
        functools.partial(
            prepare_kernel, owners=owners, each=each, chunks=chunks, count=count
        ),
        grid=(bins // step,),
        in_specs=[
            pl.BlockSpec(memory_space=SMEM),
            pl.BlockSpec((2, count, step, frames), lambda b: (0, 0, b, 0)),
        ],
        out_specs=specs,
        out_shape=shapes,
        scratch_shapes=[VMEM((frames // LANES, 2 * count * step, LANES), F32)],
        compiler_params=options(),
        cost_estimate=cost(20 * spectra.size, 8 * spectra.size, spectra.size // 2),
        name="prepare",
    )(place, spectra)


def silu(v):
    return v / (1.0 + jnp.exp(-v))


def softplus(v):
    return jnp.maximum(v, 0.0) + jnp.log1p(jnp.exp(-jnp.abs(v)))


def model_kernel(place, *refs, owners):
    pieces = refs[:owners]
    gain, w_in, b_in, w_mid, b_mid, w_out, b_out = refs[owners : owners + 7]
    outs = refs[owners + 7 : 2 * owners + 7]
    normed, hidden = refs[2 * owners + 7 :]
    mine = place[0]
    bins, frames = pieces[0].shape[1:]
    total = bins * owners
    wide = frames // LANES

    def spread(column):
        return jnp.concatenate([column] * wide, axis=1)

    values = [piece[0].astype(F32) for piece in pieces]
    average = sum(jnp.sum(v, axis=0, keepdims=True) for v in values) / total
    values = [v - average for v in values]
    square = sum(jnp.sum(v * v, axis=0, keepdims=True) for v in values) / total
    scale = lax.rsqrt(square + epsilon)
    for m in range(owners):
        at = pl.multiple_of((mine ^ m) * bins, bins)
        normed[pl.ds(at, bins), :] = (
            values[m] * scale * spread(gain[pl.ds(at, bins), :])
        ).astype(BF16)

    tile = 256

    def layer(weights, bias, source, target):
        def one(h, carry):
            at = pl.multiple_of(h * tile, tile)
            v = jnp.dot(weights[pl.ds(at, tile), :], source[...], preferred_element_type=F32)
            target[pl.ds(at, tile), :] = silu(v + spread(bias[pl.ds(at, tile), :])).astype(BF16)
            return carry

        lax.fori_loop(0, weights.shape[0] // tile, one, 0)

    layer(w_in, b_in, normed, hidden)
    layer(w_mid, b_mid, hidden, normed)
    for m in range(owners):
        at = pl.multiple_of((mine ^ m) * bins, bins)
        v = jnp.dot(w_out[pl.ds(at, bins), :], normed[...], preferred_element_type=F32)
        outs[m][0] = (softplus(v + spread(b_out[pl.ds(at, bins), :])) + variance_floor).astype(
            BF16
        )


def model(pieces, place, weights):
    owners = len(pieces)
    each, bins, frames = pieces[0].shape
    hidden = weights[1].shape[0]
    block = pl.BlockSpec((1, bins, frames), lambda i: (i, 0, 0))
    whole = [pl.BlockSpec(w.shape, lambda i: (0, 0)) for w in weights]
    return pl.pallas_call(
        functools.partial(model_kernel, owners=owners),
        grid=(each,),
        in_specs=[pl.BlockSpec(memory_space=SMEM)] + [block] * owners + whole,
        out_specs=[block] * owners,
        out_shape=[jax.ShapeDtypeStruct((each, bins, frames), BF16)] * owners,
        scratch_shapes=[VMEM((hidden, frames), BF16), VMEM((hidden, frames), BF16)],
        compiler_params=options(),
        cost_estimate=cost(
            6 * each * hidden * hidden * frames, 6 * hidden * hidden, 8 * each * hidden * frames
        ),
        name="source_model",
    )(place, *pieces, *weights)


def covariance_kernel(table, place, l_ref, *refs, owners, count):
    pieces, o_ref, weight = refs[:owners], refs[owners], refs[owners + 1]
    mine = place[0]
    each, bins, frames = pieces[0].shape
    for m in range(owners):
        for i in range(each):
            weight[(mine ^ m) * each + i] = 1.0 / pieces[m][i].astype(F32)
    shape = (count, GROUP * count)
    row = lax.broadcasted_iota(jnp.int32, shape, 0)
    column = lax.rem(lax.broadcasted_iota(jnp.int32, shape, 1), count)
    real = row <= column

    def packed(f):
        left = l_ref[f]
        top = left.astype(F32)[:count]
        parts = []
        for j in range(GROUP):
            w = weight[j, pl.ds(f, 1), :]
            parts.append(top * jnp.concatenate([w, w], axis=1))
        right = jnp.concatenate(parts, axis=0)
        high = right.astype(BF16)
        low = (right - high.astype(F32)).astype(BF16)
        dims = (((1,), (1,)), ((), ()))
        v = lax.dot_general(left, high, dims, preferred_element_type=F32)
        v = v + lax.dot_general(left, low, dims, preferred_element_type=F32)
        return jnp.where(real, v[:count], v[count:])

    def one(p, carry):
        o_ref[0, p] = jnp.concatenate([packed(p), packed(p + bins // 2)], axis=1)
        return carry

    lax.fori_loop(0, bins // 2, one, 0)


def covariance(table, place, stacked, pieces, count):
    owners, shares = len(pieces), table.shape[0]
    each, bins, frames = pieces[0].shape
    share = stacked.shape[0] // lax.axis_size("frame")
    piece = pl.BlockSpec((each, share, frames), lambda r, table, place: (0, table[r], 0))
    lanes = 2 * GROUP * count
    return pl.pallas_call(
        functools.partial(covariance_kernel, owners=owners, count=count),
        grid_spec=pltpu.PrefetchScalarGridSpec(
            num_scalar_prefetch=2,
            grid=(shares,),
            in_specs=[
                pl.BlockSpec(
                    (share,) + stacked.shape[1:], lambda r, table, place: (table[r], 0, 0)
                )
            ]
            + [piece] * owners,
            out_specs=pl.BlockSpec(
                (1, share // 2, count, lanes), lambda r, table, place: (r, 0, 0, 0)
            ),
            scratch_shapes=[VMEM((GROUP, share, frames), F32)],
        ),
        out_shape=jax.ShapeDtypeStruct((shares, share // 2, count, lanes), F32),
        compiler_params=options(),
        cost_estimate=cost(
            shares * share * 8 * count * count * GROUP * frames * 2,
            shares * share * (8 * count * frames + 4 * count * count * GROUP),
        ),
        name="covariance",
    )(table, place, stacked, *pieces)


def unpack_kernel(*refs, count, share, lanes_b):
    parts, o_ref, turned = refs[:-2], refs[-2], refs[-1]
    half = GROUP * count
    blocks = o_ref.shape[1]

    def turn(a, carry):
        v = parts[0][:, a, :]
        for part in parts[1:]:
            v = v + part[:, a, :]
        v = jnp.concatenate([v[:, :half], v[:, half:]], axis=0)
        turned[a, :, 0:share] = v.T
        return carry

    lax.fori_loop(0, count, turn, 0)

    def lay(a, carry):
        for g in range(blocks):
            re, im = [], []
            for i in range(lanes_b):
                b = g * lanes_b + i
                if b >= count:
                    re.append(jnp.zeros((GROUP, share), F32))
                    im.append(jnp.zeros((GROUP, share), F32))
                    continue
                low, high = jnp.minimum(a, b), jnp.maximum(a, b)
                sign = jnp.where(a > b, 1.0, jnp.where(a < b, -1.0, 0.0))
                re.append(turned[low, pl.ds(high, GROUP, stride=count), :][:, :share])
                im.append(turned[high, pl.ds(low, GROUP, stride=count), :][:, :share] * sign)
            o_ref[a, g, 0] = jnp.concatenate(re, axis=1)
            o_ref[a, g, 1] = jnp.concatenate(im, axis=1)
        return carry

    lax.fori_loop(0, count, lay, 0)


def unpack(parts, count, share):
    lanes_b = LANES // share
    blocks = -(-count // lanes_b)
    shape = (count, blocks, 2, GROUP, LANES)
    return pl.pallas_call(
        functools.partial(unpack_kernel, count=count, share=share, lanes_b=lanes_b),
        out_shape=jax.ShapeDtypeStruct(shape, F32),
        scratch_shapes=[VMEM((count, GROUP * count, LANES), F32)],
        compiler_params=options(),
        cost_estimate=cost(10 * parts[0].size, 4 * parts[0].size * (len(parts) + 2)),
        name="unpack",
    )(*parts)


def sweep_kernel(*refs, count, share, frames):
    chunks = count // GROUP
    v_refs, o_ref, wr, wi, diagonal, flat = refs[:chunks], *refs[chunks:]
    lanes_b = LANES // share
    blocks = v_refs[0].shape[1]
    full = (GROUP, LANES)
    sub = lax.broadcasted_iota(jnp.int32, full, 0)
    lane = lax.broadcasted_iota(jnp.int32, full, 1)
    group = [(lane >= i * share) & (lane < (i + 1) * share) for i in range(lanes_b)]
    zero = jnp.zeros(full, F32)

    def start(a, carry):
        for c in range(chunks):
            wr[a, c] = jnp.where(sub + c * GROUP == a, 1.0, 0.0)
            wi[a, c] = zero
        return carry

    lax.fori_loop(0, count, start, 0)
    for c in range(chunks):
        for g in range(blocks):
            for part in range(2):
                d = zero
                for s in range(GROUP):
                    d = jnp.where(sub == s, v_refs[c][c * GROUP + s, g, part], d)
                diagonal[c, g, part] = d

    def total(x):
        shift = share
        while shift < LANES:
            x = x + pltpu.roll(x, shift, 1)
            shift *= 2
        return x

    for k in range(count):
        ck, sk = divmod(k, GROUP)
        used = k // lanes_b + 1
        pick_r, pick_i = [], []
        for g in range(used):
            pr, pi = zero, zero
            for i in range(lanes_b):
                b = g * lanes_b + i
                if b <= k:
                    pr = jnp.where(group[i], wr[b, ck, sk : sk + 1, :], pr)
                    pi = jnp.where(group[i], wi[b, ck, sk : sk + 1, :], pi)
            pick_r.append(pr)
            pick_i.append(pi)

        def product(load):
            ur, ui = zero, zero
            for g in range(used):
                vr, vi = load(g, 0), load(g, 1)
                ur = ur + vr * pick_r[g] + vi * pick_i[g]
                ui = ui + vi * pick_r[g] - vr * pick_i[g]
            return ur, ui

        def gather(a, carry):
            out = []
            kr = wr[a, ck, sk : sk + 1, :]
            ki = wi[a, ck, sk : sk + 1, :]
            for c in range(chunks):
                nr, ni, de = carry[3 * c : 3 * c + 3]
                ur, ui = product(lambda g, part: v_refs[c][a, g, part])
                ar, ai = wr[a, c], wi[a, c]
                out.append(nr + ar * ur - ai * ui)
                out.append(ni + ar * ui + ai * ur)
                out.append(de + kr * ur - ki * ui)
            return tuple(out)

        sums = lax.fori_loop(0, k + 1, gather, (zero,) * (3 * chunks))
        steer = []
        for c in range(chunks):
            nr, ni, de = sums[3 * c : 3 * c + 3]
            if (c + 1) * GROUP > k + 1:
                ur, ui = product(lambda g, part: diagonal[c, g, part])
                later = sub + c * GROUP > k
                nr = nr + jnp.where(later, ur, 0.0)
                ni = ni + jnp.where(later, ui, 0.0)
            nr, ni, de = total(nr), total(ni), total(de)
            inverse = 1.0 / de
            vr, vi = nr * inverse, ni * inverse
            if c == ck:
                vr = jnp.where(sub == sk, 1.0 - lax.rsqrt(de / frames), vr)
                vi = jnp.where(sub == sk, 0.0, vi)
            steer.append((vr, vi))

        def update(a, carry):
            kr = jnp.broadcast_to(wr[a, ck, sk : sk + 1, :], full)
            ki = jnp.broadcast_to(wi[a, ck, sk : sk + 1, :], full)
            for c in range(chunks):
                vr, vi = steer[c]
                wr[a, c] = wr[a, c] - (vr * kr - vi * ki)
                wi[a, c] = wi[a, c] - (vr * ki + vi * kr)
            return carry

        lax.fori_loop(0, k + 1, update, 0)

    def pack(a, carry):
        for c in range(chunks):
            at = c * GROUP * 2 * count + a
            flat[pl.ds(at, GROUP, stride=2 * count), :] = wr[a, c]
            flat[pl.ds(at + count, GROUP, stride=2 * count), :] = -wi[a, c]
        return carry

    lax.fori_loop(0, count, pack, 0)
    for i in range(flat.shape[0] // LANES):
        o_ref[:, i * LANES : (i + 1) * LANES] = flat[i * LANES : (i + 1) * LANES, :].T[:share]


def sweep(parts, count, share, frames):
    chunks = count // GROUP
    blocks = parts[0].shape[1]
    state = VMEM((count, chunks, GROUP, LANES), F32)
    return pl.pallas_call(
        functools.partial(sweep_kernel, count=count, share=share, frames=frames),
        out_shape=jax.ShapeDtypeStruct((share, 2 * count * count), F32),
        scratch_shapes=[
            state,
            state,
            VMEM((chunks, blocks, 2, GROUP, LANES), F32),
            VMEM((2 * count * count, LANES), F32),
        ],
        compiler_params=options(),
        cost_estimate=cost(4500 * count**3, 4 * 3 * parts[0].size),
        name="sweep",
    )(*parts)


def apply_kernel(table, w_ref, l_ref, o_ref, mixing, rows, *, count):
    share = w_ref.shape[1]
    frames = o_ref.shape[3]
    wide = 2 * count
    tiles = frames // LANES
    pad = jnp.zeros((share, LANES - wide), F32)
    for j in range(count):
        v = jnp.concatenate([w_ref[0, :, j * wide : (j + 1) * wide], pad], axis=1)
        mixing[pl.ds(j, share, stride=count), :] = v

    def one(f, carry):
        at = pl.multiple_of(f * count, count)
        w = mixing[pl.ds(at, count), 0:wide]
        high = w.astype(BF16).astype(F32)
        middle = (w - high).astype(BF16).astype(F32)
        low = w - high - middle
        left = jnp.concatenate([high, middle, low], axis=0).astype(BF16)
        y = jnp.dot(left, l_ref[f], preferred_element_type=F32)
        y = y[:count] + (y[count : 2 * count] + y[2 * count :])
        for c in range(2):
            for i in range(tiles):
                v = y[:, c * frames + i * LANES : c * frames + (i + 1) * LANES]
                rows[i, pl.ds(c * count * share + f, count, stride=share), :] = v
        return carry

    lax.fori_loop(0, share, one, 0)
    for i in range(tiles):
        o_ref[:, :, :, i * LANES : (i + 1) * LANES] = rows[i].reshape(2, count, share, LANES)


def apply(table, mixing, stacked, count):
    shares, share = mixing.shape[:2]
    bins, frames = stacked.shape[0], stacked.shape[2] // 2
    return pl.pallas_call(
        functools.partial(apply_kernel, count=count),
        grid_spec=pltpu.PrefetchScalarGridSpec(
            num_scalar_prefetch=1,
            grid=(shares,),
            in_specs=[
                pl.BlockSpec((1,) + mixing.shape[1:], lambda r, table: (r, 0, 0)),
                pl.BlockSpec((share,) + stacked.shape[1:], lambda r, table: (table[r], 0, 0)),
            ],
            out_specs=pl.BlockSpec(
                (2, count, share, frames), lambda r, table: (0, 0, table[r], 0)
            ),
            scratch_shapes=[
                VMEM((share * count, LANES), F32),
                VMEM((frames // LANES, 2 * count * share, LANES), F32),
            ],
        ),
        out_shape=jax.ShapeDtypeStruct((2, count, bins, frames), F32),
        compiler_params=options(),
        cost_estimate=cost(
            16 * count * count * bins * frames, stacked.size * 2 + 8 * count * bins * frames
        ),
        name="apply",
    )(table, mixing, stacked)


def on_device(spectra, norm_gain, w_in, b_in, w_mid, b_mid, w_out, b_out):
    _, count, bins, frames = spectra.shape
    owners, devices = lax.axis_size("freq"), lax.axis_size("frame")
    mine, position = lax.axis_index("freq"), lax.axis_index("frame")
    each, chunks, share, depth = GROUP // owners, count // GROUP, bins // devices, devices // 2
    place = jnp.reshape(mine, (1,)).astype(jnp.int32)
    side, level = position & 1, position >> 1
    order = jnp.arange(depth, dtype=jnp.int32)
    keep = (side * depth + (level ^ order)).astype(jnp.int32)
    send = ((side ^ 1) * depth + (level ^ order)).astype(jnp.int32)

    def column(v):
        return jnp.broadcast_to(v[:, None], (v.shape[0], LANES))

    weights = (
        column(norm_gain), w_in.T, column(b_in), w_mid.T, column(b_mid), w_out.T, column(b_out),
    )
    *powers, stacked = prepare(spectra, place, owners, each, chunks)

    modelled = []
    for c in range(chunks):
        pieces = powers[c * owners : (c + 1) * owners]
        pieces = [pieces[0]] + [exchange(pieces[m], "freq", m) for m in range(1, owners)]
        out = model(pieces, place, weights)
        modelled.append([out[0]] + [exchange(out[m], "freq", m) for m in range(1, owners)])

    laid = []
    for c in range(chunks):
        sent = covariance(send, place, stacked, modelled[c], count)
        kept = covariance(keep, place, stacked, modelled[c], count)
        parts = [None] * depth
        for r in list(range(1, depth)) + [0]:
            v = kept[r] + exchange(sent[r], "frame", 1)
            parts[r] = v if r == 0 else exchange(v, "frame", 2 * r)
        laid.append(unpack(parts, count, share))

    mixing = sweep(laid, count, share, frames * devices)
    near = [mixing] + [exchange(mixing, "frame", 2 * r) for r in range(1, depth)]
    far = [exchange(v, "frame", 1) for v in near]
    demixed = apply(jnp.concatenate([keep, send]), jnp.stack(near + far), stacked, count)

    natural = []
    for c in range(chunks):
        for p in range(owners):
            v = modelled[c][0]
            for m in range(1, owners):
                v = jnp.where((mine ^ p) == m, modelled[c][m], v)
            natural.append(v)
    return demixed, jnp.concatenate(natural, axis=0)


def solution(mesh):
    in_specs = (P(None, None, "freq", "frame"), P(), P(), P(), P(), P(), P(), P())
    out_specs = (P(None, None, "freq", "frame"), P(None, "freq", "frame"))
    return jax.shard_map(
        on_device, mesh=mesh, in_specs=in_specs, out_specs=out_specs, check_vma=False
    )
```

time: 2400 us -> 506 us (0.21)
  waiting for transfers between devices: 1680 us -> 65.5 us
  other arithmetic: 548 us -> 14.4 us
  Pallas kernels: 0 us -> 324 us
  starting transfers between devices: 4.92 us -> 84.4 us
  local copies, waits for them, and re-layouts: 79.7 us -> 15.7 us
  blocking collectives: 40.9 us -> 0 us
    psum x24 -> x0, waiting for transfers between devices: 1670 us -> none  [sweep(): lax.psum((numer_real, numer_imag, denom), 'frame')]
    pallas_call x0 -> x15, Pallas kernels: none -> 324 us  [the longest x6 177 us: covariance(): pl.pallas_call(functools.partial(covariance_kernel, owners=owners, count=...]
    sub x24 -> x0, other arithmetic: 260 us -> none  [sweep(): new_imag = demix_imag - (coef_real * pick_imag + coef_imag * pick_real)]
    reduce_sum x26 -> x0, other arithmetic: 211 us -> none  [the longest x24 209 us: sweep(): jnp.sum(weight * (demix_real * pick_real + demix_imag * pick_imag), axis=2)]
    ppermute x0 -> x46, starting transfers between devices: none -> 84.4 us  [exchange(): return lax.ppermute(value, axis, [(i, i ^ mask) for i in range(size)])]
    ppermute x0 -> x46, waiting for transfers between devices: none -> 65.5 us  [exchange(): return lax.ppermute(value, axis, [(i, i ^ mask) for i in range(size)])]
    all_to_all x1 -> x0, blocking collectives: 40.9 us -> none  [on_device(): lax.all_to_all(logpower, 'freq', split_axis=2, concat_axis=1, tiled=True)]
    mul x24 -> x0, other arithmetic: 26 us -> none  [sweep(): weight * (pick_real * pick_real + pick_imag * pick_imag)]
  transfers between devices with their start and end apart: 25 -> 46, of which waited for: 25 -> 9; matrix products, arithmetic and copies ran while one was open for 1% -> 6% of each run, Pallas kernels for 0% -> 45%
where the time goes in v1:
time: 506 us; the launch traced here: 505 us
  Pallas kernels  324 us (64%)
  starting transfers between devices  84.4 us (17%)
  waiting for transfers between devices  65.5 us (13%)
  local copies, waits for them, and re-layouts  15.7 us (3%)
  other arithmetic  14.4 us (3%)
    pallas_call x6, Pallas kernels, covariance(): pl.pallas_call(functools.partial(covariance_kernel, owners=owners, count=...  177 us
    ppermute x46, starting transfers between devices, exchange(): return lax.ppermute(value, axis, [(i, i ^ mask) for i in range(size)])  84.4 us
    ppermute x46, waiting for transfers between devices, exchange(): return lax.ppermute(value, axis, [(i, i ^ mask) for i in range(size)])  65.5 us
    pallas_call x1, Pallas kernels, apply(): pl.pallas_call(functools.partial(apply_kernel, count=count), grid_spec=pl...  55.2 us
    pallas_call x3, Pallas kernels, model(): pl.pallas_call(functools.partial(model_kernel, owners=owners), grid=(each...  34.5 us
    pallas_call x3, Pallas kernels, unpack(): pl.pallas_call(functools.partial(unpack_kernel, count=count, share=share,...  25.2 us
    pallas_call x1, Pallas kernels, prepare(): pl.pallas_call(functools.partial(prepare_kernel, owners=owners, each=each...  17.5 us
    pallas_call x1, Pallas kernels, sweep(): pl.pallas_call(functools.partial(sweep_kernel, count=count, share=share,...  14.5 us
  transfers between devices with their start and end apart: 46, of which 9 were waited for; matrix products, arithmetic and copies ran while one was open for 6% of the time, Pallas kernels for 45%

profile of v1, /device:TPU:0, one launch (start us, length us, event | category | flops | bytes accessed | tf_op | source)
XLA Modules:
  0.0 505.4 jit_solution(4171838777115312786)
XLA Ops:
  0.6 17.5 %prepare.1 = (bf16[2,256,256]{2,1,0:T(8,128)(2,1)S(1)}, bf16[2,256,256]{2,1,0:T(8,128)(2,1)}, bf16[2,256,256]{2,1,0:T(8,128)(2,1)}, bf16[2,256,256]{2,1,0:T(8,12...) custom-call(s32[1]{0:T(128)} %bitcast.place, ...), custom_call_target="tpu_custom_call" | custom-call | flops 62914560 | bytes 25165824 | tf_op jit(solution)/shard_map/prepare/pallas_call | solution.py:73
  18.6 2.5 collective-permute-start.1
  21.3 1.9 collective-permute-start.14
  23.3 3.9 copy.10
  27.2 3.9 copy.11
  31.1 4.0 copy.12
  35.5 1.6 collective-permute-start.28
  37.9 11.6 %source_model.3 = (bf16[2,256,256]{2,1,0:T(8,128)(2,1)S(1)}, bf16[2,256,256]{2,1,0:T(8,128)(2,1)S(1)}, bf16[2,256,256]{2,1,0:T(8,128)(2,1)S(1)}, bf16[2,256,256]{2,1,0:T(8,128)(2,1)S(1)}) custom-call(s32[1]{0:T(128)} %bitcast.place, bf16[2,256,256]{2,1,0:T(8,128)(2,1)S(1)} %get-tuple-element.28.refs_0_, ...), custom_call_target="tpu_custom_call" | custom-call | flops 3221225472 | bytes 6291456 | tf_op jit(solution)/shard_map/source_model/pallas_call | solution.py:150
  50.6 1.5 collective-permute-start.4
  52.1 11.4 %source_model.5 = (bf16[2,256,256]{2,1,0:T(8,128)(2,1)S(1)}, bf16[2,256,256]{2,1,0:T(8,128)(2,1)S(1)}, bf16[2,256,256]{2,1,0:T(8,128)(2,1)S(1)}, bf16[2,256,256]{2,1,0:T(8,128)(2,1)S(1)}) custom-call(s32[1]{0:T(128)} %bitcast.place, bf16[2,256,256]{2,1,0:T(8,128)(2,1)S(1)} %get-tuple-element.44.refs_0_, ...), custom_call_target="tpu_custom_call" | custom-call | flops 3221225472 | bytes 6291456 | tf_op jit(solution)/shard_map/source_model/pallas_call | solution.py:150
  64.2 1.3 collective-permute-start.31
  65.5 11.4 %source_model.4 = (bf16[2,256,256]{2,1,0:T(8,128)(2,1)S(1)}, bf16[2,256,256]{2,1,0:T(8,128)(2,1)S(1)}, bf16[2,256,256]{2,1,0:T(8,128)(2,1)S(1)}, bf16[2,256,256]{2,1,0:T(8,128)(2,1)S(1)}) custom-call(s32[1]{0:T(128)} %bitcast.place, bf16[2,256,256]{2,1,0:T(8,128)(2,1)S(1)} %get-tuple-element.36.refs_0_, ...), custom_call_target="tpu_custom_call" | custom-call | flops 3221225472 | bytes 6291456 | tf_op jit(solution)/shard_map/source_model/pallas_call | solution.py:150
  77.9 1.0 collective-permute-start.18
  78.9 29.6 %covariance.11 = f32[4,16,24,384]{3,2,1,0:T(8,128)S(1)} custom-call(s32[4]{0:T(128)S(1)} %fusion.12.table, s32[1]{0:T(128)} %bitcast.place, bf16[256,48,512]{2,1,0:T(8,128)(2,1)} %get-tuple-element.27.l_ref, bf16[2,256,256]{2,1,0:T(8,128)(2,1)S(1)} %get-tuple-element.48.refs_0_, bf16[2,256,256]{2,1,0:T(8,128)(2,1)S(1)} %collective-permute-done.29.refs_1_, ...), custom_call_target="tpu_custom_call" | custom-call | flops 2415919104 | bytes 8650752 | tf_op jit(solution)/shard_map/covariance/pallas_call | solution.py:205
  109.4 1.6 collective-permute-start.37
  111.4 29.6 %covariance.9 = f32[4,16,24,384]{3,2,1,0:T(8,128)S(1)} custom-call(s32[4]{0:T(128)S(1)} %fusion.12.table, s32[1]{0:T(128)} %bitcast.place, bf16[256,48,512]{2,1,0:T(8,128)(2,1)} %get-tuple-element.27.l_ref, bf16[2,256,256]{2,1,0:T(8,128)(2,1)S(1)} %get-tuple-element.40.refs_0_, bf16[2,256,256]{2,1,0:T(8,128)(2,1)S(1)} %collective-permute-done.16.refs_1_, ...), custom_call_target="tpu_custom_call" | custom-call | flops 2415919104 | bytes 8650752 | tf_op jit(solution)/shard_map/covariance/pallas_call | solution.py:205
  141.0 1.0 slice_bitcast_fusion.8
  142.0 1.6 collective-permute-start.33
  144.0 1.6 collective-permute-start.24
  145.6 0.9 select_dynamic-update-slice_fusion.11
  146.4 0.8 select_dynamic-update-slice_fusion.10
  147.3 0.8 select_dynamic-update-slice_fusion.9
  148.1 0.8 select_dynamic-update-slice_fusion.8
  148.9 0.8 select_dynamic-update-slice_fusion.7
  149.8 0.8 select_dynamic-update-slice_fusion.6
  150.6 0.8 select_dynamic-update-slice_fusion.5
  151.5 29.7 %covariance.7 = f32[4,16,24,384]{3,2,1,0:T(8,128)S(1)} custom-call(s32[4]{0:T(128)S(1)} %fusion.12.table, s32[1]{0:T(128)} %bitcast.place, bf16[256,48,512]{2,1,0:T(8,128)(2,1)} %get-tuple-element.27.l_ref, bf16[2,256,256]{2,1,0:T(8,128)(2,1)S(1)} %get-tuple-element.32.refs_0_, bf16[2,256,256]{2,1,0:T(8,128)(2,1)S(1)} %collective-permute-done.3.refs_1_, ...), custom_call_target="tpu_custom_call" | custom-call | flops 2415919104 | bytes 8650752 | tf_op jit(solution)/shard_map/covariance/pallas_call | solution.py:205
  181.2 1.0 slice_bitcast_fusion.16
  182.7 0.8 select_dynamic-update-slice_fusion.4
  183.5 1.6 collective-permute-start.20
  185.5 29.6 %covariance.10 = f32[4,16,24,384]{3,2,1,0:T(8,128)S(1)} custom-call(s32[4]{0:T(128)S(1)} %fusion.13.table, s32[1]{0:T(128)} %bitcast.place, bf16[256,48,512]{2,1,0:T(8,128)(2,1)} %get-tuple-element.27.l_ref, bf16[2,256,256]{2,1,0:T(8,128)(2,1)S(1)} %get-tuple-element.48.refs_0_, bf16[2,256,256]{2,1,0:T(8,128)(2,1)S(1)} %collective-permute-done.29.refs_1_, ...), custom_call_target="tpu_custom_call" | custom-call | flops 2415919104 | bytes 8650752 | tf_op jit(solution)/shard_map/covariance/pallas_call | solution.py:205
  215.1 29.6 %covariance.8 = f32[4,16,24,384]{3,2,1,0:T(8,128)S(1)} custom-call(s32[4]{0:T(128)S(1)} %fusion.13.table, s32[1]{0:T(128)} %bitcast.place, bf16[256,48,512]{2,1,0:T(8,128)(2,1)} %get-tuple-element.27.l_ref, bf16[2,256,256]{2,1,0:T(8,128)(2,1)S(1)} %get-tuple-element.40.refs_0_, bf16[2,256,256]{2,1,0:T(8,128)(2,1)S(1)} %collective-permute-done.16.refs_1_, ...), custom_call_target="tpu_custom_call" | custom-call | flops 2415919104 | bytes 8650752 | tf_op jit(solution)/shard_map/covariance/pallas_call | solution.py:205
  245.5 1.6 collective-permute-start.11
  247.5 1.6 collective-permute-start.7
  249.1 2.2 fusion
  251.7 3.7 collective-permute-start.38
  255.4 1.7 fusion.4
  257.1 4.8 collective-permute-done.11
  262.0 2.6 collective-permute-start.36
  264.6 10.0 %collective-permute-done.9 = f32[16,24,384]{2,1,0:T(8,128)S(1)} collective-permute-done((f32[16,24,384]{2,1,0:T(8,128)S(1)}, f32[16,24,384]{2,1,0:T(8,128)S(1)}, u32[]{:S(2)}, u32[]{:S(2)}) %collective-permute-start.9) | collective-permute-done | bytes 589856 | tf_op jit(solution)/shard_map/ppermute | solution.py:33
  274.6 1.6 collective-permute-start.34
  276.2 11.0 %collective-permute-done.7 = f32[16,24,384]{2,1,0:T(8,128)S(1)} collective-permute-done((f32[16,24,384]{2,1,0:T(8,128)S(1)}, f32[16,24,384]{2,1,0:T(8,128)S(1)}, u32[]{:S(2)}, u32[]{:S(2)}) %collective-permute-start.7) | collective-permute-done | bytes 589856 | tf_op jit(solution)/shard_map/ppermute | solution.py:33
  287.3 3.7 collective-permute-start.25
  290.9 0.8 select_dynamic-update-slice_fusion.3
  291.8 29.6 %covariance.6 = f32[4,16,24,384]{3,2,1,0:T(8,128)S(1)} custom-call(s32[4]{0:T(128)S(1)} %fusion.13.table, s32[1]{0:T(128)} %bitcast.place, bf16[256,48,512]{2,1,0:T(8,128)(2,1)} %get-tuple-element.27.l_ref, bf16[2,256,256]{2,1,0:T(8,128)(2,1)S(1)} %get-tuple-element.32.refs_0_, bf16[2,256,256]{2,1,0:T(8,128)(2,1)S(1)} %collective-permute-done.3.refs_1_, ...), custom_call_target="tpu_custom_call" | custom-call | flops 2415919104 | bytes 8650752 | tf_op jit(solution)/shard_map/covariance/pallas_call | solution.py:205
  321.8 1.4 collective-permute-start.21
  323.1 3.1 collective-permute-start.12
  326.3 34.0 %collective-permute-start.8 = (f32[16,24,384]{2,1,0:T(8,128)S(1)}, f32[16,24,384]{2,1,0:T(8,128)S(1)}, u32[]{:S(2)}, u32[]{:S(2)}) collective-permute-start(f32[16,24,384]{2,1,0:T(8,128)S(1)} %get-tuple-element.70), channel_id=1, source_target_pairs={{0,2},{1,3},{2,0},{3,1},{4,6},{5,7},{6,4},{7,5},{8,10},{9,11},{10,... | collective-permute-start | bytes 1769480 | tf_op jit(solution)/shard_map/ppermute | solution.py:33
  360.2 0.8 select_dynamic-update-slice_fusion.2
  361.0 0.8 select_dynamic-update-slice_fusion.1
  362.7 8.4 %unpack.5.refs_2_ = f32[24,6,2,8,128]{4,3,2,1,0:T(8,128)S(1)} custom-call(f32[16,24,384]{2,1,0:T(8,128)S(1)} %get-tuple-element.55.refs_0_, f32[16,24,384]{2,1,0:T(8,128)S(1)} %collective-permute-done.34.refs_1_, f32[16,24,384]{2,1,0:T(8,128)S(1)} %collective-permute-done.36.refs_2_, f32[16,24,384]{2,1,0:T(8,128)S(1)} %collective-permute-done.38.refs_3_), custom_call_target="tpu_custom_call" | custom-call | flops 1474560 | bytes 3538944 | tf_op jit(solution)/shard_map/unpack/pallas_call | solution.py:270
  371.1 8.5 %collective-permute-done.23.refs_2_ = f32[16,24,384]{2,1,0:T(8,128)S(1)} collective-permute-done((f32[16,24,384]{2,1,0:T(8,128)S(1)}, f32[16,24,384]{2,1,0:T(8,128)S(1)}, u32[]{:S(2)}, u32[]{:S(2)}) %collective-permute-start.23) | collective-permute-done | bytes 589856 | tf_op jit(solution)/shard_map/ppermute | solution.py:33
  379.6 8.4 %unpack.4.refs_1_ = f32[24,6,2,8,128]{4,3,2,1,0:T(8,128)S(1)} custom-call(f32[16,24,384]{2,1,0:T(8,128)S(1)} %get-tuple-element.63.refs_0_, f32[16,24,384]{2,1,0:T(8,128)S(1)} %collective-permute-done.21.refs_1_, f32[16,24,384]{2,1,0:T(8,128)S(1)} %collective-permute-done.23.refs_2_, f32[16,24,384]{2,1,0:T(8,128)S(1)} %collective-permute-done.25.refs_3_), custom_call_target="tpu_custom_call" | custom-call | flops 1474560 | bytes 3538944 | tf_op jit(solution)/shard_map/unpack/pallas_call | solution.py:270
  388.0 15.9 %collective-permute-done.10.refs_2_ = f32[16,24,384]{2,1,0:T(8,128)S(1)} collective-permute-done((f32[16,24,384]{2,1,0:T(8,128)S(1)}, f32[16,24,384]{2,1,0:T(8,128)S(1)}, u32[]{:S(2)}, u32[]{:S(2)}) %collective-permute-start.10) | collective-permute-done | bytes 589856 | tf_op jit(solution)/shard_map/ppermute | solution.py:33
  403.8 8.4 %unpack.3.refs_0_ = f32[24,6,2,8,128]{4,3,2,1,0:T(8,128)S(1)} custom-call(f32[16,24,384]{2,1,0:T(8,128)S(1)} %get-tuple-element.71.refs_0_, f32[16,24,384]{2,1,0:T(8,128)S(1)} %collective-permute-done.8.refs_1_, f32[16,24,384]{2,1,0:T(8,128)S(1)} %collective-permute-done.10.refs_2_, f32[16,24,384]{2,1,0:T(8,128)S(1)} %collective-permute-done.12.refs_3_), custom_call_target="tpu_custom_call" | custom-call | flops 1474560 | bytes 3538944 | tf_op jit(solution)/shard_map/unpack/pallas_call | solution.py:270
  412.2 14.5 %sweep.1 = f32[32,1152]{1,0:T(8,128)S(1)} custom-call(f32[24,6,2,8,128]{4,3,2,1,0:T(8,128)S(1)} %unpack.3.refs_0_, f32[24,6,2,8,128]{4,3,2,1,0:T(8,128)S(1)} %unpack.4.refs_1_, f32[24,6,2,8,128]{4,3,2,1,0:T(8,128)S(1)} %unpack.5.refs_2_), custom_call_target="tpu_custom_call" | custom-call | flops 62208000 | bytes 3538944 | tf_op jit(solution)/shard_map/sweep/pallas_call | solution.py:392
  426.8 1.6 collective-permute-start.42
  428.4 2.5 collective-permute-start.41
  430.9 1.9 collective-permute-start.39
  432.8 4.2 collective-permute-done.41
  437.5 4.7 collective-permute-done.40
  442.6 1.5 collective-permute-start.43
  444.2 5.9 %collective-permute-done.43 = f32[32,1152]{1,0:T(8,128)S(1)} collective-permute-done((f32[32,1152]{1,0:T(8,128)S(1)}, f32[32,1152]{1,0:T(8,128)S(1)}, u32[]{:S(2)}, u32[]{:S(2)}) %collective-permute-start.43) | collective-permute-done | bytes 147488 | tf_op jit(solution)/shard_map/ppermute | solution.py:33
  450.2 55.2 %apply.1 = f32[2,24,256,256]{3,2,1,0:T(8,128)} custom-call(s32[8]{0:T(128)S(1)} %pad_add_fusion.table, f32[8,32,1152]{2,1,0:T(8,128)S(1)} %bitcast_dynamic-update-slice_fusion.w_ref, bf16[256,48,512]{2,1,0:T(8,128)(2,1)} %get-tuple-element.27.l_ref), custom_call_target="tpu_custom_call" | custom-call | flops 603979776 | bytes 25165824 | tf_op jit(solution)/shard_map/apply/pallas_call | solution.py:440
  (97 shorter events, 11.3 us)
Async XLA Ops:
  18.2 17.1 %collective-permute-start = (bf16[2,256,256]{2,1,0:T(8,128)(2,1)}, bf16[2,256,256]{2,1,0:T(8,128)(2,1)S(1)}, u32[]{:S(2)}, u32[]{:S(2)}) collective-permute-start(bf16[2,256,256]{2,1,0:T(8,128)(2,1)} %get-tuple-element.29), channel_id=1, source_target_pairs={{0,8},{8,0},{16,24},{24,16},{1,9},{9,1},{17,25},{25,17},{2,10},{10... | collective-permute-start | bytes 786440 | tf_op jit(solution)/shard_map/ppermute | solution.py:33
  18.6 16.6 %collective-permute-start.1 = (bf16[2,256,256]{2,1,0:T(8,128)(2,1)}, bf16[2,256,256]{2,1,0:T(8,128)(2,1)}, u32[]{:S(2)}, u32[]{:S(2)}) collective-permute-start(bf16[2,256,256]{2,1,0:T(8,128)(2,1)} %get-tuple-element.30), channel_id=1, source_target_pairs={{0,16},{8,24},{16,0},{24,8},{1,17},{9,25},{17,1},{25,9},{2,18},{10... | collective-permute-start | bytes 786440 | tf_op jit(solution)/shard_map/ppermute | solution.py:33
  21.1 14.4 %collective-permute-start.2 = (bf16[2,256,256]{2,1,0:T(8,128)(2,1)S(1)}, bf16[2,256,256]{2,1,0:T(8,128)(2,1)}, u32[]{:S(2)}, u32[]{:S(2)}) collective-permute-start(bf16[2,256,256]{2,1,0:T(8,128)(2,1)S(1)} %get-tuple-element.31), channel_id=1, source_target_pairs={{0,24},{8,16},{16,8},{24,0},{1,25},{9,17},{17,9},{25,1},{2,26},{10... | collective-permute-start | bytes 786440 | tf_op jit(solution)/shard_map/ppermute | solution.py:33
  21.3 42.3 %collective-permute-start.13 = (bf16[2,256,256]{2,1,0:T(8,128)(2,1)S(1)}, bf16[2,256,256]{2,1,0:T(8,128)(2,1)S(1)}, u32[]{:S(2)}, u32[]{:S(2)}) collective-permute-start(bf16[2,256,256]{2,1,0:T(8,128)(2,1)S(1)} %get-tuple-element.37), channel_id=1, source_target_pairs={{0,8},{8,0},{16,24},{24,16},{1,9},{9,1},{17,25},{25,17},{2,10},{10... | collective-permute-start | bytes 786440 | tf_op jit(solution)/shard_map/ppermute | solution.py:33
  21.3 42.3 %collective-permute-start.14 = (bf16[2,256,256]{2,1,0:T(8,128)(2,1)S(1)}, bf16[2,256,256]{2,1,0:T(8,128)(2,1)S(1)}, u32[]{:S(2)}, u32[]{:S(2)}) collective-permute-start(bf16[2,256,256]{2,1,0:T(8,128)(2,1)S(1)} %get-tuple-element.38), channel_id=1, source_target_pairs={{0,16},{8,24},{16,0},{24,8},{1,17},{9,25},{17,1},{25,9},{2,18},{10... | collective-permute-start | bytes 786440 | tf_op jit(solution)/shard_map/ppermute | solution.py:33
  31.1 6.0 %copy-start.5 = (f32[1024]{0:T(1024)S(1)}, f32[1024]{0:T(1024)}, u32[]{:S(2)}) copy-start(f32[1024]{0:T(1024)} %param.9) | copy-start | bytes 12292
  31.1 6.2 %copy-start.6 = (f32[1024]{0:T(1024)S(1)}, f32[1024]{0:T(1024)}, u32[]{:S(2)}) copy-start(f32[1024]{0:T(1024)} %param.11) | copy-start | bytes 12292
  31.1 6.4 %copy-start.7 = (f32[1024]{0:T(1024)S(1)}, f32[1024]{0:T(1024)}, u32[]{:S(2)}) copy-start(f32[1024]{0:T(1024)} %param.13) | copy-start | bytes 12292
  31.1 6.6 %copy-start.8 = (f32[1024]{0:T(1024)S(1)}, f32[1024]{0:T(1024)}, u32[]{:S(2)}) copy-start(f32[1024]{0:T(1024)} %param.15) | copy-start | bytes 12292
  35.2 14.3 %collective-permute-start.26 = (bf16[2,256,256]{2,1,0:T(8,128)(2,1)S(1)}, bf16[2,256,256]{2,1,0:T(8,128)(2,1)S(1)}, u32[]{:S(2)}, u32[]{:S(2)}) collective-permute-start(bf16[2,256,256]{2,1,0:T(8,128)(2,1)S(1)} %get-tuple-element.45), channel_id=1, source_target_pairs={{0,8},{8,0},{16,24},{24,16},{1,9},{9,1},{17,25},{25,17},{2,10},{10... | collective-permute-start | bytes 786440 | tf_op jit(solution)/shard_map/ppermute | solution.py:33
  35.3 14.5 %collective-permute-start.27 = (bf16[2,256,256]{2,1,0:T(8,128)(2,1)S(1)}, bf16[2,256,256]{2,1,0:T(8,128)(2,1)S(1)}, u32[]{:S(2)}, u32[]{:S(2)}) collective-permute-start(bf16[2,256,256]{2,1,0:T(8,128)(2,1)S(1)} %get-tuple-element.46), channel_id=1, source_target_pairs={{0,16},{8,24},{16,0},{24,8},{1,17},{9,25},{17,1},{25,9},{2,18},{10... | collective-permute-start | bytes 786440 | tf_op jit(solution)/shard_map/ppermute | solution.py:33
  35.5 15.1 %collective-permute-start.28 = (bf16[2,256,256]{2,1,0:T(8,128)(2,1)S(1)}, bf16[2,256,256]{2,1,0:T(8,128)(2,1)S(1)}, u32[]{:S(2)}, u32[]{:S(2)}) collective-permute-start(bf16[2,256,256]{2,1,0:T(8,128)(2,1)S(1)} %get-tuple-element.47), channel_id=1, source_target_pairs={{0,24},{8,16},{16,8},{24,0},{1,25},{9,17},{17,9},{25,1},{2,26},{10... | collective-permute-start | bytes 786440 | tf_op jit(solution)/shard_map/ppermute | solution.py:33
  49.6 14.6 %collective-permute-start.15 = (bf16[2,256,256]{2,1,0:T(8,128)(2,1)S(1)}, bf16[2,256,256]{2,1,0:T(8,128)(2,1)S(1)}, u32[]{:S(2)}, u32[]{:S(2)}) collective-permute-start(bf16[2,256,256]{2,1,0:T(8,128)(2,1)S(1)} %get-tuple-element.39), channel_id=1, source_target_pairs={{0,24},{8,16},{16,8},{24,0},{1,25},{9,17},{17,9},{25,1},{2,26},{10... | collective-permute-start | bytes 786440 | tf_op jit(solution)/shard_map/ppermute | solution.py:33
  49.8 92.2 %collective-permute-start.3 = (bf16[2,256,256]{2,1,0:T(8,128)(2,1)S(1)}, bf16[2,256,256]{2,1,0:T(8,128)(2,1)S(1)}, u32[]{:S(2)}, u32[]{:S(2)}) collective-permute-start(bf16[2,256,256]{2,1,0:T(8,128)(2,1)S(1)} %get-tuple-element.33), channel_id=1, source_target_pairs={{0,8},{8,0},{16,24},{24,16},{1,9},{9,1},{17,25},{25,17},{2,10},{10... | collective-permute-start | bytes 786440 | tf_op jit(solution)/shard_map/ppermute | solution.py:33
  50.6 93.0 %collective-permute-start.4 = (bf16[2,256,256]{2,1,0:T(8,128)(2,1)S(1)}, bf16[2,256,256]{2,1,0:T(8,128)(2,1)S(1)}, u32[]{:S(2)}, u32[]{:S(2)}) collective-permute-start(bf16[2,256,256]{2,1,0:T(8,128)(2,1)S(1)} %get-tuple-element.34), channel_id=1, source_target_pairs={{0,16},{8,24},{16,0},{24,8},{1,17},{9,25},{17,1},{25,9},{2,18},{10... | collective-permute-start | bytes 786440 | tf_op jit(solution)/shard_map/ppermute | solution.py:33
  63.6 13.4 %collective-permute-start.29 = (bf16[2,256,256]{2,1,0:T(8,128)(2,1)S(1)}, bf16[2,256,256]{2,1,0:T(8,128)(2,1)S(1)}, u32[]{:S(2)}, u32[]{:S(2)}) collective-permute-start(bf16[2,256,256]{2,1,0:T(8,128)(2,1)S(1)} %get-tuple-element.49), channel_id=1, source_target_pairs={{0,8},{8,0},{16,24},{24,16},{1,9},{9,1},{17,25},{25,17},{2,10},{10... | collective-permute-start | bytes 786440 | tf_op jit(solution)/shard_map/ppermute | solution.py:33
  63.6 13.7 %collective-permute-start.30 = (bf16[2,256,256]{2,1,0:T(8,128)(2,1)S(1)}, bf16[2,256,256]{2,1,0:T(8,128)(2,1)S(1)}, u32[]{:S(2)}, u32[]{:S(2)}) collective-permute-start(bf16[2,256,256]{2,1,0:T(8,128)(2,1)S(1)} %get-tuple-element.50), channel_id=1, source_target_pairs={{0,16},{8,24},{16,0},{24,8},{1,17},{9,25},{17,1},{25,9},{2,18},{10... | collective-permute-start | bytes 786440 | tf_op jit(solution)/shard_map/ppermute | solution.py:33
  64.2 13.7 %collective-permute-start.31 = (bf16[2,256,256]{2,1,0:T(8,128)(2,1)S(1)}, bf16[2,256,256]{2,1,0:T(8,128)(2,1)S(1)}, u32[]{:S(2)}, u32[]{:S(2)}) collective-permute-start(bf16[2,256,256]{2,1,0:T(8,128)(2,1)S(1)} %get-tuple-element.51), channel_id=1, source_target_pairs={{0,24},{8,16},{16,8},{24,0},{1,25},{9,17},{17,9},{25,1},{2,26},{10... | collective-permute-start | bytes 786440 | tf_op jit(solution)/shard_map/ppermute | solution.py:33
  76.9 31.7 %collective-permute-start.16 = (bf16[2,256,256]{2,1,0:T(8,128)(2,1)S(1)}, bf16[2,256,256]{2,1,0:T(8,128)(2,1)S(1)}, u32[]{:S(2)}, u32[]{:S(2)}) collective-permute-start(bf16[2,256,256]{2,1,0:T(8,128)(2,1)S(1)} %get-tuple-element.41), channel_id=1, source_target_pairs={{0,8},{8,0},{16,24},{24,16},{1,9},{9,1},{17,25},{25,17},{2,10},{10... | collective-permute-start | bytes 786440 | tf_op jit(solution)/shard_map/ppermute | solution.py:33
  77.4 32.0 %collective-permute-start.17 = (bf16[2,256,256]{2,1,0:T(8,128)(2,1)S(1)}, bf16[2,256,256]{2,1,0:T(8,128)(2,1)S(1)}, u32[]{:S(2)}, u32[]{:S(2)}) collective-permute-start(bf16[2,256,256]{2,1,0:T(8,128)(2,1)S(1)} %get-tuple-element.42), channel_id=1, source_target_pairs={{0,16},{8,24},{16,0},{24,8},{1,17},{9,25},{17,1},{25,9},{2,18},{10... | collective-permute-start | bytes 786440 | tf_op jit(solution)/shard_map/ppermute | solution.py:33
  77.9 33.1 %collective-permute-start.18 = (bf16[2,256,256]{2,1,0:T(8,128)(2,1)S(1)}, bf16[2,256,256]{2,1,0:T(8,128)(2,1)S(1)}, u32[]{:S(2)}, u32[]{:S(2)}) collective-permute-start(bf16[2,256,256]{2,1,0:T(8,128)(2,1)S(1)} %get-tuple-element.43), channel_id=1, source_target_pairs={{0,24},{8,16},{16,8},{24,0},{1,25},{9,17},{17,9},{25,1},{2,26},{10... | collective-permute-start | bytes 786440 | tf_op jit(solution)/shard_map/ppermute | solution.py:33
  108.6 35.4 %collective-permute-start.5 = (bf16[2,256,256]{2,1,0:T(8,128)(2,1)S(1)}, bf16[2,256,256]{2,1,0:T(8,128)(2,1)S(1)}, u32[]{:S(2)}, u32[]{:S(2)}) collective-permute-start(bf16[2,256,256]{2,1,0:T(8,128)(2,1)S(1)} %get-tuple-element.35), channel_id=1, source_target_pairs={{0,24},{8,16},{16,8},{24,0},{1,25},{9,17},{17,9},{25,1},{2,26},{10... | collective-permute-start | bytes 786440 | tf_op jit(solution)/shard_map/ppermute | solution.py:33
  109.4 72.8 %collective-permute-start.37 = (f32[16,24,384]{2,1,0:T(8,128)S(1)}, f32[16,24,384]{2,1,0:T(8,128)S(1)}, u32[]{:S(2)}, u32[]{:S(2)}) collective-permute-start(f32[16,24,384]{2,1,0:T(8,128)S(1)} %get-tuple-element.56), channel_id=1, source_target_pairs={{0,1},{1,0},{2,3},{3,2},{4,5},{5,4},{6,7},{7,6},{8,9},{9,8},{10,11... | collective-permute-start | bytes 1769480 | tf_op jit(solution)/shard_map/ppermute | solution.py:33
  111.0 72.5 %collective-permute-start.35 = (f32[16,24,384]{2,1,0:T(8,128)S(1)}, f32[16,24,384]{2,1,0:T(8,128)S(1)}, u32[]{:S(2)}, u32[]{:S(2)}) collective-permute-start(f32[16,24,384]{2,1,0:T(8,128)S(1)} %get-tuple-element.57), channel_id=1, source_target_pairs={{0,1},{1,0},{2,3},{3,2},{4,5},{5,4},{6,7},{7,6},{8,9},{9,8},{10,11... | collective-permute-start | bytes 1769480 | tf_op jit(solution)/shard_map/ppermute | solution.py:33
  142.0 43.1 %collective-permute-start.33 = (f32[16,24,384]{2,1,0:T(8,128)S(1)}, f32[16,24,384]{2,1,0:T(8,128)S(1)}, u32[]{:S(2)}, u32[]{:S(2)}) collective-permute-start(f32[16,24,384]{2,1,0:T(8,128)S(1)} %get-tuple-element.58), channel_id=1, source_target_pairs={{0,1},{1,0},{2,3},{3,2},{4,5},{5,4},{6,7},{7,6},{8,9},{9,8},{10,11... | collective-permute-start | bytes 1769480 | tf_op jit(solution)/shard_map/ppermute | solution.py:33
  143.5 101.1 %collective-permute-start.32 = (f32[16,24,384]{2,1,0:T(8,128)S(1)}, f32[16,24,384]{2,1,0:T(8,128)S(1)}, u32[]{:S(2)}, u32[]{:S(2)}) collective-permute-start(f32[16,24,384]{2,1,0:T(8,128)S(1)} %get-tuple-element.59), channel_id=1, source_target_pairs={{0,1},{1,0},{2,3},{3,2},{4,5},{5,4},{6,7},{7,6},{8,9},{9,8},{10,11... | collective-permute-start | bytes 1769480 | tf_op jit(solution)/shard_map/ppermute | solution.py:33
  144.0 103.1 %collective-permute-start.24 = (f32[16,24,384]{2,1,0:T(8,128)}, f32[16,24,384]{2,1,0:T(8,128)S(1)}, u32[]{:S(2)}, u32[]{:S(2)}) collective-permute-start(f32[16,24,384]{2,1,0:T(8,128)} %get-tuple-element.64), channel_id=1, source_target_pairs={{0,1},{1,0},{2,3},{3,2},{4,5},{5,4},{6,7},{7,6},{8,9},{9,8},{10,11... | collective-permute-start | bytes 1769480 | tf_op jit(solution)/shard_map/ppermute | solution.py:33
  182.2 65.3 %collective-permute-start.22 = (f32[16,24,384]{2,1,0:T(8,128)S(1)}, f32[16,24,384]{2,1,0:T(8,128)}, u32[]{:S(2)}, u32[]{:S(2)}) collective-permute-start(f32[16,24,384]{2,1,0:T(8,128)S(1)} %get-tuple-element.65), channel_id=1, source_target_pairs={{0,1},{1,0},{2,3},{3,2},{4,5},{5,4},{6,7},{7,6},{8,9},{9,8},{10,11... | collective-permute-start | bytes 1769480 | tf_op jit(solution)/shard_map/ppermute | solution.py:33
  183.5 67.8 %collective-permute-start.20 = (f32[16,24,384]{2,1,0:T(8,128)S(1)}, f32[16,24,384]{2,1,0:T(8,128)}, u32[]{:S(2)}, u32[]{:S(2)}) collective-permute-start(f32[16,24,384]{2,1,0:T(8,128)S(1)} %get-tuple-element.66), channel_id=1, source_target_pairs={{0,1},{1,0},{2,3},{3,2},{4,5},{5,4},{6,7},{7,6},{8,9},{9,8},{10,11... | collective-permute-start | bytes 1769480 | tf_op jit(solution)/shard_map/ppermute | solution.py:33
  185.1 66.6 %collective-permute-start.19 = (f32[16,24,384]{2,1,0:T(8,128)S(1)}, f32[16,24,384]{2,1,0:T(8,128)}, u32[]{:S(2)}, u32[]{:S(2)}) collective-permute-start(f32[16,24,384]{2,1,0:T(8,128)S(1)} %get-tuple-element.67), channel_id=1, source_target_pairs={{0,1},{1,0},{2,3},{3,2},{4,5},{5,4},{6,7},{7,6},{8,9},{9,8},{10,11... | collective-permute-start | bytes 1769480 | tf_op jit(solution)/shard_map/ppermute | solution.py:33
  244.7 0.8 copy-start
  245.5 16.5 %collective-permute-start.11 = (f32[16,24,384]{2,1,0:T(8,128)}, f32[16,24,384]{2,1,0:T(8,128)S(1)}, u32[]{:S(2)}, u32[]{:S(2)}) collective-permute-start(f32[16,24,384]{2,1,0:T(8,128)} %get-tuple-element.72), channel_id=1, source_target_pairs={{0,1},{1,0},{2,3},{3,2},{4,5},{5,4},{6,7},{7,6},{8,9},{9,8},{10,11... | collective-permute-start | bytes 1769480 | tf_op jit(solution)/shard_map/ppermute | solution.py:33
  247.1 27.5 %collective-permute-start.9 = (f32[16,24,384]{2,1,0:T(8,128)S(1)}, f32[16,24,384]{2,1,0:T(8,128)S(1)}, u32[]{:S(2)}, u32[]{:S(2)}) collective-permute-start(f32[16,24,384]{2,1,0:T(8,128)S(1)} %get-tuple-element.73), channel_id=1, source_target_pairs={{0,1},{1,0},{2,3},{3,2},{4,5},{5,4},{6,7},{7,6},{8,9},{9,8},{10,11... | collective-permute-start | bytes 1769480 | tf_op jit(solution)/shard_map/ppermute | solution.py:33
  247.5 39.7 %collective-permute-start.7 = (f32[16,24,384]{2,1,0:T(8,128)S(1)}, f32[16,24,384]{2,1,0:T(8,128)S(1)}, u32[]{:S(2)}, u32[]{:S(2)}) collective-permute-start(f32[16,24,384]{2,1,0:T(8,128)S(1)} %get-tuple-element.74), channel_id=1, source_target_pairs={{0,1},{1,0},{2,3},{3,2},{4,5},{5,4},{6,7},{7,6},{8,9},{9,8},{10,11... | collective-permute-start | bytes 1769480 | tf_op jit(solution)/shard_map/ppermute | solution.py:33
  251.3 70.1 %collective-permute-start.6 = (f32[16,24,384]{2,1,0:T(8,128)S(1)}, f32[16,24,384]{2,1,0:T(8,128)S(1)}, u32[]{:S(2)}, u32[]{:S(2)}) collective-permute-start(f32[16,24,384]{2,1,0:T(8,128)S(1)} %get-tuple-element.75), channel_id=1, source_target_pairs={{0,1},{1,0},{2,3},{3,2},{4,5},{5,4},{6,7},{7,6},{8,9},{9,8},{10,11... | collective-permute-start | bytes 1769480 | tf_op jit(solution)/shard_map/ppermute | solution.py:33
  251.7 70.0 %collective-permute-start.38 = (f32[16,24,384]{2,1,0:T(8,128)}, f32[16,24,384]{2,1,0:T(8,128)S(1)}, u32[]{:S(2)}, u32[]{:S(2)}) collective-permute-start(f32[16,24,384]{2,1,0:T(8,128)} %get-tuple-element.52), channel_id=1, source_target_pairs={{0,6},{1,7},{2,4},{3,5},{4,2},{5,3},{6,0},{7,1},{8,14},{9,15},{10,... | collective-permute-start | bytes 1769480 | tf_op jit(solution)/shard_map/ppermute | solution.py:33
  262.0 61.2 %collective-permute-start.36 = (f32[16,24,384]{2,1,0:T(8,128)S(1)}, f32[16,24,384]{2,1,0:T(8,128)S(1)}, u32[]{:S(2)}, u32[]{:S(2)}) collective-permute-start(f32[16,24,384]{2,1,0:T(8,128)S(1)} %get-tuple-element.53), channel_id=1, source_target_pairs={{0,4},{1,5},{2,6},{3,7},{4,0},{5,1},{6,2},{7,3},{8,12},{9,13},{10,... | collective-permute-start | bytes 1769480 | tf_op jit(solution)/shard_map/ppermute | solution.py:33
  274.6 16.3 %copy-start.1 = (f32[16,24,384]{2,1,0:T(8,128)}, f32[16,24,384]{2,1,0:T(8,128)S(1)}, u32[]{:S(2)}) copy-start(f32[16,24,384]{2,1,0:T(8,128)S(1)} %collective-permute-done.9) | copy-start | bytes 1769476
  274.6 51.6 %collective-permute-start.34 = (f32[16,24,384]{2,1,0:T(8,128)S(1)}, f32[16,24,384]{2,1,0:T(8,128)S(1)}, u32[]{:S(2)}, u32[]{:S(2)}) collective-permute-start(f32[16,24,384]{2,1,0:T(8,128)S(1)} %get-tuple-element.54), channel_id=1, source_target_pairs={{0,2},{1,3},{2,0},{3,1},{4,6},{5,7},{6,4},{7,5},{8,10},{9,11},{10,... | collective-permute-start | bytes 1769480 | tf_op jit(solution)/shard_map/ppermute | solution.py:33
  287.3 3.7 copy-start.3
  287.3 39.0 %collective-permute-start.25 = (f32[16,24,384]{2,1,0:T(8,128)S(1)}, f32[16,24,384]{2,1,0:T(8,128)S(1)}, u32[]{:S(2)}, u32[]{:S(2)}) collective-permute-start(f32[16,24,384]{2,1,0:T(8,128)S(1)} %get-tuple-element.60), channel_id=1, source_target_pairs={{0,6},{1,7},{2,4},{3,5},{4,2},{5,3},{6,0},{7,1},{8,14},{9,15},{10,... | collective-permute-start | bytes 1769480 | tf_op jit(solution)/shard_map/ppermute | solution.py:33
  291.8 29.7 %copy-start.2 = (f32[16,24,384]{2,1,0:T(8,128)S(1)}, f32[16,24,384]{2,1,0:T(8,128)}, u32[]{:S(2)}) copy-start(f32[16,24,384]{2,1,0:T(8,128)} %copy-done.1) | copy-start | bytes 1769476
  291.8 29.7 %copy-start.4 = (f32[16,24,384]{2,1,0:T(8,128)S(1)}, f32[16,24,384]{2,1,0:T(8,128)}, u32[]{:S(2)}) copy-start(f32[16,24,384]{2,1,0:T(8,128)} %copy-done.3) | copy-start | bytes 1769476
  321.3 58.2 %collective-permute-start.23 = (f32[16,24,384]{2,1,0:T(8,128)S(1)}, f32[16,24,384]{2,1,0:T(8,128)S(1)}, u32[]{:S(2)}, u32[]{:S(2)}) collective-permute-start(f32[16,24,384]{2,1,0:T(8,128)S(1)} %get-tuple-element.61), channel_id=1, source_target_pairs={{0,4},{1,5},{2,6},{3,7},{4,0},{5,1},{6,2},{7,3},{8,12},{9,13},{10,... | collective-permute-start | bytes 1769480 | tf_op jit(solution)/shard_map/ppermute | solution.py:33
  321.8 57.8 %collective-permute-start.21 = (f32[16,24,384]{2,1,0:T(8,128)S(1)}, f32[16,24,384]{2,1,0:T(8,128)S(1)}, u32[]{:S(2)}, u32[]{:S(2)}) collective-permute-start(f32[16,24,384]{2,1,0:T(8,128)S(1)} %get-tuple-element.62), channel_id=1, source_target_pairs={{0,2},{1,3},{2,0},{3,1},{4,6},{5,7},{6,4},{7,5},{8,10},{9,11},{10,... | collective-permute-start | bytes 1769480 | tf_op jit(solution)/shard_map/ppermute | solution.py:33
  323.1 64.8 %collective-permute-start.12 = (f32[16,24,384]{2,1,0:T(8,128)S(1)}, f32[16,24,384]{2,1,0:T(8,128)S(1)}, u32[]{:S(2)}, u32[]{:S(2)}) collective-permute-start(f32[16,24,384]{2,1,0:T(8,128)S(1)} %get-tuple-element.68), channel_id=1, source_target_pairs={{0,6},{1,7},{2,4},{3,5},{4,2},{5,3},{6,0},{7,1},{8,14},{9,15},{10,... | collective-permute-start | bytes 1769480 | tf_op jit(solution)/shard_map/ppermute | solution.py:33
  326.2 77.6 %collective-permute-start.10 = (f32[16,24,384]{2,1,0:T(8,128)S(1)}, f32[16,24,384]{2,1,0:T(8,128)S(1)}, u32[]{:S(2)}, u32[]{:S(2)}) collective-permute-start(f32[16,24,384]{2,1,0:T(8,128)S(1)} %get-tuple-element.69), channel_id=1, source_target_pairs={{0,4},{1,5},{2,6},{3,7},{4,0},{5,1},{6,2},{7,3},{8,12},{9,13},{10,... | collective-permute-start | bytes 1769480 | tf_op jit(solution)/shard_map/ppermute | solution.py:33
  326.3 77.6 %collective-permute-start.8 = (f32[16,24,384]{2,1,0:T(8,128)S(1)}, f32[16,24,384]{2,1,0:T(8,128)S(1)}, u32[]{:S(2)}, u32[]{:S(2)}) collective-permute-start(f32[16,24,384]{2,1,0:T(8,128)S(1)} %get-tuple-element.70), channel_id=1, source_target_pairs={{0,2},{1,3},{2,0},{3,1},{4,6},{5,7},{6,4},{7,5},{8,10},{9,11},{10,... | collective-permute-start | bytes 1769480 | tf_op jit(solution)/shard_map/ppermute | solution.py:33
  426.8 17.4 %collective-permute-start.42 = (f32[32,1152]{1,0:T(8,128)S(1)}, f32[32,1152]{1,0:T(8,128)S(1)}, u32[]{:S(2)}, u32[]{:S(2)}) collective-permute-start(f32[32,1152]{1,0:T(8,128)S(1)} %sweep.1), channel_id=1, source_target_pairs={{0,1},{1,0},{2,3},{3,2},{4,5},{5,4},{6,7},{7,6},{8,9},{9,8},{10,11... | collective-permute-start | bytes 442376 | tf_op jit(solution)/shard_map/ppermute | solution.py:33
  428.4 8.6 %collective-permute-start.41 = (f32[32,1152]{1,0:T(8,128)S(1)}, f32[32,1152]{1,0:T(8,128)S(1)}, u32[]{:S(2)}, u32[]{:S(2)}) collective-permute-start(f32[32,1152]{1,0:T(8,128)S(1)} %sweep.1), channel_id=1, source_target_pairs={{0,6},{1,7},{2,4},{3,5},{4,2},{5,3},{6,0},{7,1},{8,14},{9,15},{10,... | collective-permute-start | bytes 442376 | tf_op jit(solution)/shard_map/ppermute | solution.py:33
  430.9 11.2 %collective-permute-start.40 = (f32[32,1152]{1,0:T(8,128)S(1)}, f32[32,1152]{1,0:T(8,128)S(1)}, u32[]{:S(2)}, u32[]{:S(2)}) collective-permute-start(f32[32,1152]{1,0:T(8,128)S(1)} %sweep.1), channel_id=1, source_target_pairs={{0,4},{1,5},{2,6},{3,7},{4,0},{5,1},{6,2},{7,3},{8,12},{9,13},{10,... | collective-permute-start | bytes 442376 | tf_op jit(solution)/shard_map/ppermute | solution.py:33
  430.9 11.7 %collective-permute-start.39 = (f32[32,1152]{1,0:T(8,128)S(1)}, f32[32,1152]{1,0:T(8,128)S(1)}, u32[]{:S(2)}, u32[]{:S(2)}) collective-permute-start(f32[32,1152]{1,0:T(8,128)S(1)} %sweep.1), channel_id=1, source_target_pairs={{0,2},{1,3},{2,0},{3,1},{4,6},{5,7},{6,4},{7,5},{8,10},{9,11},{10,... | collective-permute-start | bytes 442376 | tf_op jit(solution)/shard_map/ppermute | solution.py:33
  436.9 13.2 %collective-permute-start.45 = (f32[32,1152]{1,0:T(8,128)S(1)}, f32[32,1152]{1,0:T(8,128)S(1)}, u32[]{:S(2)}, u32[]{:S(2)}) collective-permute-start(f32[32,1152]{1,0:T(8,128)S(1)} %collective-permute-done.41), channel_id=1, source_target_pairs={{0,1},{1,0},{2,3},{3,2},{4,5},{5,4},{6,7},{7,6},{8,9},{9,8},{10,11... | collective-permute-start | bytes 442376 | tf_op jit(solution)/shard_map/ppermute | solution.py:33
  442.1 8.0 %collective-permute-start.44 = (f32[32,1152]{1,0:T(8,128)S(1)}, f32[32,1152]{1,0:T(8,128)S(1)}, u32[]{:S(2)}, u32[]{:S(2)}) collective-permute-start(f32[32,1152]{1,0:T(8,128)S(1)} %collective-permute-done.40), channel_id=1, source_target_pairs={{0,1},{1,0},{2,3},{3,2},{4,5},{5,4},{6,7},{7,6},{8,9},{9,8},{10,11... | collective-permute-start | bytes 442376 | tf_op jit(solution)/shard_map/ppermute | solution.py:33
  442.6 7.5 %collective-permute-start.43 = (f32[32,1152]{1,0:T(8,128)S(1)}, f32[32,1152]{1,0:T(8,128)S(1)}, u32[]{:S(2)}, u32[]{:S(2)}) collective-permute-start(f32[32,1152]{1,0:T(8,128)S(1)} %collective-permute-done.39), channel_id=1, source_target_pairs={{0,1},{1,0},{2,3},{3,2},{4,5},{5,4},{6,7},{7,6},{8,9},{9,8},{10,11... | collective-permute-start | bytes 442376 | tf_op jit(solution)/shard_map/ppermute | solution.py:33

commit v2 on v1

--- a/solution.py
+++ b/solution.py
@@ -45,13 +45,16 @@
                 im = x_ref[1, source].astype(F32)
                 powers[c * owners + m][i] = jnp.log(re * re + im * im + power_floor).astype(BF16)
     wide = frames // LANES
+    pitch = rows.shape[1] // (2 * count)
     for i in range(wide):
         block = x_ref[:, :, :, i * LANES : (i + 1) * LANES].astype(F32)
-        rows[i] = block.reshape(2 * count * bins, LANES)
+        block = block.reshape(2 * count, bins, LANES)
+        for n in range(2 * count):
+            rows[i, n * pitch : n * pitch + bins] = block[n]
 
     def one(f, carry):
         both = jnp.concatenate(
-            [rows[i, pl.ds(f, 2 * count, stride=bins), :] for i in range(wide)], axis=1
+            [rows[i, pl.ds(f, 2 * count, stride=pitch), :] for i in range(wide)], axis=1
         )
         re, im = both[:count], both[count:]
         upper = jnp.concatenate([re, im], axis=1)
@@ -59,7 +62,7 @@
         l_ref[f] = jnp.concatenate([upper, lower], axis=0).astype(BF16)
         return carry
 
-    lax.fori_loop(0, bins, one, 0)
+    lax.fori_loop(0, bins, one, 0, unroll=8)
 
 
 def prepare(spectra, place, owners, each, chunks):
@@ -81,7 +84,7 @@
         ],
         out_specs=specs,
         out_shape=shapes,
-        scratch_shapes=[VMEM((frames // LANES, 2 * count * step, LANES), F32)],
+        scratch_shapes=[VMEM((frames // LANES, 2 * count * (step + 8), LANES), F32)],
         compiler_params=options(),
         cost_estimate=cost(20 * spectra.size, 8 * spectra.size, spectra.size // 2),
         name="prepare",
@@ -129,7 +132,7 @@
             target[pl.ds(at, tile), :] = silu(v + spread(bias[pl.ds(at, tile), :])).astype(BF16)
             return carry
 
-        lax.fori_loop(0, weights.shape[0] // tile, one, 0)
+        lax.fori_loop(0, weights.shape[0] // tile, one, 0, unroll=4)
 
     layer(w_in, b_in, normed, hidden)
     layer(w_mid, b_mid, hidden, normed)
@@ -163,18 +166,22 @@
 
 
 def covariance_kernel(table, place, l_ref, *refs, owners, count):
-    pieces, o_ref, weight = refs[:owners], refs[owners], refs[owners + 1]
+    pieces, (_, o_ref, natural, weight) = refs[:owners], refs[owners:]
     mine = place[0]
     each, bins, frames = pieces[0].shape
     for m in range(owners):
         for i in range(each):
-            weight[(mine ^ m) * each + i] = 1.0 / pieces[m][i].astype(F32)
+            source = (mine ^ m) * each + i
+            natural[source] = pieces[m][i]
+            weight[source] = 1.0 / pieces[m][i].astype(F32)
     shape = (count, GROUP * count)
     row = lax.broadcasted_iota(jnp.int32, shape, 0)
     column = lax.rem(lax.broadcasted_iota(jnp.int32, shape, 1), count)
     real = row <= column
-
-    def packed(f):
+    half = bins // 2
+    together = min(8, half)
+
+    def weighted(f):
         left = l_ref[f]
         top = left.astype(F32)[:count]
         parts = []
@@ -183,20 +190,26 @@
             parts.append(top * jnp.concatenate([w, w], axis=1))
         right = jnp.concatenate(parts, axis=0)
         high = right.astype(BF16)
-        low = (right - high.astype(F32)).astype(BF16)
+        return left, high, (right - high.astype(F32)).astype(BF16)
+
+    def summed(left, high, low):
         dims = (((1,), (1,)), ((), ()))
         v = lax.dot_general(left, high, dims, preferred_element_type=F32)
         v = v + lax.dot_general(left, low, dims, preferred_element_type=F32)
         return jnp.where(real, v[:count], v[count:])
 
-    def one(p, carry):
-        o_ref[0, p] = jnp.concatenate([packed(p), packed(p + bins // 2)], axis=1)
-        return carry
-
-    lax.fori_loop(0, bins // 2, one, 0)
-
-
-def covariance(table, place, stacked, pieces, count):
+    def some(n, carry):
+        first = n * together
+        operands = [weighted(first + i + e * half) for i in range(together) for e in range(2)]
+        sums = [summed(*o) for o in operands]
+        for i in range(together):
+            o_ref[0, first + i] = jnp.concatenate([sums[2 * i], sums[2 * i + 1]], axis=1)
+        return carry
+
+    lax.fori_loop(0, half // together, some, 0)
+
+
+def covariance(table, place, stacked, pieces, natural, chunk, count):
     owners, shares = len(pieces), table.shape[0]
     each, bins, frames = pieces[0].shape
     share = stacked.shape[0] // lax.axis_size("frame")
@@ -212,20 +225,30 @@
                     (share,) + stacked.shape[1:], lambda r, table, place: (table[r], 0, 0)
                 )
             ]
-            + [piece] * owners,
-            out_specs=pl.BlockSpec(
-                (1, share // 2, count, lanes), lambda r, table, place: (r, 0, 0, 0)
-            ),
+            + [piece] * owners
+            + [pl.BlockSpec(memory_space=pl.ANY)],
+            out_specs=[
+                pl.BlockSpec(
+                    (1, share // 2, count, lanes), lambda r, table, place: (r, 0, 0, 0)
+                ),
+                pl.BlockSpec(
+                    (GROUP, share, frames), lambda r, table, place: (chunk, table[r], 0)
+                ),
+            ],
             scratch_shapes=[VMEM((GROUP, share, frames), F32)],
         ),
-        out_shape=jax.ShapeDtypeStruct((shares, share // 2, count, lanes), F32),
+        out_shape=[
+            jax.ShapeDtypeStruct((shares, share // 2, count, lanes), F32),
+            jax.ShapeDtypeStruct((count, bins, frames), BF16),
+        ],
+        input_output_aliases={} if natural.shape[0] != count else {3 + owners: 1},
         compiler_params=options(),
         cost_estimate=cost(
             shares * share * 8 * count * count * GROUP * frames * 2,
             shares * share * (8 * count * frames + 4 * count * count * GROUP),
         ),
         name="covariance",
-    )(table, place, stacked, *pieces)
+    )(table, place, stacked, *pieces, natural)
 
 
 def unpack_kernel(*refs, count, share, lanes_b):
@@ -241,7 +264,7 @@
         turned[a, :, 0:share] = v.T
         return carry
 
-    lax.fori_loop(0, count, turn, 0)
+    lax.fori_loop(0, count, turn, 0, unroll=8)
 
     def lay(a, carry):
         for g in range(blocks):
@@ -260,7 +283,7 @@
             o_ref[a, g, 1] = jnp.concatenate(im, axis=1)
         return carry
 
-    lax.fori_loop(0, count, lay, 0)
+    lax.fori_loop(0, count, lay, 0, unroll=4)
 
 
 def unpack(parts, count, share):
@@ -345,7 +368,7 @@
                 out.append(de + kr * ur - ki * ui)
             return tuple(out)
 
-        sums = lax.fori_loop(0, k + 1, gather, (zero,) * (3 * chunks))
+        sums = lax.fori_loop(0, k + 1, gather, (zero,) * (3 * chunks), unroll=min(2, k + 1))
         steer = []
         for c in range(chunks):
             nr, ni, de = sums[3 * c : 3 * c + 3]
@@ -371,7 +394,7 @@
                 wi[a, c] = wi[a, c] - (vr * ki + vi * kr)
             return carry
 
-        lax.fori_loop(0, k + 1, update, 0)
+        lax.fori_loop(0, k + 1, update, 0, unroll=min(2, k + 1))
 
     def pack(a, carry):
         for c in range(chunks):
@@ -409,6 +432,7 @@
     frames = o_ref.shape[3]
     wide = 2 * count
     tiles = frames // LANES
+    pitch = share + 8
     pad = jnp.zeros((share, LANES - wide), F32)
     for j in range(count):
         v = jnp.concatenate([w_ref[0, :, j * wide : (j + 1) * wide], pad], axis=1)
@@ -426,12 +450,13 @@
         for c in range(2):
             for i in range(tiles):
                 v = y[:, c * frames + i * LANES : c * frames + (i + 1) * LANES]
-                rows[i, pl.ds(c * count * share + f, count, stride=share), :] = v
-        return carry
-
-    lax.fori_loop(0, share, one, 0)
+                rows[i, pl.ds(c * count * pitch + f, count, stride=pitch), :] = v
+        return carry
+
+    lax.fori_loop(0, share, one, 0, unroll=8)
     for i in range(tiles):
-        o_ref[:, :, :, i * LANES : (i + 1) * LANES] = rows[i].reshape(2, count, share, LANES)
+        v = rows[i].reshape(2, count, pitch, LANES)[:, :, :share]
+        o_ref[:, :, :, i * LANES : (i + 1) * LANES] = v
 
 
 def apply(table, mixing, stacked, count):
@@ -451,7 +476,7 @@
             ),
             scratch_shapes=[
                 VMEM((share * count, LANES), F32),
-                VMEM((frames // LANES, 2 * count * share, LANES), F32),
+                VMEM((frames // LANES, 2 * count * (share + 8), LANES), F32),
             ],
         ),
         out_shape=jax.ShapeDtypeStruct((2, count, bins, frames), F32),
@@ -490,9 +515,10 @@
         modelled.append([out[0]] + [exchange(out[m], "freq", m) for m in range(1, owners)])
 
     laid = []
+    variances = place
     for c in range(chunks):
-        sent = covariance(send, place, stacked, modelled[c], count)
-        kept = covariance(keep, place, stacked, modelled[c], count)
+        sent, variances = covariance(send, place, stacked, modelled[c], variances, c, count)
+        kept, variances = covariance(keep, place, stacked, modelled[c], variances, c, count)
         parts = [None] * depth
         for r in list(range(1, depth)) + [0]:
             v = kept[r] + exchange(sent[r], "frame", 1)
@@ -504,14 +530,7 @@
     far = [exchange(v, "frame", 1) for v in near]
     demixed = apply(jnp.concatenate([keep, send]), jnp.stack(near + far), stacked, count)
 
-    natural = []
-    for c in range(chunks):
-        for p in range(owners):
-            v = modelled[c][0]
-            for m in range(1, owners):
-                v = jnp.where((mine ^ p) == m, modelled[c][m], v)
-            natural.append(v)
-    return demixed, jnp.concatenate(natural, axis=0)
+    return demixed, variances
 
 
 def solution(mesh):

time: 506 us -> 424 us (0.84)
  Pallas kernels: 324 us -> 206 us
  waiting for transfers between devices: 65.5 us -> 114 us
  other arithmetic: 14.4 us -> 1.92 us
    pallas_call x6, Pallas kernels: 177 us -> 122 us  [covariance(): pl.pallas_call(functools.partial(covariance_kernel, owners=owners, count=...]
    ppermute x46, waiting for transfers between devices: 65.5 us -> 114 us  [exchange(): return lax.ppermute(value, axis, [(i, i ^ mask) for i in range(size)])]
    pallas_call x1, Pallas kernels: 55.2 us -> 17.3 us  [apply(): pl.pallas_call(functools.partial(apply_kernel, count=count), grid_spec=pl...]
    pallas_call x3, Pallas kernels: 25.2 us -> 12.6 us  [unpack(): pl.pallas_call(functools.partial(unpack_kernel, count=count, share=share,...]
    unnamed x11 -> x0, other arithmetic: 9.27 us -> none
    pallas_call x3, Pallas kernels: 34.5 us -> 26.4 us  [model(): pl.pallas_call(functools.partial(model_kernel, owners=owners), grid=(each...]
    unnamed x28 -> x18, local copies, waits for them, and re-layouts: 12.8 us -> 12 us
  transfers between devices with their start and end apart: 46 -> 46, of which waited for: 9 -> 12; matrix products, arithmetic and copies ran while one was open for 6% -> 4% of each run, Pallas kernels for 45% -> 37%
where the time goes in v2:
time: 424 us; the launch traced here: 423 us
  Pallas kernels  206 us (49%)
  waiting for transfers between devices  114 us (27%)
  starting transfers between devices  86.4 us (20%)
  local copies, waits for them, and re-layouts  14.2 us (3%)
    pallas_call x6, Pallas kernels, covariance(): pl.pallas_call(functools.partial(covariance_kernel, owners=owners, count=...  122 us
    ppermute x46, waiting for transfers between devices, exchange(): return lax.ppermute(value, axis, [(i, i ^ mask) for i in range(size)])  114 us
    ppermute x46, starting transfers between devices, exchange(): return lax.ppermute(value, axis, [(i, i ^ mask) for i in range(size)])  86.4 us
    pallas_call x3, Pallas kernels, model(): pl.pallas_call(functools.partial(model_kernel, owners=owners), grid=(each...  26.4 us
    pallas_call x1, Pallas kernels, apply(): pl.pallas_call(functools.partial(apply_kernel, count=count), grid_spec=pl...  17.3 us
    pallas_call x1, Pallas kernels, prepare(): pl.pallas_call(functools.partial(prepare_kernel, owners=owners, each=each...  14.8 us
    pallas_call x3, Pallas kernels, unpack(): pl.pallas_call(functools.partial(unpack_kernel, count=count, share=share,...  12.6 us
    pallas_call x1, Pallas kernels, sweep(): pl.pallas_call(functools.partial(sweep_kernel, count=count, share=share,...  12.5 us
  transfers between devices with their start and end apart: 46, of which 12 were waited for; matrix products, arithmetic and copies ran while one was open for 4% of the time, Pallas kernels for 37%

profile of v2, /device:TPU:0, one launch (start us, length us, event | category | flops | bytes accessed | tf_op | source)
XLA Modules:
  0.0 422.9 jit_solution(16254478916668348180)
XLA Ops:
  0.6 14.8 %prepare.1 = (bf16[2,256,256]{2,1,0:T(8,128)(2,1)S(1)}, bf16[2,256,256]{2,1,0:T(8,128)(2,1)}, bf16[2,256,256]{2,1,0:T(8,128)(2,1)}, bf16[2,256,256]{2,1,0:T(8,12...) custom-call(s32[1]{0:T(128)} %bitcast.place.refs_4_, ...), custom_call_target="tpu_custom_call" | custom-call | flops 62914560 | bytes 25165824 | tf_op jit(solution)/shard_map/prepare/pallas_call | solution.py:76
  15.4 0.5 collective-permute-start
  15.9 2.5 collective-permute-start.1
  18.6 1.9 collective-permute-start.14
  20.5 3.9 copy.15
  24.4 3.9 copy.16
  28.4 4.0 copy.17
  32.7 1.9 collective-permute-start.27
  35.4 8.9 %source_model.3 = (bf16[2,256,256]{2,1,0:T(8,128)(2,1)S(1)}, bf16[2,256,256]{2,1,0:T(8,128)(2,1)S(1)}, bf16[2,256,256]{2,1,0:T(8,128)(2,1)S(1)}, bf16[2,256,256]{2,1,0:T(8,128)(2,1)S(1)}) custom-call(s32[1]{0:T(128)} %bitcast.place.refs_4_, bf16[2,256,256]{2,1,0:T(8,128)(2,1)S(1)} %get-tuple-element.40.refs_0_, ...), custom_call_target="tpu_custom_call" | custom-call | flops 3221225472 | bytes 6291456 | tf_op jit(solution)/shard_map/source_model/pallas_call | solution.py:153
  44.7 1.9 collective-permute-start.4
  46.6 8.7 %source_model.4 = (bf16[2,256,256]{2,1,0:T(8,128)(2,1)S(1)}, bf16[2,256,256]{2,1,0:T(8,128)(2,1)S(1)}, bf16[2,256,256]{2,1,0:T(8,128)(2,1)S(1)}, bf16[2,256,256]{2,1,0:T(8,128)(2,1)S(1)}) custom-call(s32[1]{0:T(128)} %bitcast.place.refs_4_, bf16[2,256,256]{2,1,0:T(8,128)(2,1)S(1)} %get-tuple-element.51.refs_0_, ...), custom_call_target="tpu_custom_call" | custom-call | flops 3221225472 | bytes 6291456 | tf_op jit(solution)/shard_map/source_model/pallas_call | solution.py:153
  55.7 1.9 collective-permute-start.17
  57.6 8.7 %source_model.5 = (bf16[2,256,256]{2,1,0:T(8,128)(2,1)S(1)}, bf16[2,256,256]{2,1,0:T(8,128)(2,1)S(1)}, bf16[2,256,256]{2,1,0:T(8,128)(2,1)S(1)}, bf16[2,256,256]{2,1,0:T(8,128)(2,1)S(1)}) custom-call(s32[1]{0:T(128)} %bitcast.place.refs_4_, bf16[2,256,256]{2,1,0:T(8,128)(2,1)S(1)} %get-tuple-element.63.refs_0_, ...), custom_call_target="tpu_custom_call" | custom-call | flops 3221225472 | bytes 6291456 | tf_op jit(solution)/shard_map/source_model/pallas_call | solution.py:153
  66.7 20.5 %covariance.6 = (f32[4,16,24,384]{3,2,1,0:T(8,128)S(1)}, bf16[24,256,256]{2,1,0:T(8,128)(2,1)}) custom-call(s32[4]{0:T(128)S(1)} %get-tuple-element.100.table, s32[1]{0:T(128)} %bitcast.place.refs_4_, bf16[256,48,512]{2,1,0:T(8,128)(2,1)} %get-tuple-element.39.l_ref, bf16[2,256,256]{2,1,0:T(8,128)(2,1)S(1)} %get-tuple-element.44.refs_0_, ...), custom_call_target="tpu_custom_call" | custom-call | flops 2415919104 | bytes 8650752 | tf_op jit(solution)/shard_map/covariance/pallas_call | solution.py:218
  87.3 2.0 collective-permute-start.11
  89.3 20.3 %covariance.7 = (f32[4,16,24,384]{3,2,1,0:T(8,128)S(1)}, bf16[24,256,256]{2,1,0:T(8,128)(2,1)}) custom-call(s32[4]{0:T(128)S(1)} %get-tuple-element.101.table, s32[1]{0:T(128)} %bitcast.place.refs_4_, bf16[256,48,512]{2,1,0:T(8,128)(2,1)} %get-tuple-element.39.l_ref, ...), custom_call_target="tpu_custom_call", output_to_operand_aliasing={{1}: (7, {})} | custom-call | flops 2415919104 | bytes 8650752 | tf_op jit(solution)/shard_map/covariance/pallas_call | solution.py:218
  109.6 1.5 collective-permute-start.30
  111.1 0.6 collective-permute-start.9
  111.7 20.3 %covariance.8 = (f32[4,16,24,384]{3,2,1,0:T(8,128)S(1)}, bf16[24,256,256]{2,1,0:T(8,128)(2,1)}) custom-call(s32[4]{0:T(128)S(1)} %get-tuple-element.100.table, s32[1]{0:T(128)} %bitcast.place.refs_4_, bf16[256,48,512]{2,1,0:T(8,128)(2,1)} %get-tuple-element.39.l_ref, ...), custom_call_target="tpu_custom_call", output_to_operand_aliasing={{1}: (7, {})} | custom-call | flops 2415919104 | bytes 8650752 | tf_op jit(solution)/shard_map/covariance/pallas_call | solution.py:218
  132.0 1.5 collective-permute-start.7
  133.5 1.2 slice_bitcast_fusion.4
  134.7 0.5 collective-permute-start.6
  135.2 1.5 collective-permute-start.24
  136.7 0.5 collective-permute-start.22
  137.2 20.3 %covariance.9 = (f32[4,16,24,384]{3,2,1,0:T(8,128)S(1)}, bf16[24,256,256]{2,1,0:T(8,128)(2,1)}) custom-call(s32[4]{0:T(128)S(1)} %get-tuple-element.101.table, s32[1]{0:T(128)} %bitcast.place.refs_4_, bf16[256,48,512]{2,1,0:T(8,128)(2,1)} %get-tuple-element.39.l_ref, ...), custom_call_target="tpu_custom_call", output_to_operand_aliasing={{1}: (7, {})} | custom-call | flops 2415919104 | bytes 8650752 | tf_op jit(solution)/shard_map/covariance/pallas_call | solution.py:218
  157.5 20.3 %covariance.10 = (f32[4,16,24,384]{3,2,1,0:T(8,128)S(1)}, bf16[24,256,256]{2,1,0:T(8,128)(2,1)}) custom-call(s32[4]{0:T(128)S(1)} %get-tuple-element.100.table, s32[1]{0:T(128)} %bitcast.place.refs_4_, bf16[256,48,512]{2,1,0:T(8,128)(2,1)} %get-tuple-element.39.l_ref, ...), custom_call_target="tpu_custom_call", output_to_operand_aliasing={{1}: (7, {})} | custom-call | flops 2415919104 | bytes 8650752 | tf_op jit(solution)/shard_map/covariance/pallas_call | solution.py:218
  177.8 1.5 collective-permute-start.20
  179.3 0.5 collective-permute-start.19
  180.0 1.6 collective-permute-start.37
  181.6 0.5 collective-permute-start.35
  182.1 3.9 collective-permute-done.22
  186.1 1.5 collective-permute-start.33
  187.8 10.9 %collective-permute-done.20 = f32[16,24,384]{2,1,0:T(8,128)S(1)} collective-permute-done((f32[16,24,384]{2,1,0:T(8,128)S(1)}, f32[16,24,384]{2,1,0:T(8,128)S(1)}, u32[]{:S(2)}, u32[]{:S(2)}) %collective-permute-start.20) | collective-permute-done | bytes 589856 | tf_op jit(solution)/shard_map/ppermute | solution.py:33
  198.7 1.5 collective-permute-start.32
  200.2 11.2 %collective-permute-done.19 = f32[16,24,384]{2,1,0:T(8,128)S(1)} collective-permute-done((f32[16,24,384]{2,1,0:T(8,128)S(1)}, f32[16,24,384]{2,1,0:T(8,128)S(1)}, u32[]{:S(2)}, u32[]{:S(2)}) %collective-permute-start.19) | collective-permute-done | bytes 589856 | tf_op jit(solution)/shard_map/ppermute | solution.py:33
  211.4 3.6 collective-permute-start.12
  215.3 8.7 %collective-permute-done.37 = f32[16,24,384]{2,1,0:T(8,128)S(1)} collective-permute-done((f32[16,24,384]{2,1,0:T(8,128)S(1)}, f32[16,24,384]{2,1,0:T(8,128)S(1)}, u32[]{:S(2)}, u32[]{:S(2)}) %collective-permute-start.37) | collective-permute-done | bytes 589856 | tf_op jit(solution)/shard_map/ppermute | solution.py:33
  224.0 2.6 collective-permute-start.10
  226.6 10.1 %collective-permute-done.35 = f32[16,24,384]{2,1,0:T(8,128)S(1)} collective-permute-done((f32[16,24,384]{2,1,0:T(8,128)S(1)}, f32[16,24,384]{2,1,0:T(8,128)S(1)}, u32[]{:S(2)}, u32[]{:S(2)}) %collective-permute-start.35) | collective-permute-done | bytes 589856 | tf_op jit(solution)/shard_map/ppermute | solution.py:33
  236.6 1.5 collective-permute-start.8
  238.2 11.1 %collective-permute-done.33 = f32[16,24,384]{2,1,0:T(8,128)S(1)} collective-permute-done((f32[16,24,384]{2,1,0:T(8,128)S(1)}, f32[16,24,384]{2,1,0:T(8,128)S(1)}, u32[]{:S(2)}, u32[]{:S(2)}) %collective-permute-start.33) | collective-permute-done | bytes 589856 | tf_op jit(solution)/shard_map/ppermute | solution.py:33
  249.3 3.6 collective-permute-start.25
  252.8 20.5 %covariance.11 = (f32[4,16,24,384]{3,2,1,0:T(8,128)S(1)}, bf16[24,256,256]{2,1,0:T(8,128)(2,1)}) custom-call(s32[4]{0:T(128)S(1)} %get-tuple-element.101.table, s32[1]{0:T(128)} %bitcast.place.refs_4_, bf16[256,48,512]{2,1,0:T(8,128)(2,1)} %get-tuple-element.39.l_ref, ...), custom_call_target="tpu_custom_call", output_to_operand_aliasing={{1}: (7, {})} | custom-call | flops 2415919104 | bytes 8650752 | tf_op jit(solution)/shard_map/covariance/pallas_call | solution.py:218
  273.4 1.2 bitcast_add_fusion
  274.6 0.8 collective-permute-start.21
  275.4 15.2 %collective-permute-done.10.refs_2_ = f32[16,24,384]{2,1,0:T(8,128)S(1)} collective-permute-done((f32[16,24,384]{2,1,0:T(8,128)S(1)}, f32[16,24,384]{2,1,0:T(8,128)S(1)}, u32[]{:S(2)}, u32[]{:S(2)}) %collective-permute-start.10) | collective-permute-done | bytes 589856 | tf_op jit(solution)/shard_map/ppermute | solution.py:33
  290.7 3.5 collective-permute-start.38
  294.2 35.1 %collective-permute-start.34 = (f32[16,24,384]{2,1,0:T(8,128)S(1)}, f32[16,24,384]{2,1,0:T(8,128)S(1)}, u32[]{:S(2)}, u32[]{:S(2)}) collective-permute-start(f32[16,24,384]{2,1,0:T(8,128)S(1)} %get-tuple-element.78), channel_id=1, source_target_pairs={{0,2},{1,3},{2,0},{3,1},{4,6},{5,7},{6,4},{7,5},{8,10},{9,11},{10,... | collective-permute-start | bytes 1769480 | tf_op jit(solution)/shard_map/ppermute | solution.py:33
  329.4 4.2 unpack.3.refs_0_
  333.6 7.7 %collective-permute-done.23.refs_2_ = f32[16,24,384]{2,1,0:T(8,128)S(1)} collective-permute-done((f32[16,24,384]{2,1,0:T(8,128)S(1)}, f32[16,24,384]{2,1,0:T(8,128)S(1)}, u32[]{:S(2)}, u32[]{:S(2)}) %collective-permute-start.23) | collective-permute-done | bytes 589856 | tf_op jit(solution)/shard_map/ppermute | solution.py:33
  341.3 4.2 unpack.4.refs_1_
  345.5 20.0 %collective-permute-done.36.refs_2_ = f32[16,24,384]{2,1,0:T(8,128)S(1)} collective-permute-done((f32[16,24,384]{2,1,0:T(8,128)}, f32[16,24,384]{2,1,0:T(8,128)S(1)}, u32[]{:S(2)}, u32[]{:S(2)}) %collective-permute-start.36) | collective-permute-done | bytes 589856 | tf_op jit(solution)/shard_map/ppermute | solution.py:33
  365.6 4.2 unpack.5.refs_2_
  369.8 12.5 %sweep.1 = f32[32,1152]{1,0:T(8,128)S(1)} custom-call(f32[24,6,2,8,128]{4,3,2,1,0:T(8,128)S(1)} %unpack.3.refs_0_, f32[24,6,2,8,128]{4,3,2,1,0:T(8,128)S(1)} %unpack.4.refs_1_, f32[24,6,2,8,128]{4,3,2,1,0:T(8,128)S(1)} %unpack.5.refs_2_), custom_call_target="tpu_custom_call" | custom-call | flops 62208000 | bytes 3538944 | tf_op jit(solution)/shard_map/sweep/pallas_call | solution.py:415
  382.2 1.6 collective-permute-start.42
  383.8 2.5 collective-permute-start.41
  386.3 1.9 collective-permute-start.39
  388.2 4.2 collective-permute-done.41
  392.4 0.5 collective-permute-start.45
  392.9 4.7 %collective-permute-done.40 = f32[32,1152]{1,0:T(8,128)S(1)} collective-permute-done((f32[32,1152]{1,0:T(8,128)S(1)}, f32[32,1152]{1,0:T(8,128)S(1)}, u32[]{:S(2)}, u32[]{:S(2)}) %collective-permute-start.40) | collective-permute-done | bytes 147488 | tf_op jit(solution)/shard_map/ppermute | solution.py:33
  397.6 0.5 collective-permute-start.44
  398.1 1.5 collective-permute-start.43
  399.8 5.8 %collective-permute-done.43 = f32[32,1152]{1,0:T(8,128)S(1)} collective-permute-done((f32[32,1152]{1,0:T(8,128)S(1)}, f32[32,1152]{1,0:T(8,128)S(1)}, u32[]{:S(2)}, u32[]{:S(2)}) %collective-permute-start.43) | collective-permute-done | bytes 147488 | tf_op jit(solution)/shard_map/ppermute | solution.py:33
  405.7 17.3 %apply.1 = f32[2,24,256,256]{3,2,1,0:T(8,128)} custom-call(s32[8]{0:T(128)S(1)} %pad_add_fusion.table, f32[8,32,1152]{2,1,0:T(8,128)S(1)} %bitcast_dynamic-update-slice_fusion.w_ref, bf16[256,48,512]{2,1,0:T(8,128)(2,1)} %get-tuple-element.39.l_ref), custom_call_target="tpu_custom_call" | custom-call | flops 603979776 | bytes 25165824 | tf_op jit(solution)/shard_map/apply/pallas_call | solution.py:465
  (74 shorter events, 3.4 us)
Async XLA Ops:
  15.4 17.0 %collective-permute-start = (bf16[2,256,256]{2,1,0:T(8,128)(2,1)}, bf16[2,256,256]{2,1,0:T(8,128)(2,1)S(1)}, u32[]{:S(2)}, u32[]{:S(2)}) collective-permute-start(bf16[2,256,256]{2,1,0:T(8,128)(2,1)} %get-tuple-element.41), channel_id=1, source_target_pairs={{0,8},{8,0},{16,24},{24,16},{1,9},{9,1},{17,25},{25,17},{2,10},{10... | collective-permute-start | bytes 786440 | tf_op jit(solution)/shard_map/ppermute | solution.py:33
  15.9 16.6 %collective-permute-start.1 = (bf16[2,256,256]{2,1,0:T(8,128)(2,1)}, bf16[2,256,256]{2,1,0:T(8,128)(2,1)}, u32[]{:S(2)}, u32[]{:S(2)}) collective-permute-start(bf16[2,256,256]{2,1,0:T(8,128)(2,1)} %get-tuple-element.42), channel_id=1, source_target_pairs={{0,16},{8,24},{16,0},{24,8},{1,17},{9,25},{17,1},{25,9},{2,18},{10... | collective-permute-start | bytes 786440 | tf_op jit(solution)/shard_map/ppermute | solution.py:33
  18.4 14.3 %collective-permute-start.2 = (bf16[2,256,256]{2,1,0:T(8,128)(2,1)S(1)}, bf16[2,256,256]{2,1,0:T(8,128)(2,1)}, u32[]{:S(2)}, u32[]{:S(2)}) collective-permute-start(bf16[2,256,256]{2,1,0:T(8,128)(2,1)S(1)} %get-tuple-element.43), channel_id=1, source_target_pairs={{0,24},{8,16},{16,8},{24,0},{1,25},{9,17},{17,9},{25,1},{2,26},{10... | collective-permute-start | bytes 786440 | tf_op jit(solution)/shard_map/ppermute | solution.py:33
  18.5 25.9 %collective-permute-start.13 = (bf16[2,256,256]{2,1,0:T(8,128)(2,1)S(1)}, bf16[2,256,256]{2,1,0:T(8,128)(2,1)S(1)}, u32[]{:S(2)}, u32[]{:S(2)}) collective-permute-start(bf16[2,256,256]{2,1,0:T(8,128)(2,1)S(1)} %get-tuple-element.52), channel_id=1, source_target_pairs={{0,8},{8,0},{16,24},{24,16},{1,9},{9,1},{17,25},{25,17},{2,10},{10... | collective-permute-start | bytes 786440 | tf_op jit(solution)/shard_map/ppermute | solution.py:33
  18.6 25.9 %collective-permute-start.14 = (bf16[2,256,256]{2,1,0:T(8,128)(2,1)S(1)}, bf16[2,256,256]{2,1,0:T(8,128)(2,1)S(1)}, u32[]{:S(2)}, u32[]{:S(2)}) collective-permute-start(bf16[2,256,256]{2,1,0:T(8,128)(2,1)S(1)} %get-tuple-element.53), channel_id=1, source_target_pairs={{0,16},{8,24},{16,0},{24,8},{1,17},{9,25},{17,1},{25,9},{2,18},{10... | collective-permute-start | bytes 786440 | tf_op jit(solution)/shard_map/ppermute | solution.py:33
  28.4 6.2 %copy-start = (f32[1024]{0:T(1024)S(1)}, f32[1024]{0:T(1024)}, u32[]{:S(2)}) copy-start(f32[1024]{0:T(1024)} %param.9) | copy-start | bytes 12292
  28.4 6.4 %copy-start.1 = (f32[1024]{0:T(1024)S(1)}, f32[1024]{0:T(1024)}, u32[]{:S(2)}) copy-start(f32[1024]{0:T(1024)} %param.11) | copy-start | bytes 12292
  28.4 6.7 %copy-start.2 = (f32[1024]{0:T(1024)S(1)}, f32[1024]{0:T(1024)}, u32[]{:S(2)}) copy-start(f32[1024]{0:T(1024)} %param.13) | copy-start | bytes 12292
  28.4 6.9 %copy-start.3 = (f32[1024]{0:T(1024)S(1)}, f32[1024]{0:T(1024)}, u32[]{:S(2)}) copy-start(f32[1024]{0:T(1024)} %param.15) | copy-start | bytes 12292
  32.4 12.3 %collective-permute-start.15 = (bf16[2,256,256]{2,1,0:T(8,128)(2,1)S(1)}, bf16[2,256,256]{2,1,0:T(8,128)(2,1)S(1)}, u32[]{:S(2)}, u32[]{:S(2)}) collective-permute-start(bf16[2,256,256]{2,1,0:T(8,128)(2,1)S(1)} %get-tuple-element.54), channel_id=1, source_target_pairs={{0,24},{8,16},{16,8},{24,0},{1,25},{9,17},{17,9},{25,1},{2,26},{10... | collective-permute-start | bytes 786440 | tf_op jit(solution)/shard_map/ppermute | solution.py:33
  32.5 22.9 %collective-permute-start.26 = (bf16[2,256,256]{2,1,0:T(8,128)(2,1)S(1)}, bf16[2,256,256]{2,1,0:T(8,128)(2,1)S(1)}, u32[]{:S(2)}, u32[]{:S(2)}) collective-permute-start(bf16[2,256,256]{2,1,0:T(8,128)(2,1)S(1)} %get-tuple-element.64), channel_id=1, source_target_pairs={{0,8},{8,0},{16,24},{24,16},{1,9},{9,1},{17,25},{25,17},{2,10},{10... | collective-permute-start | bytes 786440 | tf_op jit(solution)/shard_map/ppermute | solution.py:33
  32.7 22.7 %collective-permute-start.27 = (bf16[2,256,256]{2,1,0:T(8,128)(2,1)S(1)}, bf16[2,256,256]{2,1,0:T(8,128)(2,1)S(1)}, u32[]{:S(2)}, u32[]{:S(2)}) collective-permute-start(bf16[2,256,256]{2,1,0:T(8,128)(2,1)S(1)} %get-tuple-element.65), channel_id=1, source_target_pairs={{0,16},{8,24},{16,0},{24,8},{1,17},{9,25},{17,1},{25,9},{2,18},{10... | collective-permute-start | bytes 786440 | tf_op jit(solution)/shard_map/ppermute | solution.py:33
  44.4 11.3 %collective-permute-start.28 = (bf16[2,256,256]{2,1,0:T(8,128)(2,1)S(1)}, bf16[2,256,256]{2,1,0:T(8,128)(2,1)S(1)}, u32[]{:S(2)}, u32[]{:S(2)}) collective-permute-start(bf16[2,256,256]{2,1,0:T(8,128)(2,1)S(1)} %get-tuple-element.66), channel_id=1, source_target_pairs={{0,24},{8,16},{16,8},{24,0},{1,25},{9,17},{17,9},{25,1},{2,26},{10... | collective-permute-start | bytes 786440 | tf_op jit(solution)/shard_map/ppermute | solution.py:33
  44.5 21.8 %collective-permute-start.3 = (bf16[2,256,256]{2,1,0:T(8,128)(2,1)S(1)}, bf16[2,256,256]{2,1,0:T(8,128)(2,1)S(1)}, u32[]{:S(2)}, u32[]{:S(2)}) collective-permute-start(bf16[2,256,256]{2,1,0:T(8,128)(2,1)S(1)} %get-tuple-element.45), channel_id=1, source_target_pairs={{0,8},{8,0},{16,24},{24,16},{1,9},{9,1},{17,25},{25,17},{2,10},{10... | collective-permute-start | bytes 786440 | tf_op jit(solution)/shard_map/ppermute | solution.py:33
  44.7 21.7 %collective-permute-start.4 = (bf16[2,256,256]{2,1,0:T(8,128)(2,1)S(1)}, bf16[2,256,256]{2,1,0:T(8,128)(2,1)S(1)}, u32[]{:S(2)}, u32[]{:S(2)}) collective-permute-start(bf16[2,256,256]{2,1,0:T(8,128)(2,1)S(1)} %get-tuple-element.46), channel_id=1, source_target_pairs={{0,16},{8,24},{16,0},{24,8},{1,17},{9,25},{17,1},{25,9},{2,18},{10... | collective-permute-start | bytes 786440 | tf_op jit(solution)/shard_map/ppermute | solution.py:33
  55.4 11.3 %collective-permute-start.5 = (bf16[2,256,256]{2,1,0:T(8,128)(2,1)S(1)}, bf16[2,256,256]{2,1,0:T(8,128)(2,1)S(1)}, u32[]{:S(2)}, u32[]{:S(2)}) collective-permute-start(bf16[2,256,256]{2,1,0:T(8,128)(2,1)S(1)} %get-tuple-element.47), channel_id=1, source_target_pairs={{0,24},{8,16},{16,8},{24,0},{1,25},{9,17},{17,9},{25,1},{2,26},{10... | collective-permute-start | bytes 786440 | tf_op jit(solution)/shard_map/ppermute | solution.py:33
  55.5 54.1 %collective-permute-start.16 = (bf16[2,256,256]{2,1,0:T(8,128)(2,1)S(1)}, bf16[2,256,256]{2,1,0:T(8,128)(2,1)S(1)}, u32[]{:S(2)}, u32[]{:S(2)}) collective-permute-start(bf16[2,256,256]{2,1,0:T(8,128)(2,1)S(1)} %get-tuple-element.56), channel_id=1, source_target_pairs={{0,8},{8,0},{16,24},{24,16},{1,9},{9,1},{17,25},{25,17},{2,10},{10... | collective-permute-start | bytes 786440 | tf_op jit(solution)/shard_map/ppermute | solution.py:33
  55.7 55.4 %collective-permute-start.17 = (bf16[2,256,256]{2,1,0:T(8,128)(2,1)S(1)}, bf16[2,256,256]{2,1,0:T(8,128)(2,1)S(1)}, u32[]{:S(2)}, u32[]{:S(2)}) collective-permute-start(bf16[2,256,256]{2,1,0:T(8,128)(2,1)S(1)} %get-tuple-element.57), channel_id=1, source_target_pairs={{0,16},{8,24},{16,0},{24,8},{1,17},{9,25},{17,1},{25,9},{2,18},{10... | collective-permute-start | bytes 786440 | tf_op jit(solution)/shard_map/ppermute | solution.py:33
  66.3 44.8 %collective-permute-start.18 = (bf16[2,256,256]{2,1,0:T(8,128)(2,1)S(1)}, bf16[2,256,256]{2,1,0:T(8,128)(2,1)S(1)}, u32[]{:S(2)}, u32[]{:S(2)}) collective-permute-start(bf16[2,256,256]{2,1,0:T(8,128)(2,1)S(1)} %get-tuple-element.58), channel_id=1, source_target_pairs={{0,24},{8,16},{16,8},{24,0},{1,25},{9,17},{17,9},{25,1},{2,26},{10... | collective-permute-start | bytes 786440 | tf_op jit(solution)/shard_map/ppermute | solution.py:33
  66.4 65.5 %collective-permute-start.29 = (bf16[2,256,256]{2,1,0:T(8,128)(2,1)S(1)}, bf16[2,256,256]{2,1,0:T(8,128)(2,1)S(1)}, u32[]{:S(2)}, u32[]{:S(2)}) collective-permute-start(bf16[2,256,256]{2,1,0:T(8,128)(2,1)S(1)} %get-tuple-element.68), channel_id=1, source_target_pairs={{0,8},{8,0},{16,24},{24,16},{1,9},{9,1},{17,25},{25,17},{2,10},{10... | collective-permute-start | bytes 786440 | tf_op jit(solution)/shard_map/ppermute | solution.py:33
  87.3 49.4 %collective-permute-start.11 = (f32[16,24,384]{2,1,0:T(8,128)S(1)}, f32[16,24,384]{2,1,0:T(8,128)S(1)}, u32[]{:S(2)}, u32[]{:S(2)}) collective-permute-start(f32[16,24,384]{2,1,0:T(8,128)S(1)} %get-tuple-element.96), channel_id=1, source_target_pairs={{0,1},{1,0},{2,3},{3,2},{4,5},{5,4},{6,7},{7,6},{8,9},{9,8},{10,11... | collective-permute-start | bytes 1769480 | tf_op jit(solution)/shard_map/ppermute | solution.py:33
  109.6 25.1 %collective-permute-start.30 = (bf16[2,256,256]{2,1,0:T(8,128)(2,1)S(1)}, bf16[2,256,256]{2,1,0:T(8,128)(2,1)S(1)}, u32[]{:S(2)}, u32[]{:S(2)}) collective-permute-start(bf16[2,256,256]{2,1,0:T(8,128)(2,1)S(1)} %get-tuple-element.69), channel_id=1, source_target_pairs={{0,16},{8,24},{16,0},{24,8},{1,17},{9,25},{17,1},{25,9},{2,18},{10... | collective-permute-start | bytes 786440 | tf_op jit(solution)/shard_map/ppermute | solution.py:33
  111.1 24.1 %collective-permute-start.31 = (bf16[2,256,256]{2,1,0:T(8,128)(2,1)S(1)}, bf16[2,256,256]{2,1,0:T(8,128)(2,1)S(1)}, u32[]{:S(2)}, u32[]{:S(2)}) collective-permute-start(bf16[2,256,256]{2,1,0:T(8,128)(2,1)S(1)} %get-tuple-element.70), channel_id=1, source_target_pairs={{0,24},{8,16},{16,8},{24,0},{1,25},{9,17},{17,9},{25,1},{2,26},{10... | collective-permute-start | bytes 786440 | tf_op jit(solution)/shard_map/ppermute | solution.py:33
  111.1 66.7 %collective-permute-start.9 = (f32[16,24,384]{2,1,0:T(8,128)S(1)}, f32[16,24,384]{2,1,0:T(8,128)S(1)}, u32[]{:S(2)}, u32[]{:S(2)}) collective-permute-start(f32[16,24,384]{2,1,0:T(8,128)S(1)} %get-tuple-element.97), channel_id=1, source_target_pairs={{0,1},{1,0},{2,3},{3,2},{4,5},{5,4},{6,7},{7,6},{8,9},{9,8},{10,11... | collective-permute-start | bytes 1769480 | tf_op jit(solution)/shard_map/ppermute | solution.py:33
  132.0 47.4 %collective-permute-start.7 = (f32[16,24,384]{2,1,0:T(8,128)S(1)}, f32[16,24,384]{2,1,0:T(8,128)S(1)}, u32[]{:S(2)}, u32[]{:S(2)}) collective-permute-start(f32[16,24,384]{2,1,0:T(8,128)S(1)} %get-tuple-element.98), channel_id=1, source_target_pairs={{0,1},{1,0},{2,3},{3,2},{4,5},{5,4},{6,7},{7,6},{8,9},{9,8},{10,11... | collective-permute-start | bytes 1769480 | tf_op jit(solution)/shard_map/ppermute | solution.py:33
  134.7 45.4 %collective-permute-start.6 = (f32[16,24,384]{2,1,0:T(8,128)S(1)}, f32[16,24,384]{2,1,0:T(8,128)S(1)}, u32[]{:S(2)}, u32[]{:S(2)}) collective-permute-start(f32[16,24,384]{2,1,0:T(8,128)S(1)} %get-tuple-element.99), channel_id=1, source_target_pairs={{0,1},{1,0},{2,3},{3,2},{4,5},{5,4},{6,7},{7,6},{8,9},{9,8},{10,11... | collective-permute-start | bytes 1769480 | tf_op jit(solution)/shard_map/ppermute | solution.py:33
  135.2 46.4 %collective-permute-start.24 = (f32[16,24,384]{2,1,0:T(8,128)}, f32[16,24,384]{2,1,0:T(8,128)S(1)}, u32[]{:S(2)}, u32[]{:S(2)}) collective-permute-start(f32[16,24,384]{2,1,0:T(8,128)} %get-tuple-element.88), channel_id=1, source_target_pairs={{0,1},{1,0},{2,3},{3,2},{4,5},{5,4},{6,7},{7,6},{8,9},{9,8},{10,11... | collective-permute-start | bytes 1769480 | tf_op jit(solution)/shard_map/ppermute | solution.py:33
  136.7 49.4 %collective-permute-start.22 = (f32[16,24,384]{2,1,0:T(8,128)}, f32[16,24,384]{2,1,0:T(8,128)S(1)}, u32[]{:S(2)}, u32[]{:S(2)}) collective-permute-start(f32[16,24,384]{2,1,0:T(8,128)} %get-tuple-element.89), channel_id=1, source_target_pairs={{0,1},{1,0},{2,3},{3,2},{4,5},{5,4},{6,7},{7,6},{8,9},{9,8},{10,11... | collective-permute-start | bytes 1769480 | tf_op jit(solution)/shard_map/ppermute | solution.py:33
  177.8 20.9 %collective-permute-start.20 = (f32[16,24,384]{2,1,0:T(8,128)S(1)}, f32[16,24,384]{2,1,0:T(8,128)S(1)}, u32[]{:S(2)}, u32[]{:S(2)}) collective-permute-start(f32[16,24,384]{2,1,0:T(8,128)S(1)} %get-tuple-element.90), channel_id=1, source_target_pairs={{0,1},{1,0},{2,3},{3,2},{4,5},{5,4},{6,7},{7,6},{8,9},{9,8},{10,11... | collective-permute-start | bytes 1769480 | tf_op jit(solution)/shard_map/ppermute | solution.py:33
  179.3 32.0 %collective-permute-start.19 = (f32[16,24,384]{2,1,0:T(8,128)S(1)}, f32[16,24,384]{2,1,0:T(8,128)S(1)}, u32[]{:S(2)}, u32[]{:S(2)}) collective-permute-start(f32[16,24,384]{2,1,0:T(8,128)S(1)} %get-tuple-element.91), channel_id=1, source_target_pairs={{0,1},{1,0},{2,3},{3,2},{4,5},{5,4},{6,7},{7,6},{8,9},{9,8},{10,11... | collective-permute-start | bytes 1769480 | tf_op jit(solution)/shard_map/ppermute | solution.py:33
  180.0 44.0 %collective-permute-start.37 = (f32[16,24,384]{2,1,0:T(8,128)S(1)}, f32[16,24,384]{2,1,0:T(8,128)S(1)}, u32[]{:S(2)}, u32[]{:S(2)}) collective-permute-start(f32[16,24,384]{2,1,0:T(8,128)S(1)} %get-tuple-element.80), channel_id=1, source_target_pairs={{0,1},{1,0},{2,3},{3,2},{4,5},{5,4},{6,7},{7,6},{8,9},{9,8},{10,11... | collective-permute-start | bytes 1769480 | tf_op jit(solution)/shard_map/ppermute | solution.py:33
  181.6 55.0 %collective-permute-start.35 = (f32[16,24,384]{2,1,0:T(8,128)S(1)}, f32[16,24,384]{2,1,0:T(8,128)S(1)}, u32[]{:S(2)}, u32[]{:S(2)}) collective-permute-start(f32[16,24,384]{2,1,0:T(8,128)S(1)} %get-tuple-element.81), channel_id=1, source_target_pairs={{0,1},{1,0},{2,3},{3,2},{4,5},{5,4},{6,7},{7,6},{8,9},{9,8},{10,11... | collective-permute-start | bytes 1769480 | tf_op jit(solution)/shard_map/ppermute | solution.py:33
  186.1 63.2 %collective-permute-start.33 = (f32[16,24,384]{2,1,0:T(8,128)S(1)}, f32[16,24,384]{2,1,0:T(8,128)S(1)}, u32[]{:S(2)}, u32[]{:S(2)}) collective-permute-start(f32[16,24,384]{2,1,0:T(8,128)S(1)} %get-tuple-element.82), channel_id=1, source_target_pairs={{0,1},{1,0},{2,3},{3,2},{4,5},{5,4},{6,7},{7,6},{8,9},{9,8},{10,11... | collective-permute-start | bytes 1769480 | tf_op jit(solution)/shard_map/ppermute | solution.py:33
  198.7 74.7 %collective-permute-start.32 = (f32[16,24,384]{2,1,0:T(8,128)S(1)}, f32[16,24,384]{2,1,0:T(8,128)S(1)}, u32[]{:S(2)}, u32[]{:S(2)}) collective-permute-start(f32[16,24,384]{2,1,0:T(8,128)S(1)} %get-tuple-element.83), channel_id=1, source_target_pairs={{0,1},{1,0},{2,3},{3,2},{4,5},{5,4},{6,7},{7,6},{8,9},{9,8},{10,11... | collective-permute-start | bytes 1769480 | tf_op jit(solution)/shard_map/ppermute | solution.py:33
  211.4 63.3 %collective-permute-start.12 = (f32[16,24,384]{2,1,0:T(8,128)S(1)}, f32[16,24,384]{2,1,0:T(8,128)S(1)}, u32[]{:S(2)}, u32[]{:S(2)}) collective-permute-start(f32[16,24,384]{2,1,0:T(8,128)S(1)} %get-tuple-element.92), channel_id=1, source_target_pairs={{0,6},{1,7},{2,4},{3,5},{4,2},{5,3},{6,0},{7,1},{8,14},{9,15},{10,... | collective-permute-start | bytes 1769480 | tf_op jit(solution)/shard_map/ppermute | solution.py:33
  224.0 66.7 %collective-permute-start.10 = (f32[16,24,384]{2,1,0:T(8,128)S(1)}, f32[16,24,384]{2,1,0:T(8,128)S(1)}, u32[]{:S(2)}, u32[]{:S(2)}) collective-permute-start(f32[16,24,384]{2,1,0:T(8,128)S(1)} %get-tuple-element.93), channel_id=1, source_target_pairs={{0,4},{1,5},{2,6},{3,7},{4,0},{5,1},{6,2},{7,3},{8,12},{9,13},{10,... | collective-permute-start | bytes 1769480 | tf_op jit(solution)/shard_map/ppermute | solution.py:33
  236.6 57.6 %collective-permute-start.8 = (f32[16,24,384]{2,1,0:T(8,128)S(1)}, f32[16,24,384]{2,1,0:T(8,128)S(1)}, u32[]{:S(2)}, u32[]{:S(2)}) collective-permute-start(f32[16,24,384]{2,1,0:T(8,128)S(1)} %get-tuple-element.94), channel_id=1, source_target_pairs={{0,2},{1,3},{2,0},{3,1},{4,6},{5,7},{6,4},{7,5},{8,10},{9,11},{10,... | collective-permute-start | bytes 1769480 | tf_op jit(solution)/shard_map/ppermute | solution.py:33
  249.3 44.9 %collective-permute-start.25 = (f32[16,24,384]{2,1,0:T(8,128)S(1)}, f32[16,24,384]{2,1,0:T(8,128)S(1)}, u32[]{:S(2)}, u32[]{:S(2)}) collective-permute-start(f32[16,24,384]{2,1,0:T(8,128)S(1)} %get-tuple-element.84), channel_id=1, source_target_pairs={{0,6},{1,7},{2,4},{3,5},{4,2},{5,3},{6,0},{7,1},{8,14},{9,15},{10,... | collective-permute-start | bytes 1769480 | tf_op jit(solution)/shard_map/ppermute | solution.py:33
  273.4 67.9 %collective-permute-start.23 = (f32[16,24,384]{2,1,0:T(8,128)S(1)}, f32[16,24,384]{2,1,0:T(8,128)S(1)}, u32[]{:S(2)}, u32[]{:S(2)}) collective-permute-start(f32[16,24,384]{2,1,0:T(8,128)S(1)} %get-tuple-element.85), channel_id=1, source_target_pairs={{0,4},{1,5},{2,6},{3,7},{4,0},{5,1},{6,2},{7,3},{8,12},{9,13},{10,... | collective-permute-start | bytes 1769480 | tf_op jit(solution)/shard_map/ppermute | solution.py:33
  274.6 66.7 %collective-permute-start.21 = (f32[16,24,384]{2,1,0:T(8,128)S(1)}, f32[16,24,384]{2,1,0:T(8,128)S(1)}, u32[]{:S(2)}, u32[]{:S(2)}) collective-permute-start(f32[16,24,384]{2,1,0:T(8,128)S(1)} %get-tuple-element.86), channel_id=1, source_target_pairs={{0,2},{1,3},{2,0},{3,1},{4,6},{5,7},{6,4},{7,5},{8,10},{9,11},{10,... | collective-permute-start | bytes 1769480 | tf_op jit(solution)/shard_map/ppermute | solution.py:33
  290.7 54.8 %collective-permute-start.38 = (f32[16,24,384]{2,1,0:T(8,128)}, f32[16,24,384]{2,1,0:T(8,128)S(1)}, u32[]{:S(2)}, u32[]{:S(2)}) collective-permute-start(f32[16,24,384]{2,1,0:T(8,128)} %get-tuple-element.76), channel_id=1, source_target_pairs={{0,6},{1,7},{2,4},{3,5},{4,2},{5,3},{6,0},{7,1},{8,14},{9,15},{10,... | collective-permute-start | bytes 1769480 | tf_op jit(solution)/shard_map/ppermute | solution.py:33
  294.2 71.3 %collective-permute-start.36 = (f32[16,24,384]{2,1,0:T(8,128)}, f32[16,24,384]{2,1,0:T(8,128)S(1)}, u32[]{:S(2)}, u32[]{:S(2)}) collective-permute-start(f32[16,24,384]{2,1,0:T(8,128)} %get-tuple-element.77), channel_id=1, source_target_pairs={{0,4},{1,5},{2,6},{3,7},{4,0},{5,1},{6,2},{7,3},{8,12},{9,13},{10,... | collective-permute-start | bytes 1769480 | tf_op jit(solution)/shard_map/ppermute | solution.py:33
  294.2 71.3 %collective-permute-start.34 = (f32[16,24,384]{2,1,0:T(8,128)S(1)}, f32[16,24,384]{2,1,0:T(8,128)S(1)}, u32[]{:S(2)}, u32[]{:S(2)}) collective-permute-start(f32[16,24,384]{2,1,0:T(8,128)S(1)} %get-tuple-element.78), channel_id=1, source_target_pairs={{0,2},{1,3},{2,0},{3,1},{4,6},{5,7},{6,4},{7,5},{8,10},{9,11},{10,... | collective-permute-start | bytes 1769480 | tf_op jit(solution)/shard_map/ppermute | solution.py:33
  382.2 17.5 %collective-permute-start.42 = (f32[32,1152]{1,0:T(8,128)S(1)}, f32[32,1152]{1,0:T(8,128)S(1)}, u32[]{:S(2)}, u32[]{:S(2)}) collective-permute-start(f32[32,1152]{1,0:T(8,128)S(1)} %sweep.1), channel_id=1, source_target_pairs={{0,1},{1,0},{2,3},{3,2},{4,5},{5,4},{6,7},{7,6},{8,9},{9,8},{10,11... | collective-permute-start | bytes 442376 | tf_op jit(solution)/shard_map/ppermute | solution.py:33
  383.8 8.6 %collective-permute-start.41 = (f32[32,1152]{1,0:T(8,128)S(1)}, f32[32,1152]{1,0:T(8,128)S(1)}, u32[]{:S(2)}, u32[]{:S(2)}) collective-permute-start(f32[32,1152]{1,0:T(8,128)S(1)} %sweep.1), channel_id=1, source_target_pairs={{0,6},{1,7},{2,4},{3,5},{4,2},{5,3},{6,0},{7,1},{8,14},{9,15},{10,... | collective-permute-start | bytes 442376 | tf_op jit(solution)/shard_map/ppermute | solution.py:33
  386.3 11.3 %collective-permute-start.40 = (f32[32,1152]{1,0:T(8,128)S(1)}, f32[32,1152]{1,0:T(8,128)S(1)}, u32[]{:S(2)}, u32[]{:S(2)}) collective-permute-start(f32[32,1152]{1,0:T(8,128)S(1)} %sweep.1), channel_id=1, source_target_pairs={{0,4},{1,5},{2,6},{3,7},{4,0},{5,1},{6,2},{7,3},{8,12},{9,13},{10,... | collective-permute-start | bytes 442376 | tf_op jit(solution)/shard_map/ppermute | solution.py:33
  386.3 11.9 %collective-permute-start.39 = (f32[32,1152]{1,0:T(8,128)S(1)}, f32[32,1152]{1,0:T(8,128)S(1)}, u32[]{:S(2)}, u32[]{:S(2)}) collective-permute-start(f32[32,1152]{1,0:T(8,128)S(1)} %sweep.1), channel_id=1, source_target_pairs={{0,2},{1,3},{2,0},{3,1},{4,6},{5,7},{6,4},{7,5},{8,10},{9,11},{10,... | collective-permute-start | bytes 442376 | tf_op jit(solution)/shard_map/ppermute | solution.py:33
  392.4 13.2 %collective-permute-start.45 = (f32[32,1152]{1,0:T(8,128)S(1)}, f32[32,1152]{1,0:T(8,128)S(1)}, u32[]{:S(2)}, u32[]{:S(2)}) collective-permute-start(f32[32,1152]{1,0:T(8,128)S(1)} %collective-permute-done.41), channel_id=1, source_target_pairs={{0,1},{1,0},{2,3},{3,2},{4,5},{5,4},{6,7},{7,6},{8,9},{9,8},{10,11... | collective-permute-start | bytes 442376 | tf_op jit(solution)/shard_map/ppermute | solution.py:33
  397.6 8.0 %collective-permute-start.44 = (f32[32,1152]{1,0:T(8,128)S(1)}, f32[32,1152]{1,0:T(8,128)S(1)}, u32[]{:S(2)}, u32[]{:S(2)}) collective-permute-start(f32[32,1152]{1,0:T(8,128)S(1)} %collective-permute-done.40), channel_id=1, source_target_pairs={{0,1},{1,0},{2,3},{3,2},{4,5},{5,4},{6,7},{7,6},{8,9},{9,8},{10,11... | collective-permute-start | bytes 442376 | tf_op jit(solution)/shard_map/ppermute | solution.py:33
  398.1 7.4 %collective-permute-start.43 = (f32[32,1152]{1,0:T(8,128)S(1)}, f32[32,1152]{1,0:T(8,128)S(1)}, u32[]{:S(2)}, u32[]{:S(2)}) collective-permute-start(f32[32,1152]{1,0:T(8,128)S(1)} %collective-permute-done.39), channel_id=1, source_target_pairs={{0,1},{1,0},{2,3},{3,2},{4,5},{5,4},{6,7},{7,6},{8,9},{9,8},{10,11... | collective-permute-start | bytes 442376 | tf_op jit(solution)/shard_map/ppermute | solution.py:33

commit v3 on v2

--- a/solution.py
+++ b/solution.py
@@ -10,6 +10,8 @@
 epsilon = 1e-05
 power_floor = 0.001
 variance_floor = 0.25
+ridge = 2.0**-14
+floor = 1e-8
 GROUP = 8
 LANES = 128
 BF16 = jnp.bfloat16
@@ -178,8 +180,8 @@
     row = lax.broadcasted_iota(jnp.int32, shape, 0)
     column = lax.rem(lax.broadcasted_iota(jnp.int32, shape, 1), count)
     real = row <= column
-    half = bins // 2
-    together = min(8, half)
+    quarter = bins // 4
+    together = min(4, quarter)
 
     def weighted(f):
         left = l_ref[f]
@@ -188,28 +190,27 @@
         for j in range(GROUP):
             w = weight[j, pl.ds(f, 1), :]
             parts.append(top * jnp.concatenate([w, w], axis=1))
-        right = jnp.concatenate(parts, axis=0)
-        high = right.astype(BF16)
-        return left, high, (right - high.astype(F32)).astype(BF16)
-
-    def summed(left, high, low):
+        return left, jnp.concatenate(parts, axis=0).astype(BF16)
+
+    def summed(left, right):
         dims = (((1,), (1,)), ((), ()))
-        v = lax.dot_general(left, high, dims, preferred_element_type=F32)
-        v = v + lax.dot_general(left, low, dims, preferred_element_type=F32)
+        v = lax.dot_general(left, right, dims, preferred_element_type=F32)
         return jnp.where(real, v[:count], v[count:])
 
     def some(n, carry):
         first = n * together
-        operands = [weighted(first + i + e * half) for i in range(together) for e in range(2)]
+        operands = [weighted(first + i + e * quarter) for i in range(together) for e in range(4)]
         sums = [summed(*o) for o in operands]
         for i in range(together):
-            o_ref[0, first + i] = jnp.concatenate([sums[2 * i], sums[2 * i + 1]], axis=1)
-        return carry
-
-    lax.fori_loop(0, half // together, some, 0)
-
-
-def covariance(table, place, stacked, pieces, natural, chunk, count):
+            v = sums[4 * i : 4 * i + 4]
+            rows = [jnp.concatenate([v[e], v[e + 2]], axis=1) for e in range(2)]
+            o_ref[0, first + i] = jnp.concatenate(rows, axis=0).astype(o_ref.dtype)
+        return carry
+
+    lax.fori_loop(0, quarter // together, some, 0)
+
+
+def covariance(table, place, stacked, pieces, natural, chunk, count, held):
     owners, shares = len(pieces), table.shape[0]
     each, bins, frames = pieces[0].shape
     share = stacked.shape[0] // lax.axis_size("frame")
@@ -229,7 +230,7 @@
             + [pl.BlockSpec(memory_space=pl.ANY)],
             out_specs=[
                 pl.BlockSpec(
-                    (1, share // 2, count, lanes), lambda r, table, place: (r, 0, 0, 0)
+                    (1, share // 4, 2 * count, lanes), lambda r, table, place: (r, 0, 0, 0)
                 ),
                 pl.BlockSpec(
                     (GROUP, share, frames), lambda r, table, place: (chunk, table[r], 0)
@@ -238,7 +239,7 @@
             scratch_shapes=[VMEM((GROUP, share, frames), F32)],
         ),
         out_shape=[
-            jax.ShapeDtypeStruct((shares, share // 2, count, lanes), F32),
+            jax.ShapeDtypeStruct((shares, share // 4, 2 * count, lanes), held),
             jax.ShapeDtypeStruct((count, bins, frames), BF16),
         ],
         input_output_aliases={} if natural.shape[0] != count else {3 + owners: 1},
@@ -252,15 +253,18 @@
 
 
 def unpack_kernel(*refs, count, share, lanes_b):
-    parts, o_ref, turned = refs[:-2], refs[-2], refs[-1]
+    parts, o_ref, added, turned = refs[:-3], refs[-3], refs[-2], refs[-1]
     half = GROUP * count
     blocks = o_ref.shape[1]
 
+    v = parts[0][...].astype(F32)
+    for part in parts[1:]:
+        v = v + part[...].astype(F32)
+    added[...] = v
+
     def turn(a, carry):
-        v = parts[0][:, a, :]
-        for part in parts[1:]:
-            v = v + part[:, a, :]
-        v = jnp.concatenate([v[:, :half], v[:, half:]], axis=0)
+        v, w = added[:, a, :], added[:, count + a, :]
+        v = jnp.concatenate([v[:, :half], w[:, :half], v[:, half:], w[:, half:]], axis=0)
         turned[a, :, 0:share] = v.T
         return carry
 
@@ -293,7 +297,7 @@
     return pl.pallas_call(
         functools.partial(unpack_kernel, count=count, share=share, lanes_b=lanes_b),
         out_shape=jax.ShapeDtypeStruct(shape, F32),
-        scratch_shapes=[VMEM((count, GROUP * count, LANES), F32)],
+        scratch_shapes=[VMEM(parts[0].shape, F32), VMEM((count, GROUP * count, LANES), F32)],
         compiler_params=options(),
         cost_estimate=cost(10 * parts[0].size, 4 * parts[0].size * (len(parts) + 2)),
         name="unpack",
@@ -302,7 +306,8 @@
 
 def sweep_kernel(*refs, count, share, frames):
     chunks = count // GROUP
-    v_refs, o_ref, wr, wi, diagonal, flat = refs[:chunks], *refs[chunks:]
+    v_refs = refs[:chunks]
+    factor, inverse_ref, o_ref, wr, wi, diagonal, flat = refs[chunks:]
     lanes_b = LANES // share
     blocks = v_refs[0].shape[1]
     full = (GROUP, LANES)
@@ -311,20 +316,18 @@
     group = [(lane >= i * share) & (lane < (i + 1) * share) for i in range(lanes_b)]
     zero = jnp.zeros(full, F32)
 
-    def start(a, carry):
-        for c in range(chunks):
-            wr[a, c] = jnp.where(sub + c * GROUP == a, 1.0, 0.0)
-            wi[a, c] = zero
-        return carry
-
-    lax.fori_loop(0, count, start, 0)
+    wr[...] = jnp.zeros_like(wr)
+    wi[...] = jnp.zeros_like(wi)
     for c in range(chunks):
         for g in range(blocks):
-            for part in range(2):
-                d = zero
-                for s in range(GROUP):
-                    d = jnp.where(sub == s, v_refs[c][c * GROUP + s, g, part], d)
-                diagonal[c, g, part] = d
+
+            def own(a, carry):
+                lr, li = factor[a, 0, c], factor[a, 1, c]
+                vr, vi = v_refs[c][a, g, 0], v_refs[c][a, g, 1]
+                return carry[0] + lr * vr - li * vi, carry[1] + lr * vi + li * vr
+
+            first = lax.fori_loop(0, (c + 1) * GROUP, own, (zero, zero), unroll=4)
+            diagonal[c, g, 0], diagonal[c, g, 1] = first
 
     def total(x):
         shift = share
@@ -336,6 +339,9 @@
     for k in range(count):
         ck, sk = divmod(k, GROUP)
         used = k // lanes_b + 1
+        for a in range(k + 1):
+            wr[a, ck] = wr[a, ck] + jnp.where(sub == sk, factor[a, 0, ck], 0.0)
+            wi[a, ck] = wi[a, ck] + jnp.where(sub == sk, factor[a, 1, ck], 0.0)
         pick_r, pick_i = [], []
         for g in range(used):
             pr, pi = zero, zero
@@ -396,19 +402,135 @@
 
         lax.fori_loop(0, k + 1, update, 0, unroll=min(2, k + 1))
 
-    def pack(a, carry):
+    for a in range(count):
+
+        def product(b, carry):
+            tr = inverse_ref[a, 0, pl.ds(b, 1), :]
+            ti = inverse_ref[a, 1, pl.ds(b, 1), :]
+            out = []
+            for c in range(chunks):
+                r, i = wr[b, c], wi[b, c]
+                out.append(carry[2 * c] + r * tr - i * ti)
+                out.append(carry[2 * c + 1] + r * ti + i * tr)
+            return tuple(out)
+
+        sums = lax.fori_loop(a, count, product, (zero,) * (2 * chunks), unroll=min(4, count - a))
         for c in range(chunks):
             at = c * GROUP * 2 * count + a
-            flat[pl.ds(at, GROUP, stride=2 * count), :] = wr[a, c]
-            flat[pl.ds(at + count, GROUP, stride=2 * count), :] = -wi[a, c]
-        return carry
-
-    lax.fori_loop(0, count, pack, 0)
+            flat[pl.ds(at, GROUP, stride=2 * count), :] = sums[2 * c]
+            flat[pl.ds(at + count, GROUP, stride=2 * count), :] = -sums[2 * c + 1]
+    flatten(flat, o_ref, share)
+
+
+def flatten(flat, o_ref, share):
     for i in range(flat.shape[0] // LANES):
         o_ref[:, i * LANES : (i + 1) * LANES] = flat[i * LANES : (i + 1) * LANES, :].T[:share]
 
 
-def sweep(parts, count, share, frames):
+def whiten_kernel(table, l_ref, factor, inverse_ref, o_ref, raw, ar, ai, flat, *, count, frames):
+    share = l_ref.shape[0]
+    chunks = count // GROUP
+    wide = 2 * count
+    copies = LANES // share
+    dims = (((1,), (1,)), ((), ()))
+
+    def sums(f, carry):
+        left = l_ref[f]
+        v = lax.dot_general(left, left, dims, preferred_element_type=F32)
+        at = pl.multiple_of(f * wide, wide)
+        pad = jnp.zeros((wide, LANES - wide), F32)
+        raw[pl.ds(at, wide), :] = jnp.concatenate([v * (1.0 / frames), pad], axis=1)
+        return carry
+
+    lax.fori_loop(0, share, sums, 0, unroll=8)
+
+    def turn(a, carry):
+        re = raw[pl.ds(a, share, stride=wide), :].T[:count]
+        im = raw[pl.ds(count + a, share, stride=wide), :].T[:count]
+        ar[a] = jnp.concatenate([re] * copies, axis=1)
+        ai[a] = jnp.concatenate([-im] * copies, axis=1)
+        return carry
+
+    lax.fori_loop(0, count, turn, 0, unroll=4)
+    row = lax.broadcasted_iota(jnp.int32, (count, LANES), 0)
+    zero = jnp.zeros((count, LANES), F32)
+
+    def begin(a, carry):
+        inverse_ref[a, 0] = jnp.where(row == a, 1.0, 0.0)
+        inverse_ref[a, 1] = zero
+        ar[a] = ar[a] + jnp.where(row == a, ar[a] * ridge + floor, 0.0)
+        return carry
+
+    lax.fori_loop(0, count, begin, 0, unroll=4)
+    for k in range(count):
+        scale = lax.rsqrt(ar[k, k : k + 1, :])
+        lr = jnp.where(row >= k, ar[k] * scale, 0.0)
+        li = jnp.where(row > k, ai[k] * scale, 0.0)
+        for c in range(chunks):
+            factor[k, 0, c] = lr[c * GROUP : (c + 1) * GROUP]
+            factor[k, 1, c] = li[c * GROUP : (c + 1) * GROUP]
+        ar[k], ai[k] = lr, li
+
+        def right(b, carry):
+            br, bi = ar[k, pl.ds(b, 1), :], ai[k, pl.ds(b, 1), :]
+            ar[b] = ar[b] - (lr * br + li * bi)
+            ai[b] = ai[b] - (li * br - lr * bi)
+            return carry
+
+        if k + 1 < count:
+            lax.fori_loop(k + 1, count, right, 0, unroll=min(2, count - k - 1))
+
+        def left(b, carry):
+            tr = inverse_ref[b, 0, k : k + 1, :] * scale
+            ti = inverse_ref[b, 1, k : k + 1, :] * scale
+            r, i = inverse_ref[b, 0], inverse_ref[b, 1]
+            nr, ni = r - (lr * tr - li * ti), i - (lr * ti + li * tr)
+            inverse_ref[b, 0] = jnp.where(row == k, tr, nr)
+            inverse_ref[b, 1] = jnp.where(row == k, ti, ni)
+            return carry
+
+        lax.fori_loop(0, k + 1, left, 0, unroll=min(2, k + 1))
+    for a in range(count):
+        for c in range(chunks):
+            at = c * GROUP * wide + a
+            rows = slice(c * GROUP, (c + 1) * GROUP)
+            flat[pl.ds(at, GROUP, stride=wide), :] = inverse_ref[a, 0, rows, :]
+            flat[pl.ds(at + count, GROUP, stride=wide), :] = -inverse_ref[a, 1, rows, :]
+    flatten(flat, o_ref, share)
+
+
+def whiten(table, stacked, count, share):
+    wide, frames = 2 * count, stacked.shape[2] // 2
+    shapes = [
+        (count, 2, count // GROUP, GROUP, LANES),
+        (count, 2, count, LANES),
+        (share, wide * count),
+    ]
+    state = VMEM((count, count, LANES), F32)
+    return pl.pallas_call(
+        functools.partial(whiten_kernel, count=count, frames=frames),
+        grid_spec=pltpu.PrefetchScalarGridSpec(
+            num_scalar_prefetch=1,
+            grid=(1,),
+            in_specs=[
+                pl.BlockSpec((share,) + stacked.shape[1:], lambda r, table: (table[0], 0, 0))
+            ],
+            out_specs=[
+                pl.BlockSpec(x, functools.partial(lambda n, r, table: (0,) * n, len(x)))
+                for x in shapes
+            ],
+            scratch_shapes=[
+                VMEM((share * wide, LANES), F32), state, state, VMEM((wide * count, LANES), F32),
+            ],
+        ),
+        out_shape=[jax.ShapeDtypeStruct(x, F32) for x in shapes],
+        compiler_params=options(),
+        cost_estimate=cost(3000 * count**3, share * stacked.shape[1] * stacked.shape[2] * 2),
+        name="whiten",
+    )(table, stacked)
+
+
+def sweep(parts, factor, inverse, count, share, frames):
     chunks = count // GROUP
     blocks = parts[0].shape[1]
     state = VMEM((count, chunks, GROUP, LANES), F32)
@@ -424,12 +546,12 @@
         compiler_params=options(),
         cost_estimate=cost(4500 * count**3, 4 * 3 * parts[0].size),
         name="sweep",
-    )(*parts)
-
-
-def apply_kernel(table, w_ref, l_ref, o_ref, mixing, rows, *, count):
+    )(*parts, factor, inverse)
+
+
+def apply_kernel(table, w_ref, l_ref, o_ref, mixing, *rows, count, spectra):
     share = w_ref.shape[1]
-    frames = o_ref.shape[3]
+    frames = l_ref.shape[2] // 2
     wide = 2 * count
     tiles = frames // LANES
     pitch = share + 8
@@ -447,44 +569,50 @@
         left = jnp.concatenate([high, middle, low], axis=0).astype(BF16)
         y = jnp.dot(left, l_ref[f], preferred_element_type=F32)
         y = y[:count] + (y[count : 2 * count] + y[2 * count :])
+        if not spectra:
+            lower = jnp.concatenate([y[:, frames:], -y[:, :frames]], axis=1)
+            o_ref[f] = jnp.concatenate([y, lower], axis=0).astype(BF16)
+            return carry
         for c in range(2):
             for i in range(tiles):
                 v = y[:, c * frames + i * LANES : c * frames + (i + 1) * LANES]
-                rows[i, pl.ds(c * count * pitch + f, count, stride=pitch), :] = v
+                rows[0][i, pl.ds(c * count * pitch + f, count, stride=pitch), :] = v
         return carry
 
     lax.fori_loop(0, share, one, 0, unroll=8)
+    if not spectra:
+        return
     for i in range(tiles):
-        v = rows[i].reshape(2, count, pitch, LANES)[:, :, :share]
+        v = rows[0][i].reshape(2, count, pitch, LANES)[:, :, :share]
         o_ref[:, :, :, i * LANES : (i + 1) * LANES] = v
 
 
-def apply(table, mixing, stacked, count):
+def apply(table, mixing, stacked, count, spectra):
     shares, share = mixing.shape[:2]
     bins, frames = stacked.shape[0], stacked.shape[2] // 2
+    block = pl.BlockSpec((share,) + stacked.shape[1:], lambda r, table: (table[r], 0, 0))
+    scratch = [VMEM((share * count, LANES), F32)]
+    if spectra:
+        shape = jax.ShapeDtypeStruct((2, count, bins, frames), F32)
+        out = pl.BlockSpec((2, count, share, frames), lambda r, table: (0, 0, table[r], 0))
+        scratch.append(VMEM((frames // LANES, 2 * count * (share + 8), LANES), F32))
+    else:
+        shape, out = jax.ShapeDtypeStruct(stacked.shape, BF16), block
     return pl.pallas_call(
-        functools.partial(apply_kernel, count=count),
+        functools.partial(apply_kernel, count=count, spectra=spectra),
         grid_spec=pltpu.PrefetchScalarGridSpec(
             num_scalar_prefetch=1,
             grid=(shares,),
-            in_specs=[
-                pl.BlockSpec((1,) + mixing.shape[1:], lambda r, table: (r, 0, 0)),
-                pl.BlockSpec((share,) + stacked.shape[1:], lambda r, table: (table[r], 0, 0)),
-            ],
-            out_specs=pl.BlockSpec(
-                (2, count, share, frames), lambda r, table: (0, 0, table[r], 0)
-            ),
-            scratch_shapes=[
-                VMEM((share * count, LANES), F32),
-                VMEM((frames // LANES, 2 * count * (share + 8), LANES), F32),
-            ],
+            in_specs=[pl.BlockSpec((1,) + mixing.shape[1:], lambda r, table: (r, 0, 0)), block],
+            out_specs=out,
+            scratch_shapes=scratch,
         ),
-        out_shape=jax.ShapeDtypeStruct((2, count, bins, frames), F32),
+        out_shape=shape,
         compiler_params=options(),
         cost_estimate=cost(
             16 * count * count * bins * frames, stacked.size * 2 + 8 * count * bins * frames
         ),
-        name="apply",
+        name="apply" if spectra else "whitened",
     )(table, mixing, stacked)
 
 
@@ -507,29 +635,36 @@
     )
     *powers, stacked = prepare(spectra, place, owners, each, chunks)
 
+    def shared(mixing):
+        near = [mixing] + [exchange(mixing, "frame", 2 * r) for r in range(1, depth)]
+        return jnp.stack(near + [exchange(v, "frame", 1) for v in near])
+
+    every = jnp.concatenate([keep, send])
+    factor, inverse, unmixing = whiten(keep, stacked, count, share)
+    white = apply(every, shared(unmixing), stacked, count, False)
+
+    arrived = []
+    for c in range(chunks):
+        pieces = powers[c * owners : (c + 1) * owners]
+        arrived.append([pieces[0]] + [exchange(pieces[m], "freq", m) for m in range(1, owners)])
     modelled = []
     for c in range(chunks):
-        pieces = powers[c * owners : (c + 1) * owners]
-        pieces = [pieces[0]] + [exchange(pieces[m], "freq", m) for m in range(1, owners)]
-        out = model(pieces, place, weights)
+        out = model(arrived[c], place, weights)
         modelled.append([out[0]] + [exchange(out[m], "freq", m) for m in range(1, owners)])
 
     laid = []
     variances = place
     for c in range(chunks):
-        sent, variances = covariance(send, place, stacked, modelled[c], variances, c, count)
-        kept, variances = covariance(keep, place, stacked, modelled[c], variances, c, count)
+        sent, variances = covariance(send, place, white, modelled[c], variances, c, count, BF16)
+        kept, variances = covariance(keep, place, white, modelled[c], variances, c, count, F32)
         parts = [None] * depth
         for r in list(range(1, depth)) + [0]:
             v = kept[r] + exchange(sent[r], "frame", 1)
-            parts[r] = v if r == 0 else exchange(v, "frame", 2 * r)
+            parts[r] = v if r == 0 else exchange(v.astype(BF16), "frame", 2 * r)
         laid.append(unpack(parts, count, share))
 
-    mixing = sweep(laid, count, share, frames * devices)
-    near = [mixing] + [exchange(mixing, "frame", 2 * r) for r in range(1, depth)]
-    far = [exchange(v, "frame", 1) for v in near]
-    demixed = apply(jnp.concatenate([keep, send]), jnp.stack(near + far), stacked, count)
-
+    mixing = sweep(laid, factor, inverse, count, share, frames * devices)
+    demixed = apply(every, shared(mixing), stacked, count, True)
     return demixed, variances
 
 

time: 424 us -> 352 us (0.83)
  waiting for transfers between devices: 114 us -> 70.6 us
  Pallas kernels: 206 us -> 184 us
  starting transfers between devices: 86.4 us -> 76.3 us
    pallas_call x6, Pallas kernels: 122 us -> 75.1 us  [covariance(): pl.pallas_call(functools.partial(covariance_kernel, owners=owners, count=...]
    ppermute x46 -> x53, waiting for transfers between devices: 114 us -> 70.6 us  [exchange(): return lax.ppermute(value, axis, [(i, i ^ mask) for i in range(size)])]
    pallas_call x1 -> x3, Pallas kernels: 17.3 us -> 42.4 us  [the longest x2 33.8 us: apply(): pl.pallas_call(functools.partial(apply_kernel, count=count, spectra=spect...]
    ppermute x46 -> x53, starting transfers between devices: 86.4 us -> 76.3 us  [exchange(): return lax.ppermute(value, axis, [(i, i ^ mask) for i in range(size)])]
    unnamed x18 -> x49, local copies, waits for them, and re-layouts: 12 us -> 16.9 us
  transfers between devices with their start and end apart: 46 -> 53, of which waited for: 12 -> 15; matrix products, arithmetic and copies ran while one was open for 4% -> 5% of each run, Pallas kernels for 37% -> 36%
where the time goes in v3:
time: 352 us; the launch traced here: 351 us
  Pallas kernels  184 us (52%)
  starting transfers between devices  76.3 us (22%)
  waiting for transfers between devices  70.6 us (20%)
  local copies, waits for them, and re-layouts  18 us (5%)
    ppermute x53, starting transfers between devices, exchange(): return lax.ppermute(value, axis, [(i, i ^ mask) for i in range(size)])  76.3 us
    pallas_call x6, Pallas kernels, covariance(): pl.pallas_call(functools.partial(covariance_kernel, owners=owners, count=...  75.1 us
    ppermute x53, waiting for transfers between devices, exchange(): return lax.ppermute(value, axis, [(i, i ^ mask) for i in range(size)])  70.6 us
    pallas_call x2, Pallas kernels, apply(): pl.pallas_call(functools.partial(apply_kernel, count=count, spectra=spect...  33.8 us
    pallas_call x3, Pallas kernels, model(): pl.pallas_call(functools.partial(model_kernel, owners=owners), grid=(each...  26.3 us
    unnamed x49, local copies, waits for them, and re-layouts  16.9 us
    pallas_call x1, Pallas kernels, prepare(): pl.pallas_call(functools.partial(prepare_kernel, owners=owners, each=each...  14.6 us
    pallas_call x1, Pallas kernels, sweep(): pl.pallas_call(functools.partial(sweep_kernel, count=count, share=share,...  14.5 us
  transfers between devices with their start and end apart: 53, of which 15 were waited for; matrix products, arithmetic and copies ran while one was open for 5% of the time, Pallas kernels for 36%

profile of v3, /device:TPU:0, one launch (start us, length us, event | category | flops | bytes accessed | tf_op | source)
XLA Modules:
  0.0 351.0 jit_solution(1881026870340405765)
XLA Ops:
  0.7 14.6 %prepare.1 = (bf16[2,256,256]{2,1,0:T(8,128)(2,1)S(1)}, bf16[2,256,256]{2,1,0:T(8,128)(2,1)}, bf16[2,256,256]{2,1,0:T(8,128)(2,1)S(1)}, bf16[2,256,256]{2,1,0:T(...) custom-call(s32[1]{0:T(128)} %bitcast.place.refs_4_, ...), custom_call_target="tpu_custom_call" | custom-call | flops 62914560 | bytes 25165824 | tf_op jit(solution)/shard_map/prepare/pallas_call | solution.py:78
  17.4 8.6 %whiten.1 = (f32[24,2,3,8,128]{4,3,2,1,0:T(8,128)S(1)}, f32[24,2,24,128]{3,2,1,0:T(8,128)S(1)}, f32[32,1152]{1,0:T(8,128)S(1)}) custom-call(s32[4]{0:T(128)S(1)} %fusion.10.table, bf16[256,48,512]{2,1,0:T(8,128)(2,1)} %get-tuple-element.42.l_ref), custom_call_target="tpu_custom_call" | custom-call | flops 41472000 | bytes 1572864 | tf_op jit(solution)/shard_map/whiten/pallas_call | solution.py:510
  26.0 3.0 collective-permute-start.3
  29.1 3.6 %collective-permute-start.2 = (f32[32,1152]{1,0:T(8,128)S(1)}, f32[32,1152]{1,0:T(8,128)S(1)}, u32[]{:S(2)}, u32[]{:S(2)}) collective-permute-start(f32[32,1152]{1,0:T(8,128)S(1)} %get-tuple-element.43), channel_id=1, source_target_pairs={{0,6},{1,7},{2,4},{3,5},{4,2},{5,3},{6,0},{7,1},{8,14},{9,15},{10,... | collective-permute-start | bytes 442376 | tf_op jit(solution)/shard_map/ppermute | solution.py:35
  33.5 3.9 %copy.15 = bf16[1024,1024]{0,1:T(8,128)(2,1)} copy(bf16[1024,1024]{1,0:T(8,128)(2,1)} %param.10) | data formatting | bytes 4194304 | tf_op args[2]
  37.4 3.9 %copy.16 = bf16[1024,1024]{0,1:T(8,128)(2,1)} copy(bf16[1024,1024]{1,0:T(8,128)(2,1)} %param.12) | data formatting | bytes 4194304 | tf_op args[4]
  41.4 3.9 %copy.17 = bf16[1024,1024]{0,1:T(8,128)(2,1)} copy(bf16[1024,1024]{1,0:T(8,128)(2,1)} %param.14) | data formatting | bytes 4194304 | tf_op args[6]
  45.4 1.5 collective-permute-start.8
  46.9 0.9 bitcast_dynamic-update-slice_fusion.14
  48.3 0.9 bitcast_dynamic-update-slice_fusion.13
  49.6 1.6 collective-permute-start.21
  51.2 0.9 bitcast_dynamic-update-slice_fusion.11
  52.3 2.5 collective-permute-done.8.refs_2_
  54.8 4.8 %collective-permute-done.9.refs_3_ = bf16[2,256,256]{2,1,0:T(8,128)(2,1)S(1)} collective-permute-done((bf16[2,256,256]{2,1,0:T(8,128)(2,1)}, bf16[2,256,256]{2,1,0:T(8,128)(2,1)S(1)}, u32[]{:S(2)}, u32[]{:S(2)}) %collective-permute-start.9) | collective-permute-done | bytes 262176 | tf_op jit(solution)/shard_map/ppermute | solution.py:35
  59.6 1.5 collective-permute-start.34
  61.9 8.9 %source_model.3 = (bf16[2,256,256]{2,1,0:T(8,128)(2,1)S(1)}, bf16[2,256,256]{2,1,0:T(8,128)(2,1)S(1)}, bf16[2,256,256]{2,1,0:T(8,128)(2,1)S(1)}, bf16[2,256,256]{2,1,0:T(8,128)(2,1)S(1)}) custom-call(s32[1]{0:T(128)} %bitcast.place.refs_4_, bf16[2,256,256]{2,1,0:T(8,128)(2,1)S(1)} %copy-done.9, bf16[2,256,256]{2,1,0:T(8,128)(2,1)} %collective-permute-done.7.refs_1_, ...), custom_call_target="tpu_custom_call" | custom-call | flops 3221225472 | bytes 6291456 | tf_op jit(solution)/shard_map/source_model/pallas_call | solution.py:155
  71.6 1.7 collective-permute-start.5
  73.4 8.7 %source_model.4 = (bf16[2,256,256]{2,1,0:T(8,128)(2,1)S(1)}, bf16[2,256,256]{2,1,0:T(8,128)(2,1)S(1)}, bf16[2,256,256]{2,1,0:T(8,128)(2,1)S(1)}, bf16[2,256,256]{2,1,0:T(8,128)(2,1)S(1)}) custom-call(s32[1]{0:T(128)} %bitcast.place.refs_4_, bf16[2,256,256]{2,1,0:T(8,128)(2,1)S(1)} %copy-done.3, bf16[2,256,256]{2,1,0:T(8,128)(2,1)S(1)} %collective-permute-done.20.refs_1_, ...), custom_call_target="tpu_custom_call" | custom-call | flops 3221225472 | bytes 6291456 | tf_op jit(solution)/shard_map/source_model/pallas_call | solution.py:155
  82.4 1.8 collective-permute-start.11
  84.2 8.7 %source_model.5 = (bf16[2,256,256]{2,1,0:T(8,128)(2,1)S(1)}, bf16[2,256,256]{2,1,0:T(8,128)(2,1)S(1)}, bf16[2,256,256]{2,1,0:T(8,128)(2,1)S(1)}, bf16[2,256,256]{2,1,0:T(8,128)(2,1)S(1)}) custom-call(s32[1]{0:T(128)} %bitcast.place.refs_4_, bf16[2,256,256]{2,1,0:T(8,128)(2,1)S(1)} %get-tuple-element.67.refs_0_, ...), custom_call_target="tpu_custom_call" | custom-call | flops 3221225472 | bytes 6291456 | tf_op jit(solution)/shard_map/source_model/pallas_call | solution.py:155
  93.6 1.8 collective-permute-start.24
  95.4 16.6 %whitened.1.l_ref = bf16[256,48,512]{2,1,0:T(8,128)(2,1)} custom-call(s32[8]{0:T(128)S(1)} %pad_add_fusion.table, f32[8,32,1152]{2,1,0:T(8,128)S(1)} %bitcast_dynamic-update-slice_fusion.8.w_ref, bf16[256,48,512]{2,1,0:T(8,128)(2,1)} %get-tuple-element.42.l_ref), custom_call_target="tpu_custom_call" | custom-call | flops 603979776 | bytes 25165824 | tf_op jit(solution)/shard_map/whitened/pallas_call | solution.py:601
  112.4 1.7 collective-permute-start.37
  114.1 12.5 %covariance.6 = (bf16[4,8,48,384]{3,2,1,0:T(8,128)(2,1)S(1)}, bf16[24,256,256]{2,1,0:T(8,128)(2,1)}) custom-call(s32[4]{0:T(128)S(1)} %fusion.9.table, s32[1]{0:T(128)} %bitcast.place.refs_4_, bf16[256,48,512]{2,1,0:T(8,128)(2,1)} %whitened.1.l_ref, bf16[2,256,256]{2,1,0:T(8,128)(2,1)S(1)} %get-tuple-element.48.refs_0_, ...), custom_call_target="tpu_custom_call" | custom-call | flops 2415919104 | bytes 8650752 | tf_op jit(solution)/shard_map/covariance/pallas_call | solution.py:219
  126.6 12.5 %covariance.7 = (f32[4,8,48,384]{3,2,1,0:T(8,128)S(1)}, bf16[24,256,256]{2,1,0:T(8,128)(2,1)}) custom-call(s32[4]{0:T(128)S(1)} %fusion.10.table, s32[1]{0:T(128)} %bitcast.place.refs_4_, bf16[256,48,512]{2,1,0:T(8,128)(2,1)} %whitened.1.l_ref, bf16[2,256,256]{2,1,0:T(8,128)(2,1)S(1)} %get-tuple-element.48.refs_0_, ...), custom_call_target="tpu_custom_call", output_to_operand_aliasing={{1}: (7, {})} | custom-call | flops 2415919104 | bytes 8650752 | tf_op jit(solution)/shard_map/covariance/pallas_call | solution.py:219
  139.3 1.6 collective-permute-start.18
  141.4 12.5 %covariance.8 = (bf16[4,8,48,384]{3,2,1,0:T(8,128)(2,1)S(1)}, bf16[24,256,256]{2,1,0:T(8,128)(2,1)}) custom-call(s32[4]{0:T(128)S(1)} %fusion.9.table, s32[1]{0:T(128)} %bitcast.place.refs_4_, bf16[256,48,512]{2,1,0:T(8,128)(2,1)} %whitened.1.l_ref, bf16[2,256,256]{2,1,0:T(8,128)(2,1)S(1)} %get-tuple-element.59.refs_0_, ...), custom_call_target="tpu_custom_call", output_to_operand_aliasing={{1}: (7, {})} | custom-call | flops 2415919104 | bytes 8650752 | tf_op jit(solution)/shard_map/covariance/pallas_call | solution.py:219
  153.9 12.5 %covariance.9 = (f32[4,8,48,384]{3,2,1,0:T(8,128)S(1)}, bf16[24,256,256]{2,1,0:T(8,128)(2,1)}) custom-call(s32[4]{0:T(128)S(1)} %fusion.10.table, s32[1]{0:T(128)} %bitcast.place.refs_4_, bf16[256,48,512]{2,1,0:T(8,128)(2,1)} %whitened.1.l_ref, bf16[2,256,256]{2,1,0:T(8,128)(2,1)S(1)} %get-tuple-element.59.refs_0_, ...), custom_call_target="tpu_custom_call", output_to_operand_aliasing={{1}: (7, {})} | custom-call | flops 2415919104 | bytes 8650752 | tf_op jit(solution)/shard_map/covariance/pallas_call | solution.py:219
  166.6 1.6 collective-permute-start.14
  168.7 1.5 collective-permute-start.31
  170.2 12.5 %covariance.10 = (bf16[4,8,48,384]{3,2,1,0:T(8,128)(2,1)S(1)}, bf16[24,256,256]{2,1,0:T(8,128)(2,1)}) custom-call(s32[4]{0:T(128)S(1)} %fusion.9.table, s32[1]{0:T(128)} %bitcast.place.refs_4_, bf16[256,48,512]{2,1,0:T(8,128)(2,1)} %whitened.1.l_ref, bf16[2,256,256]{2,1,0:T(8,128)(2,1)S(1)} %get-tuple-element.71.refs_0_, ...), custom_call_target="tpu_custom_call", output_to_operand_aliasing={{1}: (7, {})} | custom-call | flops 2415919104 | bytes 8650752 | tf_op jit(solution)/shard_map/covariance/pallas_call | solution.py:219
  182.7 12.5 %covariance.11 = (f32[4,8,48,384]{3,2,1,0:T(8,128)S(1)}, bf16[24,256,256]{2,1,0:T(8,128)(2,1)}) custom-call(s32[4]{0:T(128)S(1)} %fusion.10.table, s32[1]{0:T(128)} %bitcast.place.refs_4_, bf16[256,48,512]{2,1,0:T(8,128)(2,1)} %whitened.1.l_ref, bf16[2,256,256]{2,1,0:T(8,128)(2,1)S(1)} %get-tuple-element.71.refs_0_, ...), custom_call_target="tpu_custom_call", output_to_operand_aliasing={{1}: (7, {})} | custom-call | flops 2415919104 | bytes 8650752 | tf_op jit(solution)/shard_map/covariance/pallas_call | solution.py:219
  196.0 1.5 collective-permute-start.27
  198.0 1.5 collective-permute-start.44
  200.4 5.0 %collective-permute-done.29 = bf16[8,48,384]{2,1,0:T(8,128)(2,1)S(1)} collective-permute-done((bf16[8,48,384]{2,1,0:T(8,128)(2,1)S(1)}, bf16[8,48,384]{2,1,0:T(8,128)(2,1)S(1)}, u32[]{:S(2)}, u32[]{:S(2)}) %collective-permute-start.29) | collective-permute-done | bytes 294944 | tf_op jit(solution)/shard_map/ppermute | solution.py:35
  205.9 5.8 %collective-permute-done.27 = bf16[8,48,384]{2,1,0:T(8,128)(2,1)S(1)} collective-permute-done((bf16[8,48,384]{2,1,0:T(8,128)(2,1)S(1)}, bf16[8,48,384]{2,1,0:T(8,128)(2,1)S(1)}, u32[]{:S(2)}, u32[]{:S(2)}) %collective-permute-start.27) | collective-permute-done | bytes 294944 | tf_op jit(solution)/shard_map/ppermute | solution.py:35
  212.2 5.8 %collective-permute-done.26 = bf16[8,48,384]{2,1,0:T(8,128)(2,1)S(1)} collective-permute-done((bf16[8,48,384]{2,1,0:T(8,128)(2,1)S(1)}, bf16[8,48,384]{2,1,0:T(8,128)(2,1)S(1)}, u32[]{:S(2)}, u32[]{:S(2)}) %collective-permute-start.26) | collective-permute-done | bytes 294944 | tf_op jit(solution)/shard_map/ppermute | solution.py:35
  218.1 3.6 %collective-permute-start.19 = (bf16[8,48,384]{2,1,0:T(8,128)(2,1)S(1)}, bf16[8,48,384]{2,1,0:T(8,128)(2,1)S(1)}, u32[]{:S(2)}, u32[]{:S(2)}) collective-permute-start(bf16[8,48,384]{2,1,0:T(8,128)(2,1)S(1)} %get-tuple-element.90), channel_id=1, source_target_pairs={{0,6},{1,7},{2,4},{3,5},{4,2},{5,3},{6,0},{7,1},{8,14},{9,15},{10,... | collective-permute-start | bytes 884744 | tf_op jit(solution)/shard_map/ppermute | solution.py:35
  221.9 2.4 collective-permute-done.44
  224.4 2.1 collective-permute-start.17
  226.5 4.2 %collective-permute-done.42 = bf16[8,48,384]{2,1,0:T(8,128)(2,1)S(1)} collective-permute-done((bf16[8,48,384]{2,1,0:T(8,128)(2,1)S(1)}, bf16[8,48,384]{2,1,0:T(8,128)(2,1)S(1)}, u32[]{:S(2)}, u32[]{:S(2)}) %collective-permute-start.42) | collective-permute-done | bytes 294944 | tf_op jit(solution)/shard_map/ppermute | solution.py:35
  230.7 1.2 collective-permute-start.15
  231.9 5.1 %collective-permute-done.40 = bf16[8,48,384]{2,1,0:T(8,128)(2,1)S(1)} collective-permute-done((bf16[8,48,384]{2,1,0:T(8,128)(2,1)S(1)}, bf16[8,48,384]{2,1,0:T(8,128)(2,1)S(1)}, u32[]{:S(2)}, u32[]{:S(2)}) %collective-permute-start.40) | collective-permute-done | bytes 294944 | tf_op jit(solution)/shard_map/ppermute | solution.py:35
  237.0 3.6 %collective-permute-start.32 = (bf16[8,48,384]{2,1,0:T(8,128)(2,1)S(1)}, bf16[8,48,384]{2,1,0:T(8,128)(2,1)S(1)}, u32[]{:S(2)}, u32[]{:S(2)}) collective-permute-start(bf16[8,48,384]{2,1,0:T(8,128)(2,1)S(1)} %get-tuple-element.86), channel_id=1, source_target_pairs={{0,6},{1,7},{2,4},{3,5},{4,2},{5,3},{6,0},{7,1},{8,14},{9,15},{10,... | collective-permute-start | bytes 884744 | tf_op jit(solution)/shard_map/ppermute | solution.py:35
  240.6 0.8 collective-permute-done.39
  241.5 2.2 collective-permute-start.30
  243.9 2.1 collective-permute-start.28
  246.0 11.1 %collective-permute-done.17.refs_2_ = bf16[8,48,384]{2,1,0:T(8,128)(2,1)S(1)} collective-permute-done((bf16[8,48,384]{2,1,0:T(8,128)(2,1)S(1)}, bf16[8,48,384]{2,1,0:T(8,128)(2,1)S(1)}, u32[]{:S(2)}, u32[]{:S(2)}) %collective-permute-start.17) | collective-permute-done | bytes 294944 | tf_op jit(solution)/shard_map/ppermute | solution.py:35
  257.1 4.7 %collective-permute-start.45 = (bf16[8,48,384]{2,1,0:T(8,128)(2,1)S(1)}, bf16[8,48,384]{2,1,0:T(8,128)(2,1)S(1)}, u32[]{:S(2)}, u32[]{:S(2)}) collective-permute-start(bf16[8,48,384]{2,1,0:T(8,128)(2,1)S(1)} %get-tuple-element.82), channel_id=1, source_target_pairs={{0,6},{1,7},{2,4},{3,5},{4,2},{5,3},{6,0},{7,1},{8,14},{9,15},{10,... | collective-permute-start | bytes 884744 | tf_op jit(solution)/shard_map/ppermute | solution.py:35
  261.8 14.8 %collective-permute-start.41 = (bf16[8,48,384]{2,1,0:T(8,128)(2,1)S(1)}, bf16[8,48,384]{2,1,0:T(8,128)(2,1)S(1)}, u32[]{:S(2)}, u32[]{:S(2)}) collective-permute-start(bf16[8,48,384]{2,1,0:T(8,128)(2,1)S(1)} %get-tuple-element.84), channel_id=1, source_target_pairs={{0,2},{1,3},{2,0},{3,1},{4,6},{5,7},{6,4},{7,5},{8,10},{9,11},{10,... | collective-permute-start | bytes 884744 | tf_op jit(solution)/shard_map/ppermute | solution.py:35
  276.6 3.7 %unpack.3.refs_0_ = f32[24,6,2,8,128]{4,3,2,1,0:T(8,128)S(1)} custom-call(f32[8,48,384]{2,1,0:T(8,128)S(1)} %get-tuple-element.93.refs_0_, bf16[8,48,384]{2,1,0:T(8,128)(2,1)S(1)} %collective-permute-done.15.refs_1_, bf16[8,48,384]{2,1,0:T(8,128)(2,1)S(1)} %collective-permute-done.17.refs_2_, bf16[8,48,384]{2,1,0:T(8,128)(2,1)S(1)} %collective-permute-done.19.refs_3_), custom_call_target="tpu_custom_call" | custom-call | flops 1474560 | bytes 3538944 | tf_op jit(solution)/shard_map/unpack/pallas_call | solution.py:297
  280.4 2.1 collective-permute-done.30.refs_2_
  282.4 3.7 %unpack.4.refs_1_ = f32[24,6,2,8,128]{4,3,2,1,0:T(8,128)S(1)} custom-call(f32[8,48,384]{2,1,0:T(8,128)S(1)} %get-tuple-element.89.refs_0_, bf16[8,48,384]{2,1,0:T(8,128)(2,1)S(1)} %collective-permute-done.28.refs_1_, bf16[8,48,384]{2,1,0:T(8,128)(2,1)S(1)} %collective-permute-done.30.refs_2_, bf16[8,48,384]{2,1,0:T(8,128)(2,1)S(1)} %collective-permute-done.32.refs_3_), custom_call_target="tpu_custom_call" | custom-call | flops 1474560 | bytes 3538944 | tf_op jit(solution)/shard_map/unpack/pallas_call | solution.py:297
  286.2 7.4 %collective-permute-done.43.refs_2_ = bf16[8,48,384]{2,1,0:T(8,128)(2,1)S(1)} collective-permute-done((bf16[8,48,384]{2,1,0:T(8,128)(2,1)S(1)}, bf16[8,48,384]{2,1,0:T(8,128)(2,1)S(1)}, u32[]{:S(2)}, u32[]{:S(2)}) %collective-permute-start.43) | collective-permute-done | bytes 294944 | tf_op jit(solution)/shard_map/ppermute | solution.py:35
  293.6 3.7 %unpack.5.refs_2_ = f32[24,6,2,8,128]{4,3,2,1,0:T(8,128)S(1)} custom-call(f32[8,48,384]{2,1,0:T(8,128)S(1)} %get-tuple-element.85.refs_0_, bf16[8,48,384]{2,1,0:T(8,128)(2,1)S(1)} %collective-permute-done.41.refs_1_, bf16[8,48,384]{2,1,0:T(8,128)(2,1)S(1)} %collective-permute-done.43.refs_2_, bf16[8,48,384]{2,1,0:T(8,128)(2,1)S(1)} %collective-permute-done.45.refs_3_), custom_call_target="tpu_custom_call" | custom-call | flops 1474560 | bytes 3538944 | tf_op jit(solution)/shard_map/unpack/pallas_call | solution.py:297
  297.3 14.5 %sweep.1 = f32[32,1152]{1,0:T(8,128)S(1)} custom-call(f32[24,6,2,8,128]{4,3,2,1,0:T(8,128)S(1)} %unpack.3.refs_0_, f32[24,6,2,8,128]{4,3,2,1,0:T(8,128)S(1)} %unpack.4.refs_1_, f32[24,6,2,8,128]{4,3,2,1,0:T(8,128)S(1)} %unpack.5.refs_2_, f32[24,2,3,8,128]{4,3,2,1,0:T(8,128)S(1)} %get-tuple-element.79.refs_3_, f32[24,2,24,128]{3,2,1,0:T(8,128)S(1)} %get-tuple-element.80.refs_4_), custom_call_target="tpu_custom_call" | custom-call | flops 62208000 | bytes 3538944 | tf_op jit(solution)/shard_map/sweep/pallas_call | solution.py:537
  312.3 2.4 collective-permute-start.48
  314.8 2.0 collective-permute-start.46
  316.8 4.2 %collective-permute-done.48 = f32[32,1152]{1,0:T(8,128)S(1)} collective-permute-done((f32[32,1152]{1,0:T(8,128)S(1)}, f32[32,1152]{1,0:T(8,128)S(1)}, u32[]{:S(2)}, u32[]{:S(2)}) %collective-permute-start.48) | collective-permute-done | bytes 147488 | tf_op jit(solution)/shard_map/ppermute | solution.py:35
  320.9 1.5 collective-permute-start.52
  322.5 3.5 %collective-permute-done.47 = f32[32,1152]{1,0:T(8,128)S(1)} collective-permute-done((f32[32,1152]{1,0:T(8,128)S(1)}, f32[32,1152]{1,0:T(8,128)S(1)}, u32[]{:S(2)}, u32[]{:S(2)}) %collective-permute-start.47) | collective-permute-done | bytes 147488 | tf_op jit(solution)/shard_map/ppermute | solution.py:35
  326.0 1.5 collective-permute-start.51
  328.1 5.5 %collective-permute-done.50 = f32[32,1152]{1,0:T(8,128)S(1)} collective-permute-done((f32[32,1152]{1,0:T(8,128)S(1)}, f32[32,1152]{1,0:T(8,128)S(1)}, u32[]{:S(2)}, u32[]{:S(2)}) %collective-permute-start.50) | collective-permute-done | bytes 147488 | tf_op jit(solution)/shard_map/ppermute | solution.py:35
  333.7 17.3 %apply.1 = f32[2,24,256,256]{3,2,1,0:T(8,128)} custom-call(s32[8]{0:T(128)S(1)} %pad_add_fusion.table, f32[8,32,1152]{2,1,0:T(8,128)S(1)} %bitcast_dynamic-update-slice_fusion.w_ref, bf16[256,48,512]{2,1,0:T(8,128)(2,1)} %get-tuple-element.42.l_ref), custom_call_target="tpu_custom_call" | custom-call | flops 603979776 | bytes 25165824 | tf_op jit(solution)/shard_map/apply/pallas_call | solution.py:601
  (123 shorter events, 12.9 us)
Async XLA Ops:
  17.4 8.6 %copy-start.2 = (bf16[2,256,256]{2,1,0:T(8,128)(2,1)}, bf16[2,256,256]{2,1,0:T(8,128)(2,1)S(1)}, u32[]{:S(2)}) copy-start(bf16[2,256,256]{2,1,0:T(8,128)(2,1)S(1)} %get-tuple-element.55.refs_0_) | copy-start | bytes 786436
  17.4 8.6 %copy-start.4 = (bf16[2,256,256]{2,1,0:T(8,128)(2,1)}, bf16[2,256,256]{2,1,0:T(8,128)(2,1)S(1)}, u32[]{:S(2)}) copy-start(bf16[2,256,256]{2,1,0:T(8,128)(2,1)S(1)} %get-tuple-element.58) | copy-start | bytes 786436
  17.4 8.6 %copy-start.6 = (bf16[2,256,256]{2,1,0:T(8,128)(2,1)}, bf16[2,256,256]{2,1,0:T(8,128)(2,1)S(1)}, u32[]{:S(2)}) copy-start(bf16[2,256,256]{2,1,0:T(8,128)(2,1)S(1)} %get-tuple-element.57) | copy-start | bytes 786436
  17.4 8.6 %copy-start.7 = (bf16[2,256,256]{2,1,0:T(8,128)(2,1)}, bf16[2,256,256]{2,1,0:T(8,128)(2,1)S(1)}, u32[]{:S(2)}) copy-start(bf16[2,256,256]{2,1,0:T(8,128)(2,1)S(1)} %get-tuple-element.56) | copy-start | bytes 786436
  26.0 23.6 %collective-permute-start.3 = (f32[32,1152]{1,0:T(8,128)S(1)}, f32[32,1152]{1,0:T(8,128)}, u32[]{:S(2)}, u32[]{:S(2)}) collective-permute-start(f32[32,1152]{1,0:T(8,128)S(1)} %get-tuple-element.43), channel_id=1, source_target_pairs={{0,1},{1,0},{2,3},{3,2},{4,5},{5,4},{6,7},{7,6},{8,9},{9,8},{10,11... | collective-permute-start | bytes 442376 | tf_op jit(solution)/shard_map/ppermute | solution.py:35
  29.1 20.2 %collective-permute-start.2 = (f32[32,1152]{1,0:T(8,128)S(1)}, f32[32,1152]{1,0:T(8,128)S(1)}, u32[]{:S(2)}, u32[]{:S(2)}) collective-permute-start(f32[32,1152]{1,0:T(8,128)S(1)} %get-tuple-element.43), channel_id=1, source_target_pairs={{0,6},{1,7},{2,4},{3,5},{4,2},{5,3},{6,0},{7,1},{8,14},{9,15},{10,... | collective-permute-start | bytes 442376 | tf_op jit(solution)/shard_map/ppermute | solution.py:35
  32.7 15.2 %collective-permute-start.1 = (f32[32,1152]{1,0:T(8,128)S(1)}, f32[32,1152]{1,0:T(8,128)}, u32[]{:S(2)}, u32[]{:S(2)}) collective-permute-start(f32[32,1152]{1,0:T(8,128)S(1)} %get-tuple-element.43), channel_id=1, source_target_pairs={{0,4},{1,5},{2,6},{3,7},{4,0},{5,1},{6,2},{7,3},{8,12},{9,13},{10,... | collective-permute-start | bytes 442376 | tf_op jit(solution)/shard_map/ppermute | solution.py:35
  32.7 12.7 %collective-permute-start = (f32[32,1152]{1,0:T(8,128)S(1)}, f32[32,1152]{1,0:T(8,128)}, u32[]{:S(2)}, u32[]{:S(2)}) collective-permute-start(f32[32,1152]{1,0:T(8,128)S(1)} %get-tuple-element.43), channel_id=1, source_target_pairs={{0,2},{1,3},{2,0},{3,1},{4,6},{5,7},{6,4},{7,5},{8,10},{9,11},{10,... | collective-permute-start | bytes 442376 | tf_op jit(solution)/shard_map/ppermute | solution.py:35
  33.5 18.7 %collective-permute-start.7 = (bf16[2,256,256]{2,1,0:T(8,128)(2,1)}, bf16[2,256,256]{2,1,0:T(8,128)(2,1)}, u32[]{:S(2)}, u32[]{:S(2)}) collective-permute-start(bf16[2,256,256]{2,1,0:T(8,128)(2,1)} %get-tuple-element.45), channel_id=1, source_target_pairs={{0,8},{8,0},{16,24},{24,16},{1,9},{9,1},{17,25},{25,17},{2,10},{10... | collective-permute-start | bytes 786440 | tf_op jit(solution)/shard_map/ppermute | solution.py:35
  45.3 9.4 %copy-start.1 = (bf16[2,256,256]{2,1,0:T(8,128)(2,1)S(1)}, bf16[2,256,256]{2,1,0:T(8,128)(2,1)}, u32[]{:S(2)}) copy-start(bf16[2,256,256]{2,1,0:T(8,128)(2,1)} %copy-done) | copy-start | bytes 786436
  45.3 15.8 %copy-start.12 = (f32[1024]{0:T(1024)S(1)}, f32[1024]{0:T(1024)}, u32[]{:S(2)}) copy-start(f32[1024]{0:T(1024)} %param.9) | copy-start | bytes 12292
  45.3 16.0 %copy-start.13 = (f32[1024]{0:T(1024)S(1)}, f32[1024]{0:T(1024)}, u32[]{:S(2)}) copy-start(f32[1024]{0:T(1024)} %param.11) | copy-start | bytes 12292
  45.3 16.2 %copy-start.14 = (f32[1024]{0:T(1024)S(1)}, f32[1024]{0:T(1024)}, u32[]{:S(2)}) copy-start(f32[1024]{0:T(1024)} %param.13) | copy-start | bytes 12292
  45.4 9.3 %collective-permute-start.8 = (bf16[2,256,256]{2,1,0:T(8,128)(2,1)}, bf16[2,256,256]{2,1,0:T(8,128)(2,1)S(1)}, u32[]{:S(2)}, u32[]{:S(2)}) collective-permute-start(bf16[2,256,256]{2,1,0:T(8,128)(2,1)} %copy-done.11), channel_id=1, source_target_pairs={{0,16},{8,24},{16,0},{24,8},{1,17},{9,25},{17,1},{25,9},{2,18},{10... | collective-permute-start | bytes 786440 | tf_op jit(solution)/shard_map/ppermute | solution.py:35
  47.9 13.8 %copy-start.15 = (f32[1024]{0:T(1024)S(1)}, f32[1024]{0:T(1024)}, u32[]{:S(2)}) copy-start(f32[1024]{0:T(1024)} %param.15) | copy-start | bytes 12292
  47.9 11.7 %collective-permute-start.9 = (bf16[2,256,256]{2,1,0:T(8,128)(2,1)}, bf16[2,256,256]{2,1,0:T(8,128)(2,1)S(1)}, u32[]{:S(2)}, u32[]{:S(2)}) collective-permute-start(bf16[2,256,256]{2,1,0:T(8,128)(2,1)} %copy-done.10), channel_id=1, source_target_pairs={{0,24},{8,16},{16,8},{24,0},{1,25},{9,17},{17,9},{25,1},{2,26},{10... | collective-permute-start | bytes 786440 | tf_op jit(solution)/shard_map/ppermute | solution.py:35
  49.2 21.6 %collective-permute-start.20 = (bf16[2,256,256]{2,1,0:T(8,128)(2,1)}, bf16[2,256,256]{2,1,0:T(8,128)(2,1)S(1)}, u32[]{:S(2)}, u32[]{:S(2)}) collective-permute-start(bf16[2,256,256]{2,1,0:T(8,128)(2,1)} %copy-done.7), channel_id=1, source_target_pairs={{0,8},{8,0},{16,24},{24,16},{1,9},{9,1},{17,25},{25,17},{2,10},{10... | collective-permute-start | bytes 786440 | tf_op jit(solution)/shard_map/ppermute | solution.py:35
  49.6 12.3 %copy-start.9 = (bf16[2,256,256]{2,1,0:T(8,128)(2,1)S(1)}, bf16[2,256,256]{2,1,0:T(8,128)(2,1)}, u32[]{:S(2)}) copy-start(bf16[2,256,256]{2,1,0:T(8,128)(2,1)} %copy-done.8) | copy-start | bytes 786436
  49.6 21.7 %collective-permute-start.21 = (bf16[2,256,256]{2,1,0:T(8,128)(2,1)}, bf16[2,256,256]{2,1,0:T(8,128)(2,1)S(1)}, u32[]{:S(2)}, u32[]{:S(2)}) collective-permute-start(bf16[2,256,256]{2,1,0:T(8,128)(2,1)} %copy-done.6), channel_id=1, source_target_pairs={{0,16},{8,24},{16,0},{24,8},{1,17},{9,25},{17,1},{25,9},{2,18},{10... | collective-permute-start | bytes 786440 | tf_op jit(solution)/shard_map/ppermute | solution.py:35
  52.1 19.5 %collective-permute-start.22 = (bf16[2,256,256]{2,1,0:T(8,128)(2,1)S(1)}, bf16[2,256,256]{2,1,0:T(8,128)(2,1)S(1)}, u32[]{:S(2)}, u32[]{:S(2)}) collective-permute-start(bf16[2,256,256]{2,1,0:T(8,128)(2,1)S(1)} %copy-done.5), channel_id=1, source_target_pairs={{0,24},{8,16},{16,8},{24,0},{1,25},{9,17},{17,9},{25,1},{2,26},{10... | collective-permute-start | bytes 786440 | tf_op jit(solution)/shard_map/ppermute | solution.py:35
  54.8 27.3 %collective-permute-start.33 = (bf16[2,256,256]{2,1,0:T(8,128)(2,1)S(1)}, bf16[2,256,256]{2,1,0:T(8,128)(2,1)S(1)}, u32[]{:S(2)}, u32[]{:S(2)}) collective-permute-start(bf16[2,256,256]{2,1,0:T(8,128)(2,1)S(1)} %copy-done.1), channel_id=1, source_target_pairs={{0,8},{8,0},{16,24},{24,16},{1,9},{9,1},{17,25},{25,17},{2,10},{10... | collective-permute-start | bytes 786440 | tf_op jit(solution)/shard_map/ppermute | solution.py:35
  59.6 22.8 %collective-permute-start.34 = (bf16[2,256,256]{2,1,0:T(8,128)(2,1)S(1)}, bf16[2,256,256]{2,1,0:T(8,128)(2,1)S(1)}, u32[]{:S(2)}, u32[]{:S(2)}) collective-permute-start(bf16[2,256,256]{2,1,0:T(8,128)(2,1)S(1)} %get-tuple-element.69), channel_id=1, source_target_pairs={{0,16},{8,24},{16,0},{24,8},{1,17},{9,25},{17,1},{25,9},{2,18},{10... | collective-permute-start | bytes 786440 | tf_op jit(solution)/shard_map/ppermute | solution.py:35
  61.9 11.4 %copy-start.3 = (bf16[2,256,256]{2,1,0:T(8,128)(2,1)S(1)}, bf16[2,256,256]{2,1,0:T(8,128)(2,1)}, u32[]{:S(2)}) copy-start(bf16[2,256,256]{2,1,0:T(8,128)(2,1)} %copy-done.2) | copy-start | bytes 786436
  70.8 11.6 %collective-permute-start.35 = (bf16[2,256,256]{2,1,0:T(8,128)(2,1)S(1)}, bf16[2,256,256]{2,1,0:T(8,128)(2,1)S(1)}, u32[]{:S(2)}, u32[]{:S(2)}) collective-permute-start(bf16[2,256,256]{2,1,0:T(8,128)(2,1)S(1)} %get-tuple-element.70), channel_id=1, source_target_pairs={{0,24},{8,16},{16,8},{24,0},{1,25},{9,17},{17,9},{25,1},{2,26},{10... | collective-permute-start | bytes 786440 | tf_op jit(solution)/shard_map/ppermute | solution.py:35
  71.3 22.2 %collective-permute-start.6 = (f32[32,1152]{1,0:T(8,128)S(1)}, f32[32,1152]{1,0:T(8,128)S(1)}, u32[]{:S(2)}, u32[]{:S(2)}) collective-permute-start(f32[32,1152]{1,0:T(8,128)S(1)} %collective-permute-done.2), channel_id=1, source_target_pairs={{0,1},{1,0},{2,3},{3,2},{4,5},{5,4},{6,7},{7,6},{8,9},{9,8},{10,11... | collective-permute-start | bytes 442376 | tf_op jit(solution)/shard_map/ppermute | solution.py:35
  71.6 21.5 %collective-permute-start.5 = (f32[32,1152]{1,0:T(8,128)}, f32[32,1152]{1,0:T(8,128)S(1)}, u32[]{:S(2)}, u32[]{:S(2)}) collective-permute-start(f32[32,1152]{1,0:T(8,128)} %collective-permute-done.1), channel_id=1, source_target_pairs={{0,1},{1,0},{2,3},{3,2},{4,5},{5,4},{6,7},{7,6},{8,9},{9,8},{10,11... | collective-permute-start | bytes 442376 | tf_op jit(solution)/shard_map/ppermute | solution.py:35
  82.1 10.9 %collective-permute-start.4 = (f32[32,1152]{1,0:T(8,128)}, f32[32,1152]{1,0:T(8,128)S(1)}, u32[]{:S(2)}, u32[]{:S(2)}) collective-permute-start(f32[32,1152]{1,0:T(8,128)} %collective-permute-done), channel_id=1, source_target_pairs={{0,1},{1,0},{2,3},{3,2},{4,5},{5,4},{6,7},{7,6},{8,9},{9,8},{10,11... | collective-permute-start | bytes 442376 | tf_op jit(solution)/shard_map/ppermute | solution.py:35
  82.4 29.5 %collective-permute-start.10 = (bf16[2,256,256]{2,1,0:T(8,128)(2,1)S(1)}, bf16[2,256,256]{2,1,0:T(8,128)(2,1)S(1)}, u32[]{:S(2)}, u32[]{:S(2)}) collective-permute-start(bf16[2,256,256]{2,1,0:T(8,128)(2,1)S(1)} %get-tuple-element.49), channel_id=1, source_target_pairs={{0,8},{8,0},{16,24},{24,16},{1,9},{9,1},{17,25},{25,17},{2,10},{10... | collective-permute-start | bytes 786440 | tf_op jit(solution)/shard_map/ppermute | solution.py:35
  82.4 29.5 %collective-permute-start.11 = (bf16[2,256,256]{2,1,0:T(8,128)(2,1)S(1)}, bf16[2,256,256]{2,1,0:T(8,128)(2,1)S(1)}, u32[]{:S(2)}, u32[]{:S(2)}) collective-permute-start(bf16[2,256,256]{2,1,0:T(8,128)(2,1)S(1)} %get-tuple-element.50), channel_id=1, source_target_pairs={{0,16},{8,24},{16,0},{24,8},{1,17},{9,25},{17,1},{25,9},{2,18},{10... | collective-permute-start | bytes 786440 | tf_op jit(solution)/shard_map/ppermute | solution.py:35
  93.0 19.4 %collective-permute-start.12 = (bf16[2,256,256]{2,1,0:T(8,128)(2,1)S(1)}, bf16[2,256,256]{2,1,0:T(8,128)(2,1)S(1)}, u32[]{:S(2)}, u32[]{:S(2)}) collective-permute-start(bf16[2,256,256]{2,1,0:T(8,128)(2,1)S(1)} %get-tuple-element.51), channel_id=1, source_target_pairs={{0,24},{8,16},{16,8},{24,0},{1,25},{9,17},{17,9},{25,1},{2,26},{10... | collective-permute-start | bytes 786440 | tf_op jit(solution)/shard_map/ppermute | solution.py:35
  93.1 46.1 %collective-permute-start.23 = (bf16[2,256,256]{2,1,0:T(8,128)(2,1)S(1)}, bf16[2,256,256]{2,1,0:T(8,128)(2,1)S(1)}, u32[]{:S(2)}, u32[]{:S(2)}) collective-permute-start(bf16[2,256,256]{2,1,0:T(8,128)(2,1)S(1)} %get-tuple-element.60), channel_id=1, source_target_pairs={{0,8},{8,0},{16,24},{24,16},{1,9},{9,1},{17,25},{25,17},{2,10},{10... | collective-permute-start | bytes 786440 | tf_op jit(solution)/shard_map/ppermute | solution.py:35
  93.6 45.8 %collective-permute-start.24 = (bf16[2,256,256]{2,1,0:T(8,128)(2,1)S(1)}, bf16[2,256,256]{2,1,0:T(8,128)(2,1)S(1)}, u32[]{:S(2)}, u32[]{:S(2)}) collective-permute-start(bf16[2,256,256]{2,1,0:T(8,128)(2,1)S(1)} %get-tuple-element.61), channel_id=1, source_target_pairs={{0,16},{8,24},{16,0},{24,8},{1,17},{9,25},{17,1},{25,9},{2,18},{10... | collective-permute-start | bytes 786440 | tf_op jit(solution)/shard_map/ppermute | solution.py:35
  111.9 29.0 %collective-permute-start.25 = (bf16[2,256,256]{2,1,0:T(8,128)(2,1)S(1)}, bf16[2,256,256]{2,1,0:T(8,128)(2,1)S(1)}, u32[]{:S(2)}, u32[]{:S(2)}) collective-permute-start(bf16[2,256,256]{2,1,0:T(8,128)(2,1)S(1)} %get-tuple-element.62), channel_id=1, source_target_pairs={{0,24},{8,16},{16,8},{24,0},{1,25},{9,17},{17,9},{25,1},{2,26},{10... | collective-permute-start | bytes 786440 | tf_op jit(solution)/shard_map/ppermute | solution.py:35
  111.9 54.7 %collective-permute-start.36 = (bf16[2,256,256]{2,1,0:T(8,128)(2,1)S(1)}, bf16[2,256,256]{2,1,0:T(8,128)(2,1)S(1)}, u32[]{:S(2)}, u32[]{:S(2)}) collective-permute-start(bf16[2,256,256]{2,1,0:T(8,128)(2,1)S(1)} %get-tuple-element.72), channel_id=1, source_target_pairs={{0,8},{8,0},{16,24},{24,16},{1,9},{9,1},{17,25},{25,17},{2,10},{10... | collective-permute-start | bytes 786440 | tf_op jit(solution)/shard_map/ppermute | solution.py:35
  112.4 55.8 %collective-permute-start.37 = (bf16[2,256,256]{2,1,0:T(8,128)(2,1)S(1)}, bf16[2,256,256]{2,1,0:T(8,128)(2,1)S(1)}, u32[]{:S(2)}, u32[]{:S(2)}) collective-permute-start(bf16[2,256,256]{2,1,0:T(8,128)(2,1)S(1)} %get-tuple-element.73), channel_id=1, source_target_pairs={{0,16},{8,24},{16,0},{24,8},{1,17},{9,25},{17,1},{25,9},{2,18},{10... | collective-permute-start | bytes 786440 | tf_op jit(solution)/shard_map/ppermute | solution.py:35
  139.2 29.5 %collective-permute-start.38 = (bf16[2,256,256]{2,1,0:T(8,128)(2,1)S(1)}, bf16[2,256,256]{2,1,0:T(8,128)(2,1)S(1)}, u32[]{:S(2)}, u32[]{:S(2)}) collective-permute-start(bf16[2,256,256]{2,1,0:T(8,128)(2,1)S(1)} %get-tuple-element.74), channel_id=1, source_target_pairs={{0,24},{8,16},{16,8},{24,0},{1,25},{9,17},{17,9},{25,1},{2,26},{10... | collective-permute-start | bytes 786440 | tf_op jit(solution)/shard_map/ppermute | solution.py:35
  139.3 56.1 %collective-permute-start.18 = (bf16[8,48,384]{2,1,0:T(8,128)(2,1)S(1)}, bf16[8,48,384]{2,1,0:T(8,128)(2,1)S(1)}, u32[]{:S(2)}, u32[]{:S(2)}) collective-permute-start(bf16[8,48,384]{2,1,0:T(8,128)(2,1)S(1)} %get-tuple-element.102), channel_id=1, source_target_pairs={{0,1},{1,0},{2,3},{3,2},{4,5},{5,4},{6,7},{7,6},{8,9},{9,8},{10,11... | collective-permute-start | bytes 884744 | tf_op jit(solution)/shard_map/ppermute | solution.py:35
  140.9 55.0 %collective-permute-start.16 = (bf16[8,48,384]{2,1,0:T(8,128)(2,1)S(1)}, bf16[8,48,384]{2,1,0:T(8,128)(2,1)S(1)}, u32[]{:S(2)}, u32[]{:S(2)}) collective-permute-start(bf16[8,48,384]{2,1,0:T(8,128)(2,1)S(1)} %get-tuple-element.103), channel_id=1, source_target_pairs={{0,1},{1,0},{2,3},{3,2},{4,5},{5,4},{6,7},{7,6},{8,9},{9,8},{10,11... | collective-permute-start | bytes 884744 | tf_op jit(solution)/shard_map/ppermute | solution.py:35
  166.6 30.9 %collective-permute-start.14 = (bf16[8,48,384]{2,1,0:T(8,128)(2,1)S(1)}, bf16[8,48,384]{2,1,0:T(8,128)(2,1)S(1)}, u32[]{:S(2)}, u32[]{:S(2)}) collective-permute-start(bf16[8,48,384]{2,1,0:T(8,128)(2,1)S(1)} %get-tuple-element.104), channel_id=1, source_target_pairs={{0,1},{1,0},{2,3},{3,2},{4,5},{5,4},{6,7},{7,6},{8,9},{9,8},{10,11... | collective-permute-start | bytes 884744 | tf_op jit(solution)/shard_map/ppermute | solution.py:35
  168.2 29.8 %collective-permute-start.13 = (bf16[8,48,384]{2,1,0:T(8,128)(2,1)S(1)}, bf16[8,48,384]{2,1,0:T(8,128)(2,1)S(1)}, u32[]{:S(2)}, u32[]{:S(2)}) collective-permute-start(bf16[8,48,384]{2,1,0:T(8,128)(2,1)S(1)} %get-tuple-element.105), channel_id=1, source_target_pairs={{0,1},{1,0},{2,3},{3,2},{4,5},{5,4},{6,7},{7,6},{8,9},{9,8},{10,11... | collective-permute-start | bytes 884744 | tf_op jit(solution)/shard_map/ppermute | solution.py:35
  168.7 31.1 %collective-permute-start.31 = (bf16[8,48,384]{2,1,0:T(8,128)(2,1)S(1)}, bf16[8,48,384]{2,1,0:T(8,128)(2,1)S(1)}, u32[]{:S(2)}, u32[]{:S(2)}) collective-permute-start(bf16[8,48,384]{2,1,0:T(8,128)(2,1)S(1)} %get-tuple-element.98), channel_id=1, source_target_pairs={{0,1},{1,0},{2,3},{3,2},{4,5},{5,4},{6,7},{7,6},{8,9},{9,8},{10,11... | collective-permute-start | bytes 884744 | tf_op jit(solution)/shard_map/ppermute | solution.py:35
  195.4 10.0 %collective-permute-start.29 = (bf16[8,48,384]{2,1,0:T(8,128)(2,1)S(1)}, bf16[8,48,384]{2,1,0:T(8,128)(2,1)S(1)}, u32[]{:S(2)}, u32[]{:S(2)}) collective-permute-start(bf16[8,48,384]{2,1,0:T(8,128)(2,1)S(1)} %get-tuple-element.99), channel_id=1, source_target_pairs={{0,1},{1,0},{2,3},{3,2},{4,5},{5,4},{6,7},{7,6},{8,9},{9,8},{10,11... | collective-permute-start | bytes 884744 | tf_op jit(solution)/shard_map/ppermute | solution.py:35
  196.0 15.8 %collective-permute-start.27 = (bf16[8,48,384]{2,1,0:T(8,128)(2,1)S(1)}, bf16[8,48,384]{2,1,0:T(8,128)(2,1)S(1)}, u32[]{:S(2)}, u32[]{:S(2)}) collective-permute-start(bf16[8,48,384]{2,1,0:T(8,128)(2,1)S(1)} %get-tuple-element.100), channel_id=1, source_target_pairs={{0,1},{1,0},{2,3},{3,2},{4,5},{5,4},{6,7},{7,6},{8,9},{9,8},{10,11... | collective-permute-start | bytes 884744 | tf_op jit(solution)/shard_map/ppermute | solution.py:35
  197.5 20.5 %collective-permute-start.26 = (bf16[8,48,384]{2,1,0:T(8,128)(2,1)S(1)}, bf16[8,48,384]{2,1,0:T(8,128)(2,1)S(1)}, u32[]{:S(2)}, u32[]{:S(2)}) collective-permute-start(bf16[8,48,384]{2,1,0:T(8,128)(2,1)S(1)} %get-tuple-element.101), channel_id=1, source_target_pairs={{0,1},{1,0},{2,3},{3,2},{4,5},{5,4},{6,7},{7,6},{8,9},{9,8},{10,11... | collective-permute-start | bytes 884744 | tf_op jit(solution)/shard_map/ppermute | solution.py:35
  198.0 26.4 %collective-permute-start.44 = (bf16[8,48,384]{2,1,0:T(8,128)(2,1)S(1)}, bf16[8,48,384]{2,1,0:T(8,128)(2,1)S(1)}, u32[]{:S(2)}, u32[]{:S(2)}) collective-permute-start(bf16[8,48,384]{2,1,0:T(8,128)(2,1)S(1)} %get-tuple-element.94), channel_id=1, source_target_pairs={{0,1},{1,0},{2,3},{3,2},{4,5},{5,4},{6,7},{7,6},{8,9},{9,8},{10,11... | collective-permute-start | bytes 884744 | tf_op jit(solution)/shard_map/ppermute | solution.py:35
  199.8 30.9 %collective-permute-start.42 = (bf16[8,48,384]{2,1,0:T(8,128)(2,1)S(1)}, bf16[8,48,384]{2,1,0:T(8,128)(2,1)S(1)}, u32[]{:S(2)}, u32[]{:S(2)}) collective-permute-start(bf16[8,48,384]{2,1,0:T(8,128)(2,1)S(1)} %get-tuple-element.95), channel_id=1, source_target_pairs={{0,1},{1,0},{2,3},{3,2},{4,5},{5,4},{6,7},{7,6},{8,9},{9,8},{10,11... | collective-permute-start | bytes 884744 | tf_op jit(solution)/shard_map/ppermute | solution.py:35
  205.4 31.6 %collective-permute-start.40 = (bf16[8,48,384]{2,1,0:T(8,128)(2,1)S(1)}, bf16[8,48,384]{2,1,0:T(8,128)(2,1)S(1)}, u32[]{:S(2)}, u32[]{:S(2)}) collective-permute-start(bf16[8,48,384]{2,1,0:T(8,128)(2,1)S(1)} %get-tuple-element.96), channel_id=1, source_target_pairs={{0,1},{1,0},{2,3},{3,2},{4,5},{5,4},{6,7},{7,6},{8,9},{9,8},{10,11... | collective-permute-start | bytes 884744 | tf_op jit(solution)/shard_map/ppermute | solution.py:35
  211.7 29.7 %collective-permute-start.39 = (bf16[8,48,384]{2,1,0:T(8,128)(2,1)S(1)}, bf16[8,48,384]{2,1,0:T(8,128)(2,1)S(1)}, u32[]{:S(2)}, u32[]{:S(2)}) collective-permute-start(bf16[8,48,384]{2,1,0:T(8,128)(2,1)S(1)} %get-tuple-element.97), channel_id=1, source_target_pairs={{0,1},{1,0},{2,3},{3,2},{4,5},{5,4},{6,7},{7,6},{8,9},{9,8},{10,11... | collective-permute-start | bytes 884744 | tf_op jit(solution)/shard_map/ppermute | solution.py:35
  218.1 25.8 %collective-permute-start.19 = (bf16[8,48,384]{2,1,0:T(8,128)(2,1)S(1)}, bf16[8,48,384]{2,1,0:T(8,128)(2,1)S(1)}, u32[]{:S(2)}, u32[]{:S(2)}) collective-permute-start(bf16[8,48,384]{2,1,0:T(8,128)(2,1)S(1)} %get-tuple-element.90), channel_id=1, source_target_pairs={{0,6},{1,7},{2,4},{3,5},{4,2},{5,3},{6,0},{7,1},{8,14},{9,15},{10,... | collective-permute-start | bytes 884744 | tf_op jit(solution)/shard_map/ppermute | solution.py:35
  224.4 32.7 %collective-permute-start.17 = (bf16[8,48,384]{2,1,0:T(8,128)(2,1)S(1)}, bf16[8,48,384]{2,1,0:T(8,128)(2,1)S(1)}, u32[]{:S(2)}, u32[]{:S(2)}) collective-permute-start(bf16[8,48,384]{2,1,0:T(8,128)(2,1)S(1)} %get-tuple-element.91), channel_id=1, source_target_pairs={{0,4},{1,5},{2,6},{3,7},{4,0},{5,1},{6,2},{7,3},{8,12},{9,13},{10,... | collective-permute-start | bytes 884744 | tf_op jit(solution)/shard_map/ppermute | solution.py:35
  230.7 31.1 %collective-permute-start.15 = (bf16[8,48,384]{2,1,0:T(8,128)(2,1)S(1)}, bf16[8,48,384]{2,1,0:T(8,128)(2,1)S(1)}, u32[]{:S(2)}, u32[]{:S(2)}) collective-permute-start(bf16[8,48,384]{2,1,0:T(8,128)(2,1)S(1)} %get-tuple-element.92), channel_id=1, source_target_pairs={{0,2},{1,3},{2,0},{3,1},{4,6},{5,7},{6,4},{7,5},{8,10},{9,11},{10,... | collective-permute-start | bytes 884744 | tf_op jit(solution)/shard_map/ppermute | solution.py:35
  237.0 24.8 %collective-permute-start.32 = (bf16[8,48,384]{2,1,0:T(8,128)(2,1)S(1)}, bf16[8,48,384]{2,1,0:T(8,128)(2,1)S(1)}, u32[]{:S(2)}, u32[]{:S(2)}) collective-permute-start(bf16[8,48,384]{2,1,0:T(8,128)(2,1)S(1)} %get-tuple-element.86), channel_id=1, source_target_pairs={{0,6},{1,7},{2,4},{3,5},{4,2},{5,3},{6,0},{7,1},{8,14},{9,15},{10,... | collective-permute-start | bytes 884744 | tf_op jit(solution)/shard_map/ppermute | solution.py:35
  241.5 41.0 %collective-permute-start.30 = (bf16[8,48,384]{2,1,0:T(8,128)(2,1)S(1)}, bf16[8,48,384]{2,1,0:T(8,128)(2,1)S(1)}, u32[]{:S(2)}, u32[]{:S(2)}) collective-permute-start(bf16[8,48,384]{2,1,0:T(8,128)(2,1)S(1)} %get-tuple-element.87), channel_id=1, source_target_pairs={{0,4},{1,5},{2,6},{3,7},{4,0},{5,1},{6,2},{7,3},{8,12},{9,13},{10,... | collective-permute-start | bytes 884744 | tf_op jit(solution)/shard_map/ppermute | solution.py:35
  243.9 38.6 %collective-permute-start.28 = (bf16[8,48,384]{2,1,0:T(8,128)(2,1)S(1)}, bf16[8,48,384]{2,1,0:T(8,128)(2,1)S(1)}, u32[]{:S(2)}, u32[]{:S(2)}) collective-permute-start(bf16[8,48,384]{2,1,0:T(8,128)(2,1)S(1)} %get-tuple-element.88), channel_id=1, source_target_pairs={{0,2},{1,3},{2,0},{3,1},{4,6},{5,7},{6,4},{7,5},{8,10},{9,11},{10,... | collective-permute-start | bytes 884744 | tf_op jit(solution)/shard_map/ppermute | solution.py:35
  257.1 29.1 %collective-permute-start.45 = (bf16[8,48,384]{2,1,0:T(8,128)(2,1)S(1)}, bf16[8,48,384]{2,1,0:T(8,128)(2,1)S(1)}, u32[]{:S(2)}, u32[]{:S(2)}) collective-permute-start(bf16[8,48,384]{2,1,0:T(8,128)(2,1)S(1)} %get-tuple-element.82), channel_id=1, source_target_pairs={{0,6},{1,7},{2,4},{3,5},{4,2},{5,3},{6,0},{7,1},{8,14},{9,15},{10,... | collective-permute-start | bytes 884744 | tf_op jit(solution)/shard_map/ppermute | solution.py:35
  261.8 31.8 %collective-permute-start.43 = (bf16[8,48,384]{2,1,0:T(8,128)(2,1)S(1)}, bf16[8,48,384]{2,1,0:T(8,128)(2,1)S(1)}, u32[]{:S(2)}, u32[]{:S(2)}) collective-permute-start(bf16[8,48,384]{2,1,0:T(8,128)(2,1)S(1)} %get-tuple-element.83), channel_id=1, source_target_pairs={{0,4},{1,5},{2,6},{3,7},{4,0},{5,1},{6,2},{7,3},{8,12},{9,13},{10,... | collective-permute-start | bytes 884744 | tf_op jit(solution)/shard_map/ppermute | solution.py:35
  261.8 31.8 %collective-permute-start.41 = (bf16[8,48,384]{2,1,0:T(8,128)(2,1)S(1)}, bf16[8,48,384]{2,1,0:T(8,128)(2,1)S(1)}, u32[]{:S(2)}, u32[]{:S(2)}) collective-permute-start(bf16[8,48,384]{2,1,0:T(8,128)(2,1)S(1)} %get-tuple-element.84), channel_id=1, source_target_pairs={{0,2},{1,3},{2,0},{3,1},{4,6},{5,7},{6,4},{7,5},{8,10},{9,11},{10,... | collective-permute-start | bytes 884744 | tf_op jit(solution)/shard_map/ppermute | solution.py:35
  311.8 16.3 %collective-permute-start.49 = (f32[32,1152]{1,0:T(8,128)S(1)}, f32[32,1152]{1,0:T(8,128)S(1)}, u32[]{:S(2)}, u32[]{:S(2)}) collective-permute-start(f32[32,1152]{1,0:T(8,128)S(1)} %sweep.1), channel_id=1, source_target_pairs={{0,1},{1,0},{2,3},{3,2},{4,5},{5,4},{6,7},{7,6},{8,9},{9,8},{10,11... | collective-permute-start | bytes 442376 | tf_op jit(solution)/shard_map/ppermute | solution.py:35
  312.3 8.6 %collective-permute-start.48 = (f32[32,1152]{1,0:T(8,128)S(1)}, f32[32,1152]{1,0:T(8,128)S(1)}, u32[]{:S(2)}, u32[]{:S(2)}) collective-permute-start(f32[32,1152]{1,0:T(8,128)S(1)} %sweep.1), channel_id=1, source_target_pairs={{0,6},{1,7},{2,4},{3,5},{4,2},{5,3},{6,0},{7,1},{8,14},{9,15},{10,... | collective-permute-start | bytes 442376 | tf_op jit(solution)/shard_map/ppermute | solution.py:35
  314.8 11.2 %collective-permute-start.47 = (f32[32,1152]{1,0:T(8,128)S(1)}, f32[32,1152]{1,0:T(8,128)S(1)}, u32[]{:S(2)}, u32[]{:S(2)}) collective-permute-start(f32[32,1152]{1,0:T(8,128)S(1)} %sweep.1), channel_id=1, source_target_pairs={{0,4},{1,5},{2,6},{3,7},{4,0},{5,1},{6,2},{7,3},{8,12},{9,13},{10,... | collective-permute-start | bytes 442376 | tf_op jit(solution)/shard_map/ppermute | solution.py:35
  314.8 12.8 %collective-permute-start.46 = (f32[32,1152]{1,0:T(8,128)S(1)}, f32[32,1152]{1,0:T(8,128)S(1)}, u32[]{:S(2)}, u32[]{:S(2)}) collective-permute-start(f32[32,1152]{1,0:T(8,128)S(1)} %sweep.1), channel_id=1, source_target_pairs={{0,2},{1,3},{2,0},{3,1},{4,6},{5,7},{6,4},{7,5},{8,10},{9,11},{10,... | collective-permute-start | bytes 442376 | tf_op jit(solution)/shard_map/ppermute | solution.py:35
  320.9 12.8 %collective-permute-start.52 = (f32[32,1152]{1,0:T(8,128)S(1)}, f32[32,1152]{1,0:T(8,128)S(1)}, u32[]{:S(2)}, u32[]{:S(2)}) collective-permute-start(f32[32,1152]{1,0:T(8,128)S(1)} %collective-permute-done.48), channel_id=1, source_target_pairs={{0,1},{1,0},{2,3},{3,2},{4,5},{5,4},{6,7},{7,6},{8,9},{9,8},{10,11... | collective-permute-start | bytes 442376 | tf_op jit(solution)/shard_map/ppermute | solution.py:35
  326.0 7.7 %collective-permute-start.51 = (f32[32,1152]{1,0:T(8,128)S(1)}, f32[32,1152]{1,0:T(8,128)S(1)}, u32[]{:S(2)}, u32[]{:S(2)}) collective-permute-start(f32[32,1152]{1,0:T(8,128)S(1)} %collective-permute-done.47), channel_id=1, source_target_pairs={{0,1},{1,0},{2,3},{3,2},{4,5},{5,4},{6,7},{7,6},{8,9},{9,8},{10,11... | collective-permute-start | bytes 442376 | tf_op jit(solution)/shard_map/ppermute | solution.py:35
  327.5 6.1 %collective-permute-start.50 = (f32[32,1152]{1,0:T(8,128)S(1)}, f32[32,1152]{1,0:T(8,128)S(1)}, u32[]{:S(2)}, u32[]{:S(2)}) collective-permute-start(f32[32,1152]{1,0:T(8,128)S(1)} %collective-permute-done.46), channel_id=1, source_target_pairs={{0,1},{1,0},{2,3},{3,2},{4,5},{5,4},{6,7},{7,6},{8,9},{9,8},{10,11... | collective-permute-start | bytes 442376 | tf_op jit(solution)/shard_map/ppermute | solution.py:35
  (5 other events, 17.5 us)
